TPU v7x, 32 devices: a whole 2x2x4 slice. The times are simulated.
32 devices in a mesh: scene: 1, panel: 16 (over z, y, x), aper: 2 (over core).
Axes of the slice: x: 2, y: 2, z: 4, core: 2. Of those that a mesh axis runs over, the one named last changes fastest.
Arguments:
- subimages: bfloat16 [4, 2, 512, 4096], P(('scene', 'aper'), None, 'panel'), may hold values from -6 to 6
- rng_taps: int32 [2, 3, 512], P('aper'), may hold values from 0 to 240
- rng_blocks: int32 [2, 3, 4], P('aper'), may hold values from 0 to 2, as said below
- rng_weights: bfloat16 [2, 3, 2, 16, 512], P('aper'), may hold values from -0.75 to 0.75
- ang_taps: int32 [2, 32768], P('aper'), may hold values from 0 to 240
- ang_blocks: int32 [2, 256], P('aper'), may hold values from 0 to 62, as said below
- ang_weights: bfloat16 [2, 2, 16, 32768], P('aper'), may hold values from -0.75 to 0.75
- owners: int32 [16384], replicated, may hold values from 0 to 63
Outputs:
- image: bfloat16 [2, 512, 16384], P(None, ('scene', 'aper'), 'panel')
- gradients: float32 [2, 64], P(('scene', 'aper'), 'panel')
Inputs may be any that keep to these rules, and one draw needn't show every extreme that they name: `ang_blocks`: numbering the output angle blocks of one slot from the start of its columns as j, block j reads input blocks starting at j // 2 - 1 or j // 2, kept within 0 to the slot's input blocks minus 2 (input blocks: 32 for slots 0 and 1, 64 for slot 2). `rng_blocks`: output range block j reads input blocks starting at j - 1 or j, kept within 0 to 2.
All inputs are finite; a program needn't handle non-finite values.
Results may differ from a plain program's by a relative error of at most 0.0071.
Values may be sent and summed in bfloat16 or wider, within the bound.
No kernel may reach another device: no remote copies, remote signals or barrier semaphores. Data moves between devices by JAX's collectives and lax.ppermute only.
A program may use at most 192 MiB of HBM per device.

v0:
```python
import jax
import jax.numpy as jnp
from jax import lax
from jax.sharding import PartitionSpec as P

TILE = 128
TAPS = 16
GRP_DEV = 4
ANG_P = 8192
ANG_F = 16384


def build_tiles(base, weights):
    span = jnp.arange(2 * TILE, dtype=jnp.int32)
    offset = span[None, :, None] - base[:, None, :]
    tiles = jnp.zeros((2,) + offset.shape, jnp.bfloat16)
    for tap in range(TAPS):
        chosen = weights[:, tap][:, :, None, :]
        tiles = tiles + jnp.where((offset == tap)[None], chosen, jnp.zeros((), jnp.bfloat16))
    return tiles


def angle_pass(child, starts, base, weights):
    rows = child.shape[1]
    count = starts.shape[0]
    blocks = child.reshape(2, rows, child.shape[2] // TILE, TILE)
    spans = jnp.concatenate(
        [jnp.take(blocks, starts, axis=2), jnp.take(blocks, starts + 1, axis=2)], axis=3
    )
    tiles = build_tiles(base.reshape(count, TILE), weights.reshape(2, TAPS, count, TILE))

    def product(left, right):
        return jnp.einsum("rnk,nka->rna", left, right, preferred_element_type=jnp.float32)

    real = product(spans[0], tiles[0]) - product(spans[1], tiles[1])
    imag = product(spans[0], tiles[1]) + product(spans[1], tiles[0])
    return jnp.stack([real, imag]).reshape(2, rows, count * TILE)


def range_pass(child, starts, base, weights):
    cols = child.shape[2]
    count = starts.shape[0]
    blocks = child.reshape(2, child.shape[1] // TILE, TILE, cols)
    spans = jnp.concatenate(
        [jnp.take(blocks, starts, axis=1), jnp.take(blocks, starts + 1, axis=1)], axis=2
    )
    tiles = build_tiles(base.reshape(count, TILE), weights.reshape(2, TAPS, count, TILE))

    def product(left, right):
        return jnp.einsum("nkr,nkc->nrc", left, right, preferred_element_type=jnp.float32)

    real = product(tiles[0], spans[0]) - product(tiles[1], spans[1])
    imag = product(tiles[0], spans[1]) + product(tiles[1], spans[0])
    return jnp.stack([real, imag]).reshape(2, count * TILE, cols)


def slot_range(which):
    if which < 2:
        return (ANG_P * which, ANG_P)
    return (2 * ANG_P, ANG_F)


def pair_sum(contribution):
    return lax.psum(contribution.astype(jnp.float32).astype(jnp.bfloat16), "aper").astype(
        jnp.float32
    )


def owner_sum(slope, owned, groups):
    marks = owned[:, None] == jnp.arange(groups, dtype=jnp.int32)[None, :]
    partial_sums = jnp.sum(jnp.where(marks, slope[:, None], 0.0), axis=0)
    return lax.psum_scatter(partial_sums, "panel", scatter_dimension=0, tiled=True)


def slope_of(focused, contribution, first_row, total_rows):
    rows = focused.shape[1]
    place = (first_row + jnp.arange(rows, dtype=jnp.int32)).astype(jnp.float32)
    weight = 1.0 + 2.0 * place / (total_rows - 1)
    own = contribution.astype(jnp.float32)
    power = focused[0] * focused[0] + focused[1] * focused[1]
    inphase = focused[0] * own[0] + focused[1] * own[1]
    return jnp.sum(weight[:, None] * power * inphase, axis=0) / total_rows


def shards(subimages, rng_taps, rng_blocks, rng_weights, ang_taps, ang_blocks, ang_weights, owners):
    panels = lax.axis_size("panel")
    place = lax.axis_index("panel")
    side = lax.axis_index("aper")
    groups = GRP_DEV * panels
    current = subimages
    for section in range(2):
        slots = [0, 1] if section == 0 else [2]
        spread = lax.all_to_all(current, "panel", split_axis=3, concat_axis=2, tiled=True)
        ranged = jnp.stack(
            [
                range_pass(
                    spread[member], rng_blocks[0, slot], rng_taps[0, slot], rng_weights[0, slot]
                ).astype(jnp.bfloat16)
                for member, slot in enumerate(slots)
            ]
        )
        back = lax.all_to_all(ranged, "panel", split_axis=2, concat_axis=3, tiled=True)
        total = None
        for member, slot in enumerate(slots):
            start, length = slot_range(slot)
            term = angle_pass(
                back[member],
                ang_blocks[0, start // TILE : (start + length) // TILE],
                ang_taps[0, start : start + length],
                ang_weights[0, :, :, start : start + length],
            )
            total = term if total is None else total + term
        current = total.astype(jnp.bfloat16)[None]
    contribution = current[0]
    focused = pair_sum(contribution)
    rows = contribution.shape[1]
    slope = slope_of(focused, contribution, place * rows, rows * panels)
    gradients = owner_sum(slope, owners, groups)
    regrouped = lax.all_to_all(
        focused.astype(jnp.bfloat16), "panel", split_axis=2, concat_axis=1, tiled=True
    )
    half = regrouped.shape[1] // 2
    image = lax.dynamic_slice_in_dim(regrouped, side * half, half, 1)
    return (image, gradients[None])


def solution(mesh):
    return jax.shard_map(
        shards,
        mesh=mesh,
        in_specs=(
            P(("scene", "aper"), None, "panel", None),
            P("aper", None, None),
            P("aper", None, None),
            P("aper", None, None, None, None),
            P("aper", None),
            P("aper", None),
            P("aper", None, None, None),
            P(),
        ),
        out_specs=(P(None, ("scene", "aper"), "panel"), P(("scene", "aper"), "panel")),
        check_vma=False,
    )
```

profile of v0, /device:TPU:0, one launch (start us, length us, event | category | flops | bytes accessed | tf_op | source)
XLA Modules:
  0.0 630.4 jit_solution(1192458819185325631)
XLA Ops:
  7.2 9.8 %copy.698 = bf16[2,2,32,4096]{2,1,0,3:T(2,128)(2,1)} copy(bf16[2,2,32,4096]{3,2,1,0:T(8,128)(2,1)} %param.16) | data formatting | bytes 2097152 | tf_op args[0]
  17.0 10.0 %reshape.683 = bf16[16,2,16384]{2,1,0:T(2,128)(2,1)} reshape(bf16[4096,2,2,32]{3,2,1,0:T(2,128)(2,1)} %bitcast.675) | data formatting | bytes 2097152
  27.0 8.5 %all-to-all-start = ((bf16[16,2,16384]{2,1,0:T(2,128)(2,1)}), bf16[16,2,16384]{2,1,0:T(2,128)(2,1)}, u32[]{:S(2)}, u32[]{:S(2)}) async-start(bf16[16,2,16384]{2,1,0:T(2,128)(2,1)} %reshape.683), calls=%async_computation | async-start | bytes 2097152 | tf_op jit(solution)/shard_map/all_to_all | solution.py:93
  36.2 22.4 %fusion.47 = (pred[64,256,128]{2,1,0:T(8,128)(4,1)}, pred[64,256,128]{2,1,0:T(8,128)(4,1)}, pred[64,256,128]{2,1,0:T(8,128)(4,1)}, pred[64,256,128]{2,1,0:T(8,12...) fusion(s32[64,128]{1,0:T(8,128)S(1)} %bitcast.700), kind=kLoop, calls=%fused_computation.67 | loop fusion | flops 35651584 | bytes 33587200 | tf_op jit(solution)/shard_map/eq | solution.py:19
  65.8 22.3 %fusion.31 = (pred[64,256,128]{2,1,0:T(8,128)(4,1)S(1)}, pred[64,256,128]{2,1,0:T(8,128)(4,1)}, pred[64,256,128]{2,1,0:T(8,128)(4,1)}, pred[64,256,128]{2,1,0:T(...) fusion(s32[64,128]{1,0:T(8,128)S(1)} %bitcast.699), kind=kLoop, calls=%fused_computation.49 | loop fusion | flops 35651584 | bytes 33587200 | tf_op jit(solution)/shard_map/eq | solution.py:19
  88.2 30.1 %select_add_fusion.2 = bf16[2,64,256,128]{3,2,1,0:T(8,128)(2,1)} fusion(pred[64,256,128]{2,1,0:T(8,128)(4,1)S(1)} %copy-done.9, pred[64,256,128]{2,1,0:T(8,128)(4,1)S(1)} %copy-done.10, pred[64,256,128]{2,1,0:T(8,128)(4,1)S(1)} %copy-done.11, pred[64,256,128]{2,1,0:T(8,128)(4,1)S(1)} %copy-done.12, pred[64,256,128]{2,1,0:T(8,128)(4,1)S(1)} %copy-done.13, ...), kind=kLoop, calls=%fused_computation.50 | loop fusion | flops 130023424 | bytes 42467328 | tf_op jit(solution)/shard_map/add | solution.py:19
  122.8 4.5 select_add_fusion.3
  127.4 4.5 select_add_fusion.4
  131.9 10.2 %reshape.684 = bf16[4096,2,2,32]{3,2,1,0:T(2,128)(2,1)} reshape(bf16[16,2,16384]{2,1,0:T(2,128)(2,1)} %all-to-all-done) | data formatting | bytes 2097152
  142.1 6.1 copy.775
  171.5 4.7 maximum_maximum_fusion
  176.2 7.0 %all-to-all-start.1 = ((bf16[2,2,512,256]{3,1,0,2:T(2,128)(2,1)}), bf16[2,2,512,256]{3,1,0,2:T(2,128)(2,1)S(1)}, u32[]{:S(2)}, u32[]{:S(2)}) async-start(bf16[2,2,512,256]{3,1,0,2:T(2,128)(2,1)} %maximum_maximum_fusion), calls=%async_computation.1 | async-start | bytes 2097152 | tf_op jit(solution)/shard_map/all_to_all | solution.py:102
  183.3 29.4 %select_add_fusion.1 = bf16[2,64,256,128]{3,2,1,0:T(8,128)(2,1)} fusion(pred[64,256,128]{2,1,0:T(8,128)(4,1)} %get-tuple-element.106, pred[64,256,128]{2,1,0:T(8,128)(4,1)} %get-tuple-element.107, pred[64,256,128]{2,1,0:T(8,128)(4,1)} %get-tuple-element.108, pred[64,256,128]{2,1,0:T(8,128)(4,1)} %get-tuple-element.109, ...), kind=kLoop, calls=%fused_computation.32 | loop fusion | flops 130023424 | bytes 42467328 | tf_op jit(solution)/shard_map/add | solution.py:19
  231.2 4.3 fusion.57
  235.6 3.9 fusion.56
  261.2 6.8 %copy.757 = bf16[1,2,32,8192]{2,1,0,3:T(2,128)(2,1)} copy(bf16[1,2,32,8192]{3,2,1,0:T(8,128)(2,1)S(1)} %fusion.67) | data formatting | bytes 2097152 | tf_op jit(solution)/shard_map/convert_element_type | solution.py:113
  268.0 10.1 %reshape.685 = bf16[16,2,16384]{2,1,0:T(2,128)(2,1)} reshape(bf16[8192,1,2,32]{3,2,1,0:T(2,128)(2,1)} %bitcast.673) | data formatting | bytes 2097152
  278.1 6.9 %all-to-all-start.2 = ((bf16[16,2,16384]{2,1,0:T(2,128)(2,1)}), bf16[16,2,16384]{2,1,0:T(2,128)(2,1)S(1)}, u32[]{:S(2)}, u32[]{:S(2)}) async-start(bf16[16,2,16384]{2,1,0:T(2,128)(2,1)} %reshape.685), calls=%async_computation.2 | async-start | bytes 2097152 | tf_op jit(solution)/shard_map/all_to_all | solution.py:93
  285.0 43.6 %fusion.15 = (pred[128,256,128]{2,1,0:T(8,128)(4,1)}, pred[128,256,128]{2,1,0:T(8,128)(4,1)}, pred[128,256,128]{2,1,0:T(8,128)(4,1)}, pred[128,256,128]{2,1,0:T(...) fusion(s32[128,128]{1,0:T(8,128)S(1)} %bitcast.698), kind=kLoop, calls=%fused_computation.29 | loop fusion | flops 71303168 | bytes 67174400 | tf_op jit(solution)/shard_map/eq | solution.py:19
  338.4 9.0 %copy.777 = bf16[1,2,32,16,512]{4,2,3,1,0:T(8,128)(2,1)S(1)} copy(bf16[1,2,32,16,512]{2,1,4,3,0:T(2,128)(2,1)} %bitcast.674) | data formatting | bytes 2097152 | tf_op jit(solution)/shard_map/all_to_all | solution.py:93
  357.2 7.1 %all-to-all-start.3 = ((bf16[1,2,512,512]{3,1,0,2:T(2,128)(2,1)}), bf16[1,2,512,512]{3,1,0,2:T(2,128)(2,1)S(1)}, u32[]{:S(2)}, u32[]{:S(2)}) async-start(bf16[1,2,512,512]{3,1,0,2:T(2,128)(2,1)} %pad_maximum_fusion.4), calls=%async_computation.3 | async-start | bytes 2097152 | tf_op jit(solution)/shard_map/all_to_all | solution.py:102
  364.4 54.7 %select_add_fusion = bf16[2,128,256,128]{3,2,1,0:T(8,128)(2,1)} fusion(pred[128,256,128]{2,1,0:T(8,128)(4,1)} %get-tuple-element.90, pred[128,256,128]{2,1,0:T(8,128)(4,1)} %get-tuple-element.91, pred[128,256,128]{2,1,0:T(8,128)(4,1)} %get-tuple-element.92, pred[128,256,128]{2,1,0:T(8,128)(4,1)} %get-tuple-element.93, ...), kind=kLoop, calls=%fused_computation.12 | loop fusion | flops 260046848 | bytes 84934656 | tf_op jit(solution)/shard_map/add | solution.py:19
  428.0 5.1 fusion.48
  433.1 6.7 %fusion.49 = f32[128,128,32]{1,2,0:T(8,128)} fusion(bf16[2,128,256,128]{3,2,1,0:T(8,128)(2,1)} %select_add_fusion, bf16[2,32,128,128]{3,1,2,0:T(8,128)(2,1)S(1)} %fusion.68, bf16[2,32,128,128]{3,1,2,0:T(8,128)(2,1)S(1)} %fusion.69), kind=kOutput, calls=%fused_computation.69 | convolution fusion | flops 272629760 | bytes 14680064 | tf_op jit(solution)/shard_map/rnk,nka->rna/dot_general | solution.py:33
  445.3 5.7 fusion.71
  457.2 24.8 %all-reduce.3.cloned.1.call-done = bf16[2,32,16384]{2,1,0:T(8,128)(2,1)} async-done(((bf16[2,32,16384]{2,1,0:T(8,128)(2,1)}), bf16[2,32,16384]{2,1,0:T(8,128)(2,1)}) %all-reduce.3.cloned.1.call-update) | async-done | bytes 2097168 | tf_op jit(solution)/shard_map/psum | solution.py:64
  482.0 17.1 %copy.772 = bf16[2,32,16384]{1,0,2:T(2,128)(2,1)} copy(bf16[2,32,16384]{2,1,0:T(8,128)(2,1)} %all-reduce.3.cloned.1.call-done) | data formatting | bytes 4194304 | tf_op jit(solution)/shard_map/psum | solution.py:64
  499.1 14.5 %reshape.687 = bf16[16,2,32768]{2,1,0:T(2,128)(2,1)} reshape(bf16[16384,2,32]{2,1,0:T(2,128)(2,1)} %bitcast.671) | data formatting | bytes 4194304
  513.6 7.2 %all-to-all-start.4 = ((bf16[16,2,32768]{2,1,0:T(2,128)(2,1)}), bf16[16,2,32768]{2,1,0:T(2,128)(2,1)}, u32[]{:S(2)}, u32[]{:S(2)}) async-start(bf16[16,2,32768]{2,1,0:T(2,128)(2,1)} %reshape.687), calls=%async_computation.4 | async-start | bytes 4194304 | tf_op jit(solution)/shard_map/all_to_all | solution.py:119
  525.7 65.3 %all-reduce = f32[64]{0:T(128)S(1)} all-reduce(f32[64]{0:T(128)S(1)} %select_reduce_fusion), channel_id=2, replica_groups=mesh['scene'=1,'panel'=16,'aper'=2] {'panel'}, use_global_device_ids=true, to_apply=%region_3.8.clone | all-reduce | flops 64 | bytes 512
  591.6 12.8 %reshape.688 = bf16[16384,2,32]{2,1,0:T(2,128)(2,1)} reshape(bf16[16,2,32768]{2,1,0:T(2,128)(2,1)} %all-to-all-done.4) | data formatting | bytes 4194304
  604.5 17.8 %copy.779 = bf16[2,32,16,1024]{3,1,2,0:T(8,128)(2,1)S(1)} copy(bf16[2,32,16,1024]{1,0,3,2:T(2,128)(2,1)} %bitcast.670) | data formatting | bytes 4194304 | tf_op jit(solution)/shard_map/all_to_all | solution.py:119
  (334 shorter events, 120.6 us)
Async XLA Ops:
  17.0 18.5 %copy-start.82 = (s32[1,3,512]{2,0,1:T(1,128)S(1)}, s32[1,3,512]{2,0,1:T(1,128)}, u32[]{:S(2)}) copy-start(s32[1,3,512]{2,0,1:T(1,128)} %param.17) | copy-start | bytes 18436
  17.0 18.6 %copy-start.55 = (bf16[1,3,2,16,512]{4,3,2,1,0:T(8,128)(2,1)S(1)}, bf16[1,3,2,16,512]{4,3,2,1,0:T(8,128)(2,1)}, u32[]{:S(2)}) copy-start(bf16[1,3,2,16,512]{4,3,2,1,0:T(8,128)(2,1)} %param.19) | copy-start | bytes 294916
  17.0 19.2 %copy-start.39 = (s32[1,32768]{1,0:T(1,128)S(1)}, s32[1,32768]{1,0:T(1,128)}, u32[]{:S(2)}) copy-start(s32[1,32768]{1,0:T(1,128)} %param.20) | copy-start | bytes 393220
  27.0 104.9 %all-to-all-start = ((bf16[16,2,16384]{2,1,0:T(2,128)(2,1)}), bf16[16,2,16384]{2,1,0:T(2,128)(2,1)}, u32[]{:S(2)}, u32[]{:S(2)}) async-start(bf16[16,2,16384]{2,1,0:T(2,128)(2,1)} %reshape.683), calls=%async_computation | async-start | bytes 2097152 | tf_op jit(solution)/shard_map/all_to_all | solution.py:93
  36.2 22.4 %copy-start.22 = (bf16[1,2,16,32768]{3,2,1,0:T(8,128)(2,1)S(1)}, bf16[1,2,16,32768]{3,2,1,0:T(8,128)(2,1)}, u32[]{:S(2)}) copy-start(bf16[1,2,16,32768]{3,2,1,0:T(8,128)(2,1)} %param.22) | copy-start | bytes 6291460
  65.7 22.4 %copy-start.8 = (pred[64,256,128]{2,1,0:T(8,128)(4,1)S(1)}, pred[64,256,128]{2,1,0:T(8,128)(4,1)}, u32[]{:S(2)}) copy-start(pred[64,256,128]{2,1,0:T(8,128)(4,1)} %get-tuple-element.153) | copy-start | bytes 6291460
  65.7 22.4 %copy-start.9 = (pred[64,256,128]{2,1,0:T(8,128)(4,1)S(1)}, pred[64,256,128]{2,1,0:T(8,128)(4,1)}, u32[]{:S(2)}) copy-start(pred[64,256,128]{2,1,0:T(8,128)(4,1)} %get-tuple-element.154) | copy-start | bytes 6291460
  65.7 22.4 %copy-start.10 = (pred[64,256,128]{2,1,0:T(8,128)(4,1)S(1)}, pred[64,256,128]{2,1,0:T(8,128)(4,1)}, u32[]{:S(2)}) copy-start(pred[64,256,128]{2,1,0:T(8,128)(4,1)} %get-tuple-element.155) | copy-start | bytes 6291460
  65.7 22.4 %copy-start.11 = (pred[64,256,128]{2,1,0:T(8,128)(4,1)S(1)}, pred[64,256,128]{2,1,0:T(8,128)(4,1)}, u32[]{:S(2)}) copy-start(pred[64,256,128]{2,1,0:T(8,128)(4,1)} %get-tuple-element.156) | copy-start | bytes 6291460
  65.7 22.4 %copy-start.12 = (pred[64,256,128]{2,1,0:T(8,128)(4,1)S(1)}, pred[64,256,128]{2,1,0:T(8,128)(4,1)}, u32[]{:S(2)}) copy-start(pred[64,256,128]{2,1,0:T(8,128)(4,1)} %get-tuple-element.157) | copy-start | bytes 6291460
  65.7 22.4 %copy-start.13 = (pred[64,256,128]{2,1,0:T(8,128)(4,1)S(1)}, pred[64,256,128]{2,1,0:T(8,128)(4,1)}, u32[]{:S(2)}) copy-start(pred[64,256,128]{2,1,0:T(8,128)(4,1)} %get-tuple-element.158) | copy-start | bytes 6291460
  65.7 22.4 %copy-start.14 = (pred[64,256,128]{2,1,0:T(8,128)(4,1)S(1)}, pred[64,256,128]{2,1,0:T(8,128)(4,1)}, u32[]{:S(2)}) copy-start(pred[64,256,128]{2,1,0:T(8,128)(4,1)} %get-tuple-element.159) | copy-start | bytes 6291460
  65.7 22.4 %copy-start.15 = (pred[64,256,128]{2,1,0:T(8,128)(4,1)S(1)}, pred[64,256,128]{2,1,0:T(8,128)(4,1)}, u32[]{:S(2)}) copy-start(pred[64,256,128]{2,1,0:T(8,128)(4,1)} %get-tuple-element.160) | copy-start | bytes 6291460
  65.8 22.4 %copy-start.16 = (pred[64,256,128]{2,1,0:T(8,128)(4,1)S(1)}, pred[64,256,128]{2,1,0:T(8,128)(4,1)}, u32[]{:S(2)}) copy-start(pred[64,256,128]{2,1,0:T(8,128)(4,1)} %get-tuple-element.161) | copy-start | bytes 6291460
  65.8 22.4 %copy-start.17 = (pred[64,256,128]{2,1,0:T(8,128)(4,1)S(1)}, pred[64,256,128]{2,1,0:T(8,128)(4,1)}, u32[]{:S(2)}) copy-start(pred[64,256,128]{2,1,0:T(8,128)(4,1)} %get-tuple-element.162) | copy-start | bytes 6291460
  170.7 12.5 %copy-start.43 = (bf16[2,64,128]{2,1,0:T(8,128)(2,1)S(1)}, bf16[2,64,128]{2,1,0:T(8,128)(2,1)}, u32[]{:S(2)}) copy-start(bf16[2,64,128]{2,1,0:T(8,128)(2,1)} %get-tuple-element.52) | copy-start | bytes 98308
  170.7 12.5 %copy-start.44 = (bf16[2,64,128]{2,1,0:T(8,128)(2,1)S(1)}, bf16[2,64,128]{2,1,0:T(8,128)(2,1)}, u32[]{:S(2)}) copy-start(bf16[2,64,128]{2,1,0:T(8,128)(2,1)} %get-tuple-element.53) | copy-start | bytes 98308
  170.7 12.5 %copy-start.45 = (bf16[2,64,128]{2,1,0:T(8,128)(2,1)S(1)}, bf16[2,64,128]{2,1,0:T(8,128)(2,1)}, u32[]{:S(2)}) copy-start(bf16[2,64,128]{2,1,0:T(8,128)(2,1)} %get-tuple-element.54) | copy-start | bytes 98308
  170.8 12.5 %copy-start.46 = (bf16[2,64,128]{2,1,0:T(8,128)(2,1)S(1)}, bf16[2,64,128]{2,1,0:T(8,128)(2,1)}, u32[]{:S(2)}) copy-start(bf16[2,64,128]{2,1,0:T(8,128)(2,1)} %get-tuple-element.55) | copy-start | bytes 98308
  170.8 12.5 %copy-start.47 = (bf16[2,64,128]{2,1,0:T(8,128)(2,1)S(1)}, bf16[2,64,128]{2,1,0:T(8,128)(2,1)}, u32[]{:S(2)}) copy-start(bf16[2,64,128]{2,1,0:T(8,128)(2,1)} %get-tuple-element.56) | copy-start | bytes 98308
  170.8 12.5 %copy-start.48 = (bf16[2,64,128]{2,1,0:T(8,128)(2,1)S(1)}, bf16[2,64,128]{2,1,0:T(8,128)(2,1)}, u32[]{:S(2)}) copy-start(bf16[2,64,128]{2,1,0:T(8,128)(2,1)} %get-tuple-element.57) | copy-start | bytes 98308
  170.8 12.5 %copy-start.49 = (bf16[2,64,128]{2,1,0:T(8,128)(2,1)S(1)}, bf16[2,64,128]{2,1,0:T(8,128)(2,1)}, u32[]{:S(2)}) copy-start(bf16[2,64,128]{2,1,0:T(8,128)(2,1)} %get-tuple-element.58) | copy-start | bytes 98308
  170.8 12.5 %copy-start.50 = (bf16[2,64,128]{2,1,0:T(8,128)(2,1)S(1)}, bf16[2,64,128]{2,1,0:T(8,128)(2,1)}, u32[]{:S(2)}) copy-start(bf16[2,64,128]{2,1,0:T(8,128)(2,1)} %get-tuple-element.59) | copy-start | bytes 98308
  170.8 12.5 %copy-start.51 = (bf16[2,64,128]{2,1,0:T(8,128)(2,1)S(1)}, bf16[2,64,128]{2,1,0:T(8,128)(2,1)}, u32[]{:S(2)}) copy-start(bf16[2,64,128]{2,1,0:T(8,128)(2,1)} %get-tuple-element.60) | copy-start | bytes 98308
  176.2 36.7 %all-to-all-start.1 = ((bf16[2,2,512,256]{3,1,0,2:T(2,128)(2,1)}), bf16[2,2,512,256]{3,1,0,2:T(2,128)(2,1)S(1)}, u32[]{:S(2)}, u32[]{:S(2)}) async-start(bf16[2,2,512,256]{3,1,0,2:T(2,128)(2,1)} %maximum_maximum_fusion), calls=%async_computation.1 | async-start | bytes 2097152 | tf_op jit(solution)/shard_map/all_to_all | solution.py:102
  183.3 29.4 %copy-start.83 = (s32[1,256]{1,0:T(1,128)S(1)}, s32[1,256]{1,0:T(1,128)}, u32[]{:S(2)}) copy-start(s32[1,256]{1,0:T(1,128)} %param.21) | copy-start | bytes 3076
  268.0 17.0 %slice-start.7 = ((s32[1,32768]{1,0:T(1,128)}), s32[1,16384]{1,0:T(1,128)S(1)}, s32[]{:S(2)}) async-start(s32[1,32768]{1,0:T(1,128)} %param.20), calls=%async_computation.13 | async-start | bytes 131072 | tf_op jit(solution)/shard_map/slice | solution.py:109
  278.1 56.8 %all-to-all-start.2 = ((bf16[16,2,16384]{2,1,0:T(2,128)(2,1)}), bf16[16,2,16384]{2,1,0:T(2,128)(2,1)S(1)}, u32[]{:S(2)}, u32[]{:S(2)}) async-start(bf16[16,2,16384]{2,1,0:T(2,128)(2,1)} %reshape.685), calls=%async_computation.2 | async-start | bytes 2097152 | tf_op jit(solution)/shard_map/all_to_all | solution.py:93
  285.0 43.6 %slice-start.6 = ((bf16[1,2,16,32768]{3,2,1,0:T(8,128)(2,1)}), bf16[1,2,16,16384]{3,2,1,0:T(8,128)(2,1)S(1)}, s32[]{:S(2)}) async-start(bf16[1,2,16,32768]{3,2,1,0:T(8,128)(2,1)} %param.22), calls=%async_computation.12 | async-start | bytes 2097152 | tf_op jit(solution)/shard_map/slice | solution.py:110
  357.2 61.9 %all-to-all-start.3 = ((bf16[1,2,512,512]{3,1,0,2:T(2,128)(2,1)}), bf16[1,2,512,512]{3,1,0,2:T(2,128)(2,1)S(1)}, u32[]{:S(2)}, u32[]{:S(2)}) async-start(bf16[1,2,512,512]{3,1,0,2:T(2,128)(2,1)} %pad_maximum_fusion.4), calls=%async_computation.3 | async-start | bytes 2097152 | tf_op jit(solution)/shard_map/all_to_all | solution.py:102
  456.5 25.5 %all-reduce.3.cloned.1.call-start = ((), (), s32[]{:S(2)}) async-start(), calls=%async_computation.5 | async-start | bytes 4194304 | tf_op jit(solution)/shard_map/psum | solution.py:64
  513.6 78.0 %all-to-all-start.4 = ((bf16[16,2,32768]{2,1,0:T(2,128)(2,1)}), bf16[16,2,32768]{2,1,0:T(2,128)(2,1)}, u32[]{:S(2)}, u32[]{:S(2)}) async-start(bf16[16,2,32768]{2,1,0:T(2,128)(2,1)} %reshape.687), calls=%async_computation.4 | async-start | bytes 4194304 | tf_op jit(solution)/shard_map/all_to_all | solution.py:119
  (75 other events, 482.1 us)
Sparse Core Ops, SparseCore 0:
  459.7 22.2 all-reduce.2
where the time goes:
time: 638 us; the launch traced here: 630 us
  other arithmetic  248 us (39%)
  local copies, waits for them, and re-layouts  183 us (29%)
  blocking collectives  65.3 us (10%)
  matrix products  54 us (8%)
  starting transfers between devices  36.8 us (6%)
  waiting for transfers between devices  25.4 us (4%)
  between operations  16.9 us (3%)
    add x6, other arithmetic, build_tiles(): tiles + jnp.where((offset == tap)[None], chosen, jnp.zeros((), jnp.bfloat...  126 us
    eq x6, other arithmetic, build_tiles(): offset == tap  93.5 us
    unnamed x210, local copies, waits for them, and re-layouts  77.3 us
    unnamed x1, blocking collectives  65.3 us
    dot_general x12, matrix products, product(): jnp.einsum('rnk,nka->rna', left, right, preferred_element_type=jnp.float32)  45.4 us
    psum x1, waiting for transfers between devices, pair_sum(): lax.psum(contribution.astype(jnp.float32).astype(jnp.bfloat16), 'aper')  24.8 us
    all_to_all x1, local copies, waits for them, and re-layouts, shards(): lax.all_to_all(focused.astype(jnp.bfloat16), 'panel', split_axis=2, conca...  17.8 us
    psum x1, local copies, waits for them, and re-layouts, pair_sum(): lax.psum(contribution.astype(jnp.float32).astype(jnp.bfloat16), 'aper')  17.1 us
  transfers between devices with their start and end apart: 6, of which 1 were waited for; matrix products, arithmetic and copies ran while one was open for 37% of the time, Pallas kernels for 0%

commit v1 on v0

v1 whole, which is shorter than its diff:
```python
import functools

import jax
import jax.numpy as jnp
from jax import lax
from jax.experimental import pallas as pl
from jax.experimental.pallas import tpu as pltpu
from jax.sharding import PartitionSpec as P

TILE = 128
PAIR = 2 * TILE
TAPS = 16
GRP_DEV = 4
F32 = jnp.float32
BF16 = jnp.bfloat16
VMEM_BYTES = 44 * 1024 * 1024


def aligned(value, step):
    return pl.multiple_of(value * step, step)


def params():
    return pltpu.CompilerParams(vmem_limit_bytes=VMEM_BYTES)


class Plan:
    def __init__(self, panels, rows, angles):
        self.panels = panels
        self.rows = rows
        self.total_rows = rows * panels
        self.in_blocks = angles // TILE
        self.own = self.in_blocks // panels
        self.cells = TILE // rows
        self.planes = panels // self.cells
        self.range_blocks = self.total_rows // TILE
        self.plane_window = min(self.cells * self.own + 4, self.in_blocks)
        self.panel_window = self.own + 4
        self.merged_window = 2 * self.own + 2
        self.out_blocks = 4 * self.own

    def plane_start(self, plane):
        return jnp.clip(
            self.cells * self.own * plane - 2, 0, self.in_blocks - self.plane_window
        )

    def panel_start(self, panel):
        return jnp.clip(self.own * panel - 2, 0, self.in_blocks - self.panel_window)

    def merged_start(self, panel):
        return jnp.clip(
            2 * self.own * panel - 1, 0, 2 * self.in_blocks - self.merged_window
        )


SMEM = pl.BlockSpec(memory_space=pltpu.SMEM)
VMEM = pl.BlockSpec(memory_space=pltpu.VMEM)


def pack_planes(plan, where, subimages):
    members = subimages.shape[0]

    def body(where_ref, x_ref, *outs):
        plane = where_ref[0] // plan.cells
        for step in range(plan.planes):
            start = plan.plane_start(lax.rem(plane + step, plan.planes))
            for member in range(members):
                out = outs[member * plan.planes + step]
                for block in range(plan.plane_window):
                    column = aligned(start + block, TILE)
                    for part in range(2):
                        at = block * PAIR + part * TILE
                        out[:, at : at + TILE] = x_ref[
                            member, part, :, pl.ds(column, TILE)
                        ]

    shape = jax.ShapeDtypeStruct((plan.rows, plan.plane_window * PAIR), BF16)
    outs = pl.pallas_call(
        body,
        out_shape=[shape] * (members * plan.planes),
        in_specs=[SMEM, VMEM],
        out_specs=[VMEM] * (members * plan.planes),
        compiler_params=params(),
        name="pack_planes",
    )(where, subimages)
    return [
        outs[member * plan.planes : (member + 1) * plan.planes]
        for member in range(members)
    ]


def pack_panels(plan, where, received):
    def body(where_ref, *refs):
        ins = refs[: plan.planes]
        outs = refs[plan.planes :]
        panel = where_ref[0]
        plane = panel // plan.cells
        cell = lax.rem(panel, plan.cells)
        base = plan.plane_start(plane)
        for flip in range(plan.cells):
            other = plane * plan.cells + (cell ^ flip)
            offset = plan.panel_start(other) - base
            for step in range(plan.planes):
                source = lax.rem(plane + plan.planes - step, plan.planes)
                outs[flip][source] = ins[step][
                    :, pl.ds(aligned(offset, PAIR), plan.panel_window * PAIR)
                ]

    shape = jax.ShapeDtypeStruct(
        (plan.planes, plan.rows, plan.panel_window * PAIR), BF16
    )
    return pl.pallas_call(
        body,
        out_shape=[shape] * plan.cells,
        in_specs=[SMEM] + [VMEM] * plan.planes,
        out_specs=[VMEM] * plan.cells,
        compiler_params=params(),
        name="pack_panels",
    )(where, *received)


def spread_taps(base, weights):
    low = base & (TAPS - 1)
    high = base >> 4
    wide = jnp.concatenate([weights, jnp.zeros_like(weights)], axis=0)
    for bit in range(4):
        moved = pltpu.roll(wide, 1 << bit, axis=0)
        wide = jnp.where(((low >> bit) & 1) == 1, moved, wide)
    zero = jnp.zeros_like(weights)
    pieces = []
    for place in range(PAIR // TAPS):
        below = jnp.where(high == place - 1, wide[TAPS:], zero)
        pieces.append(jnp.where(high == place, wide[:TAPS], below))
    return pieces


def build_angle(blocks, taps, weights):
    count = blocks.shape[0]

    def body(blocks_ref, taps_ref, weights_ref, out_ref):
        base = taps_ref[...]
        real = spread_taps(base, weights_ref[0].astype(F32))
        imag = spread_taps(base, weights_ref[1].astype(F32))
        half = TILE // TAPS
        for place in range(PAIR // TAPS):
            row = (place // half) * PAIR + (place % half) * TAPS
            re = real[place].astype(BF16)
            im = imag[place].astype(BF16)
            neg = (-imag[place]).astype(BF16)
            out_ref[0, row : row + TAPS, :TILE] = re
            out_ref[0, row : row + TAPS, TILE:] = im
            out_ref[0, TILE + row : TILE + row + TAPS, :TILE] = neg
            out_ref[0, TILE + row : TILE + row + TAPS, TILE:] = re

    return pl.pallas_call(
        body,
        out_shape=jax.ShapeDtypeStruct((count, 2 * PAIR, PAIR), BF16),
        grid_spec=pltpu.PrefetchScalarGridSpec(
            num_scalar_prefetch=1,
            grid=(count,),
            in_specs=[
                pl.BlockSpec((1, TILE), lambda i, t: (0, t[i])),
                pl.BlockSpec((2, TAPS, TILE), lambda i, t: (0, 0, t[i])),
            ],
            out_specs=pl.BlockSpec((1, 2 * PAIR, PAIR), lambda i, t: (i, 0, 0)),
        ),
        compiler_params=params(),
        name="build_angle",
    )(blocks, taps, weights)


def build_range(plan, taps, weights):
    slots = taps.shape[0]

    def body(taps_ref, weights_ref, out_ref):
        base = taps_ref[0]
        for part in range(2):
            pieces = spread_taps(base, weights_ref[0, part].astype(F32))
            matrix = jnp.concatenate(pieces, axis=0)
            out_ref[0, 0, part * TILE : (part + 1) * TILE, :] = matrix.T.astype(BF16)

    return pl.pallas_call(
        body,
        out_shape=jax.ShapeDtypeStruct((slots, plan.range_blocks, PAIR, PAIR), BF16),
        grid=(slots, plan.range_blocks),
        in_specs=[
            pl.BlockSpec((1, 1, TILE), lambda s, j: (s, 0, j)),
            pl.BlockSpec((1, 2, TAPS, TILE), lambda s, j: (s, 0, 0, j)),
        ],
        out_specs=pl.BlockSpec((1, 1, PAIR, PAIR), lambda s, j: (s, j, 0, 0)),
        compiler_params=params(),
        name="build_range",
    )(taps.reshape(slots, 1, -1), weights)


def range_step(plan, starts, matrices, source, target, blocks):
    for j in range(plan.range_blocks):
        rows = pl.ds(aligned(starts(j), TILE), PAIR)
        for block in range(blocks):
            at = block * PAIR
            res = jnp.dot(
                matrices[0, j], source[rows, at : at + PAIR], preferred_element_type=F32
            )
            real = res[:TILE, :TILE] - res[TILE:, TILE:]
            imag = res[:TILE, TILE:] + res[TILE:, :TILE]
            out = slice(j * TILE, (j + 1) * TILE)
            target[out, at : at + TILE] = real.astype(BF16)
            target[out, at + TILE : at + PAIR] = imag.astype(BF16)


def gather_rows(plan, panel, parts, target):
    cell = lax.rem(panel, plan.cells)
    for flip in range(plan.cells):
        source = cell ^ flip
        for plane in range(plan.planes):
            row = aligned(plane * plan.cells + source, plan.rows)
            target[pl.ds(row, plan.rows), :] = parts[flip][plane]


def first_member(plan, where, parts, rng_blocks, ang_blocks, rng_mats, ang_mats):
    def body(where_ref, rb_ref, ab_ref, *refs):
        ins = refs[: plan.cells]
        rm_ref, am_ref, out_ref, x_ref, z_ref = refs[plan.cells :]
        panel = where_ref[0]
        gather_rows(plan, panel, ins, x_ref)
        range_step(plan, lambda j: rb_ref[0, j], rm_ref, x_ref, z_ref, plan.panel_window)
        first = plan.merged_start(panel)
        base = plan.panel_start(panel)
        for j in range(plan.merged_window):
            start = ab_ref[0, first + j] - base
            out_ref[:, j * PAIR : (j + 1) * PAIR] = jnp.dot(
                z_ref[:, pl.ds(aligned(start, PAIR), 2 * PAIR)],
                am_ref[j],
                preferred_element_type=F32,
            )

    width = plan.panel_window * PAIR
    mwidth = plan.merged_window * PAIR
    return pl.pallas_call(
        body,
        out_shape=jax.ShapeDtypeStruct((plan.total_rows, mwidth), F32),
        grid=(1,),
        in_specs=[SMEM, SMEM, SMEM]
        + [VMEM] * plan.cells
        + [
            pl.BlockSpec((1, plan.range_blocks, PAIR, PAIR), lambda i: (0, 0, 0, 0)),
            pl.BlockSpec((plan.merged_window, 2 * PAIR, PAIR), lambda i: (0, 0, 0)),
        ],
        out_specs=VMEM,
        scratch_shapes=[pltpu.VMEM((plan.total_rows, width), BF16)] * 2,
        compiler_params=params(),
        name="first_member",
    )(where, rng_blocks, ang_blocks, *parts, rng_mats, ang_mats)


def second_member(
    plan, where, parts, partial, rng_blocks, ang_blocks, rng_mats, ang_mats, last_mats
):
    half = plan.total_rows // 2

    def body(where_ref, rb_ref, ab_ref, *refs):
        ins = refs[: plan.cells]
        (m_ref, rm_ref, r2_ref, am_ref, a2_ref, own_ref, send_ref) = refs[
            plan.cells : plan.cells + 7
        ]
        x_ref, z_ref, y_ref, s_ref = refs[plan.cells + 7 :]
        panel = where_ref[0]
        side = where_ref[1]
        gather_rows(plan, panel, ins, x_ref)
        range_step(plan, lambda j: rb_ref[1, j], rm_ref, x_ref, z_ref, plan.panel_window)
        first = plan.merged_start(panel)
        base = plan.panel_start(panel)
        for j in range(plan.merged_window):
            start = ab_ref[0, 2 * plan.in_blocks + first + j] - base
            term = jnp.dot(
                z_ref[:, pl.ds(aligned(start, PAIR), 2 * PAIR)],
                am_ref[j],
                preferred_element_type=F32,
            )
            at = slice(j * PAIR, (j + 1) * PAIR)
            y_ref[:, at] = (m_ref[:, at] + term).astype(BF16)
        range_step(plan, lambda j: rb_ref[2, j], r2_ref, y_ref, s_ref, plan.merged_window)
        for j in range(plan.out_blocks):
            place = 4 * plan.in_blocks + panel * plan.out_blocks + j
            columns = pl.ds(aligned(ab_ref[0, place] - first, PAIR), 2 * PAIR)
            for which, ref in ((1 - side, send_ref), (side, own_ref)):
                ref[:, j * PAIR : (j + 1) * PAIR] = jnp.dot(
                    s_ref[pl.ds(aligned(which, half), half), columns],
                    a2_ref[j],
                    preferred_element_type=F32,
                ).astype(BF16)

    width = plan.panel_window * PAIR
    mwidth = plan.merged_window * PAIR
    shape = jax.ShapeDtypeStruct((half, plan.out_blocks * PAIR), BF16)
    return pl.pallas_call(
        body,
        out_shape=[shape, shape],
        grid=(1,),
        in_specs=[SMEM, SMEM, SMEM]
        + [VMEM] * (plan.cells + 1)
        + [
            pl.BlockSpec((1, plan.range_blocks, PAIR, PAIR), lambda i: (1, 0, 0, 0)),
            pl.BlockSpec((1, plan.range_blocks, PAIR, PAIR), lambda i: (2, 0, 0, 0)),
            pl.BlockSpec((plan.merged_window, 2 * PAIR, PAIR), lambda i: (1, 0, 0)),
            VMEM,
        ],
        out_specs=[VMEM, VMEM],
        scratch_shapes=[pltpu.VMEM((plan.total_rows, width), BF16)] * 2
        + [pltpu.VMEM((plan.total_rows, mwidth), BF16)] * 2,
        compiler_params=params(),
        name="second_member",
    )(
        where,
        rng_blocks,
        ang_blocks,
        *parts,
        partial,
        rng_mats,
        rng_mats,
        ang_mats,
        last_mats,
    )


def focus(plan, where, own, other, owners, groups):
    half = plan.total_rows // 2
    columns = plan.out_blocks * TILE

    def body(where_ref, own_ref, oth_ref, owners_ref, image_ref, grad_ref):
        side = where_ref[1]
        row = lax.broadcasted_iota(jnp.int32, (half, TILE), 0) + side * half
        weight = 1.0 + 2.0 * row.astype(F32) / (plan.total_rows - 1)
        mine, theirs = [], []
        for j in range(plan.out_blocks):
            at = j * PAIR
            own_re = own_ref[:, at : at + TILE].astype(F32)
            own_im = own_ref[:, at + TILE : at + PAIR].astype(F32)
            oth_re = oth_ref[:, at : at + TILE].astype(F32)
            oth_im = oth_ref[:, at + TILE : at + PAIR].astype(F32)
            re = own_re + oth_re
            im = own_im + oth_im
            image_ref[0, :, j * TILE : (j + 1) * TILE] = re.astype(BF16)
            image_ref[1, :, j * TILE : (j + 1) * TILE] = im.astype(BF16)
            power = weight * (re * re + im * im)
            mine.append(
                jnp.sum(power * (re * own_re + im * own_im), axis=0, keepdims=True)
            )
            theirs.append(
                jnp.sum(power * (re * oth_re + im * oth_im), axis=0, keepdims=True)
            )
        mine = jnp.concatenate(mine, axis=1) / plan.total_rows
        theirs = jnp.concatenate(theirs, axis=1) / plan.total_rows
        zeroth = jnp.where(side == 0, mine, theirs)
        oneth = jnp.where(side == 0, theirs, mine)
        marks = owners_ref[...] == lax.broadcasted_iota(
            jnp.int32, (groups, columns), 0
        )
        for q, slope in ((0, zeroth), (1, oneth)):
            grad_ref[q] = jnp.sum(jnp.where(marks, slope, 0.0), axis=1, keepdims=True)

    return pl.pallas_call(
        body,
        out_shape=[
            jax.ShapeDtypeStruct((2, half, columns), BF16),
            jax.ShapeDtypeStruct((2, groups, 1), F32),
        ],
        in_specs=[SMEM, VMEM, VMEM, VMEM],
        out_specs=[VMEM, VMEM],
        compiler_params=params(),
        name="focus",
    )(where, own, other, owners)


def shards(subimages, rng_taps, rng_blocks, rng_weights, ang_taps, ang_blocks, ang_weights, owners):
    panels = lax.axis_size("panel")
    panel = lax.axis_index("panel").astype(jnp.int32)
    side = lax.axis_index("aper").astype(jnp.int32)
    groups = GRP_DEV * panels
    plan = Plan(panels, subimages.shape[2], subimages.shape[3])
    where = jnp.stack([panel, side])

    def plane_shift(step):
        return [
            (g * plan.cells + c, ((g + step) % plan.planes) * plan.cells + c)
            for g in range(plan.planes)
            for c in range(plan.cells)
        ]

    def cell_flip(flip):
        return [(i, i ^ flip) for i in range(panels)]

    sends = pack_planes(plan, where, subimages)
    windows = []
    after = None
    for pieces in sends:
        if after is not None:
            pieces, _ = lax.optimization_barrier((pieces, after))
        received = [pieces[0]] + [
            lax.ppermute(pieces[step], "panel", plane_shift(step))
            for step in range(1, plan.planes)
        ]
        after = received
        parts = pack_panels(plan, where, received)
        windows.append(
            [parts[0]]
            + [
                lax.ppermute(parts[flip], "panel", cell_flip(flip))
                for flip in range(1, plan.cells)
            ]
        )

    first = plan.merged_start(panel)
    near = first + jnp.arange(plan.merged_window, dtype=jnp.int32)
    merge_at = jnp.concatenate([near, 2 * plan.in_blocks + near])
    last_at = (
        4 * plan.in_blocks
        + panel * plan.out_blocks
        + jnp.arange(plan.out_blocks, dtype=jnp.int32)
    )
    ang_mats = build_angle(merge_at, ang_taps, ang_weights[0])
    last_mats = build_angle(last_at, ang_taps, ang_weights[0])
    rng_mats = build_range(plan, rng_taps[0], rng_weights[0])

    partial = first_member(
        plan, where, windows[0], rng_blocks[0], ang_blocks, rng_mats, ang_mats
    )
    own, send = second_member(
        plan, where, windows[1], partial, rng_blocks[0], ang_blocks, rng_mats, ang_mats, last_mats
    )
    other = lax.ppermute(send, "aper", [(0, 1), (1, 0)])
    columns = plan.out_blocks * TILE
    mine = lax.dynamic_slice_in_dim(owners[None], panel * columns, columns, 1)
    image, partials = focus(plan, where, own, other, mine, groups)
    pieces = lax.all_to_all(
        partials.reshape(2 * panels, GRP_DEV), ("aper", "panel"), 0, 0, tiled=True
    )
    return image, jnp.sum(pieces, axis=0)[None]


def solution(mesh):
    return jax.shard_map(
        shards,
        mesh=mesh,
        in_specs=(
            P(("scene", "aper"), None, "panel", None),
            P("aper", None, None),
            P("aper", None, None),
            P("aper", None, None, None, None),
            P("aper", None),
            P("aper", None),
            P("aper", None, None, None),
            P(),
        ),
        out_specs=(P(None, ("scene", "aper"), "panel"), P(("scene", "aper"), "panel")),
        check_vma=False,
    )
```

time: 638 us -> 93.4 us (0.15); the launches traced: 630 us -> 93.2 us
  other arithmetic: 248 us -> 0.81 us
  local copies, waits for them, and re-layouts: 183 us -> 4.6 us
  blocking collectives: 65.3 us -> 11.2 us
  matrix products: 54 us -> 0 us
  Pallas kernels: 0 us -> 21.8 us
  between operations: 16.9 us -> 0.83 us
  starting transfers between devices: 36.8 us -> 22 us
  waiting for transfers between devices: 25.4 us -> 31.8 us
    add x7 -> x2, other arithmetic: 126 us -> 0.01 us  [the longest x1 0.01 us: shards(): near = first + jnp.arange(plan.merged_window, dtype=jnp.int32)]
    eq x6 -> x0, other arithmetic: 93.5 us -> none  [build_tiles(): offset == tap]
    unnamed x210 -> x23, local copies, waits for them, and re-layouts: 77.3 us -> 3.82 us
    unnamed x1 -> x0, blocking collectives: 65.3 us -> none
    dot_general x24 -> x0, matrix products: 54 us -> none  [the longest x12 45.4 us: product(): jnp.einsum('rnk,nka->rna', left, right, preferred_element_type=jnp.float32)]
    all_to_all x5 -> x0, starting transfers between devices: 36.8 us -> none  [the longest x2 15.5 us: shards(): lax.all_to_all(current, 'panel', split_axis=3, concat_axis=2, tiled=True)]
    all_to_all x6 -> x1, local copies, waits for them, and re-layouts: 33.8 us -> 0.08 us  [shards(): lax.all_to_all(partials.reshape(2 * panels, GRP_DEV), ('aper', 'panel'),...]
    ppermute x0 -> x13, waiting for transfers between devices: none -> 31.8 us  [the longest x6 19.6 us: shards(): lax.ppermute(pieces[step], 'panel', plane_shift(step))]
  transfers between devices with their start and end apart: 6 -> 13, of which waited for: 1 -> 7; matrix products, arithmetic and copies ran while one was open for 37% -> 1% of each run, Pallas kernels for 0% -> 10%
where the time goes in v1:
time: 93.4 us; the launch traced here: 93.2 us
  waiting for transfers between devices  31.8 us (34%)
  starting transfers between devices  22 us (24%)
  Pallas kernels  21.8 us (23%)
  blocking collectives  11.2 us (12%)
  local copies, waits for them, and re-layouts  4.6 us (5%)
    ppermute x6, waiting for transfers between devices, shards(): lax.ppermute(pieces[step], 'panel', plane_shift(step))  19.6 us
    ppermute x6, starting transfers between devices, shards(): lax.ppermute(pieces[step], 'panel', plane_shift(step))  14.1 us
    all_to_all x1, blocking collectives, shards(): lax.all_to_all(partials.reshape(2 * panels, GRP_DEV), ('aper', 'panel'),...  11.2 us
    ppermute x6, waiting for transfers between devices, shards(): lax.ppermute(parts[flip], 'panel', cell_flip(flip))  10.3 us
    ppermute x6, starting transfers between devices, shards(): lax.ppermute(parts[flip], 'panel', cell_flip(flip))  7.91 us
    pallas_call x1, Pallas kernels, second_member(): pl.pallas_call(body, out_shape=[shape, shape], grid=(1,), in_specs=[SMEM,...  7.01 us
    unnamed x23, local copies, waits for them, and re-layouts  3.82 us
    pallas_call x2, Pallas kernels, pack_panels(): pl.pallas_call(body, out_shape=[shape] * plan.cells, in_specs=[SMEM] + [V...  3.23 us
  transfers between devices with their start and end apart: 13, of which 7 were waited for; matrix products, arithmetic and copies ran while one was open for 1% of the time, Pallas kernels for 10%

profile of v1, /device:TPU:0, one launch (start us, length us, event | category | flops | bytes accessed | tf_op | source)
XLA Modules:
  0.0 93.2 jit_solution(6379841976060427851)
XLA Ops:
  0.7 1.4 %copy-done.3 = bf16[2,2,32,4096]{3,2,1,0:T(8,128)(2,1)S(1)} copy-done((bf16[2,2,32,4096]{3,2,1,0:T(8,128)(2,1)S(1)}, bf16[2,2,32,4096]{3,2,1,0:T(8,128)(2,1)}, u32[]{:S(2)}) %copy-start.3) | copy-done | bytes 1048600
  2.1 1.0 %pack_planes.1 = (bf16[32,3072]{1,0:T(8,128)(2,1)S(1)}, bf16[32,3072]{1,0:T(8,128)(2,1)S(1)}, bf16[32,3072]{1,0:T(8,128)(2,1)S(1)}, bf16[32,3072]{1,0:T(8,128)(2...) custom-call(s32[2]{0:T(128)S(1)} %pad_add_fusion.where_ref, ...), custom_call_target="tpu_custom_call" | custom-call | tf_op jit(solution)/shard_map/pack_planes/pallas_call | solution.py:78
  3.1 3.1 %collective-permute-start = (bf16[32,3072]{1,0:T(8,128)(2,1)S(1)}, bf16[32,3072]{1,0:T(8,128)(2,1)S(1)}, u32[]{:S(2)}, u32[]{:S(2)}) collective-permute-start(bf16[32,3072]{1,0:T(8,128)(2,1)S(1)} %get-tuple-element.31), channel_id=1, source_target_pairs={{0,8},{2,10},{4,12},{6,14},{8,16},{10,18},{12,20},{14,22},{16,24},... | collective-permute-start | bytes 589832 | tf_op jit(solution)/shard_map/ppermute | solution.py:400
  6.1 2.6 %collective-permute-start.1 = (bf16[32,3072]{1,0:T(8,128)(2,1)S(1)}, bf16[32,3072]{1,0:T(8,128)(2,1)S(1)}, u32[]{:S(2)}, u32[]{:S(2)}) collective-permute-start(bf16[32,3072]{1,0:T(8,128)(2,1)S(1)} %get-tuple-element.32), channel_id=1, source_target_pairs={{0,16},{2,18},{4,20},{6,22},{8,24},{10,26},{12,28},{14,30},{16,0},... | collective-permute-start | bytes 589832 | tf_op jit(solution)/shard_map/ppermute | solution.py:400
  8.7 1.3 %collective-permute-start.2 = (bf16[32,3072]{1,0:T(8,128)(2,1)S(1)}, bf16[32,3072]{1,0:T(8,128)(2,1)S(1)}, u32[]{:S(2)}, u32[]{:S(2)}) collective-permute-start(bf16[32,3072]{1,0:T(8,128)(2,1)S(1)} %get-tuple-element.33), channel_id=1, source_target_pairs={{0,24},{2,26},{4,28},{6,30},{8,0},{10,2},{12,4},{14,6},{16,8},{18,... | collective-permute-start | bytes 589832 | tf_op jit(solution)/shard_map/ppermute | solution.py:400
  10.1 3.9 %collective-permute-done.refs_1_ = bf16[32,3072]{1,0:T(8,128)(2,1)S(1)} collective-permute-done((bf16[32,3072]{1,0:T(8,128)(2,1)S(1)}, bf16[32,3072]{1,0:T(8,128)(2,1)S(1)}, u32[]{:S(2)}, u32[]{:S(2)}) %collective-permute-start) | collective-permute-done | bytes 196640 | tf_op jit(solution)/shard_map/ppermute | solution.py:400
  14.0 7.6 %collective-permute-done.1.refs_2_ = bf16[32,3072]{1,0:T(8,128)(2,1)S(1)} collective-permute-done((bf16[32,3072]{1,0:T(8,128)(2,1)S(1)}, bf16[32,3072]{1,0:T(8,128)(2,1)S(1)}, u32[]{:S(2)}, u32[]{:S(2)}) %collective-permute-start.1) | collective-permute-done | bytes 196640 | tf_op jit(solution)/shard_map/ppermute | solution.py:400
  21.6 1.5 %pack_panels.3 = (bf16[4,32,1536]{2,1,0:T(8,128)(2,1)S(1)}, bf16[4,32,1536]{2,1,0:T(8,128)(2,1)}, bf16[4,32,1536]{2,1,0:T(8,128)(2,1)S(1)}, bf16[4,32,1536]{2,1,0:T(8,128)(2,1)}) custom-call(s32[2]{0:T(128)S(1)} %pad_add_fusion.where_ref, bf16[32,3072]{1,0:T(8,128)(2,1)S(1)} %get-tuple-element.30.refs_0_, bf16[32,3072]{1,0:T(8,128)(2,1)S(1)} %collective-permute-done.refs_1_, ...), custom_call_target="tpu_custom_call" | custom-call | tf_op jit(solution)/shard_map/pack_panels/pallas_call | solution.py:112
  23.2 1.5 %collective-permute-start.10 = (bf16[4,32,1536]{2,1,0:T(8,128)(2,1)S(1)}, bf16[4,32,1536]{2,1,0:T(8,128)(2,1)S(1)}, u32[]{:S(2)}, u32[]{:S(2)}) collective-permute-start(bf16[4,32,1536]{2,1,0:T(8,128)(2,1)S(1)} %get-tuple-element.44), channel_id=1, source_target_pairs={{0,4},{2,6},{4,0},{6,2},{8,12},{10,14},{12,8},{14,10},{16,20},{18,... | collective-permute-start | bytes 1179656 | tf_op jit(solution)/shard_map/ppermute | solution.py:408
  24.6 4.7 %collective-permute-start.3 = (bf16[32,3072]{1,0:T(8,128)(2,1)S(1)}, bf16[32,3072]{1,0:T(8,128)(2,1)S(1)}, u32[]{:S(2)}, u32[]{:S(2)}) collective-permute-start(bf16[32,3072]{1,0:T(8,128)(2,1)S(1)} %get-tuple-element.35), channel_id=1, source_target_pairs={{0,8},{2,10},{4,12},{6,14},{8,16},{10,18},{12,20},{14,22},{16,24},... | collective-permute-start | bytes 589832 | tf_op jit(solution)/shard_map/ppermute | solution.py:400
  29.3 1.6 %collective-permute-start.4 = (bf16[32,3072]{1,0:T(8,128)(2,1)S(1)}, bf16[32,3072]{1,0:T(8,128)(2,1)S(1)}, u32[]{:S(2)}, u32[]{:S(2)}) collective-permute-start(bf16[32,3072]{1,0:T(8,128)(2,1)S(1)} %get-tuple-element.36), channel_id=1, source_target_pairs={{0,16},{2,18},{4,20},{6,22},{8,24},{10,26},{12,28},{14,30},{16,0},... | collective-permute-start | bytes 589832 | tf_op jit(solution)/shard_map/ppermute | solution.py:400
  31.0 0.7 collective-permute-start.5
  31.7 1.4 %collective-permute-start.11 = (bf16[4,32,1536]{2,1,0:T(8,128)(2,1)}, bf16[4,32,1536]{2,1,0:T(8,128)(2,1)S(1)}, u32[]{:S(2)}, u32[]{:S(2)}) collective-permute-start(bf16[4,32,1536]{2,1,0:T(8,128)(2,1)} %get-tuple-element.45), channel_id=1, source_target_pairs={{0,6},{2,4},{4,2},{6,0},{8,14},{10,12},{12,10},{14,8},{16,22},{18,... | collective-permute-start | bytes 1179656 | tf_op jit(solution)/shard_map/ppermute | solution.py:408
  33.1 3.2 %collective-permute-done.3.refs_1_ = bf16[32,3072]{1,0:T(8,128)(2,1)S(1)} collective-permute-done((bf16[32,3072]{1,0:T(8,128)(2,1)S(1)}, bf16[32,3072]{1,0:T(8,128)(2,1)S(1)}, u32[]{:S(2)}, u32[]{:S(2)}) %collective-permute-start.3) | collective-permute-done | bytes 196640 | tf_op jit(solution)/shard_map/ppermute | solution.py:400
  36.3 1.5 %collective-permute-start.9 = (bf16[4,32,1536]{2,1,0:T(8,128)(2,1)}, bf16[4,32,1536]{2,1,0:T(8,128)(2,1)}, u32[]{:S(2)}, u32[]{:S(2)}) collective-permute-start(bf16[4,32,1536]{2,1,0:T(8,128)(2,1)} %get-tuple-element.43), channel_id=1, source_target_pairs={{0,2},{2,0},{4,6},{6,4},{8,10},{10,8},{12,14},{14,12},{16,18},{18,... | collective-permute-start | bytes 1179656 | tf_op jit(solution)/shard_map/ppermute | solution.py:408
  37.8 4.9 %collective-permute-done.4.refs_2_ = bf16[32,3072]{1,0:T(8,128)(2,1)S(1)} collective-permute-done((bf16[32,3072]{1,0:T(8,128)(2,1)S(1)}, bf16[32,3072]{1,0:T(8,128)(2,1)S(1)}, u32[]{:S(2)}, u32[]{:S(2)}) %collective-permute-start.4) | collective-permute-done | bytes 196640 | tf_op jit(solution)/shard_map/ppermute | solution.py:400
  42.7 1.7 %pack_panels.2 = (bf16[4,32,1536]{2,1,0:T(8,128)(2,1)S(1)}, bf16[4,32,1536]{2,1,0:T(8,128)(2,1)}, bf16[4,32,1536]{2,1,0:T(8,128)(2,1)}, bf16[4,32,1536]{2,1,0:T(8,128)(2,1)}) custom-call(s32[2]{0:T(128)S(1)} %pad_add_fusion.where_ref, bf16[32,3072]{1,0:T(8,128)(2,1)S(1)} %get-tuple-element.34.refs_0_, bf16[32,3072]{1,0:T(8,128)(2,1)S(1)} %collective-permute-done.3.refs_1_, ...), custom_call_target="tpu_custom_call" | custom-call | tf_op jit(solution)/shard_map/pack_panels/pallas_call | solution.py:112
  44.3 0.7 copy-done.5
  45.1 1.5 %collective-permute-start.6 = (bf16[4,32,1536]{2,1,0:T(8,128)(2,1)}, bf16[4,32,1536]{2,1,0:T(8,128)(2,1)}, u32[]{:S(2)}, u32[]{:S(2)}) collective-permute-start(bf16[4,32,1536]{2,1,0:T(8,128)(2,1)} %get-tuple-element.39), channel_id=1, source_target_pairs={{0,2},{2,0},{4,6},{6,4},{8,10},{10,8},{12,14},{14,12},{16,18},{18,... | collective-permute-start | bytes 1179656 | tf_op jit(solution)/shard_map/ppermute | solution.py:408
  47.1 1.5 %collective-permute-start.8 = (bf16[4,32,1536]{2,1,0:T(8,128)(2,1)}, bf16[4,32,1536]{2,1,0:T(8,128)(2,1)}, u32[]{:S(2)}, u32[]{:S(2)}) collective-permute-start(bf16[4,32,1536]{2,1,0:T(8,128)(2,1)} %get-tuple-element.41), channel_id=1, source_target_pairs={{0,6},{2,4},{4,2},{6,0},{8,14},{10,12},{12,10},{14,8},{16,22},{18,... | collective-permute-start | bytes 1179656 | tf_op jit(solution)/shard_map/ppermute | solution.py:408
  48.7 1.5 %build_angle.2.refs_5_.refs_7_ = bf16[12,512,256]{2,1,0:T(8,128)(2,1)S(1)} custom-call(s32[12]{0:T(128)S(1)} %pad_add_fusion.1.blocks_ref, s32[1,32768]{1,0:T(1,128)S(1)} %copy-done.4, bf16[2,16,32768]{2,1,0:T(8,128)(2,1)S(1)} %bitcast.11), custom_call_target="tpu_custom_call" | custom-call | tf_op jit(solution)/shard_map/build_angle/pallas_call | solution.py:155
  50.3 1.2 %build_angle.3.refs_8_ = bf16[8,512,256]{2,1,0:T(8,128)(2,1)S(1)} custom-call(s32[8]{0:T(128)S(1)} %iota_add_fusion.blocks_ref, s32[1,32768]{1,0:T(1,128)S(1)} %copy-done.4, bf16[2,16,32768]{2,1,0:T(8,128)(2,1)S(1)} %bitcast.12), custom_call_target="tpu_custom_call" | custom-call | tf_op jit(solution)/shard_map/build_angle/pallas_call | solution.py:155
  51.5 1.7 %build_range.1.refs_4_.refs_5_.refs_6_ = bf16[3,4,256,256]{3,2,1,0:T(8,128)(2,1)S(1)} custom-call(s32[3,1,512]{2,1,0:T(1,128)S(1)} %bitcast.17, bf16[3,2,16,512]{3,2,1,0:T(8,128)(2,1)S(1)} %bitcast.13), custom_call_target="tpu_custom_call" | custom-call | tf_op jit(solution)/shard_map/build_range/pallas_call | solution.py:182
  53.3 3.1 %first_member.1.refs_4_ = f32[512,1536]{1,0:T(8,128)S(1)} custom-call(s32[2]{0:T(128)S(1)} %pad_add_fusion.where_ref, s32[3,4]{1,0:T(4,128)S(1)} %bitcast.14, s32[1,256]{1,0:T(1,128)S(1)} %copy-done.9, bf16[4,32,1536]{2,1,0:T(8,128)(2,1)S(1)} %get-tuple-element.42.refs_0_, bf16[4,32,1536]{2,1,0:T(8,128)(2,1)} %collective-permute-done.9.refs_1_, ...), custom_call_target="tpu_custom_call" | custom-call | tf_op jit(solution)/shard_map/first_member/pallas_call | solution.py:239
  56.4 1.7 %copy-done.1 = f32[512,1536]{1,0:T(8,128)} copy-done((f32[512,1536]{1,0:T(8,128)}, f32[512,1536]{1,0:T(8,128)S(1)}, u32[]{:S(2)}) %copy-start.1) | copy-done | bytes 3145752
  58.1 2.8 %collective-permute-done.6.refs_1_ = bf16[4,32,1536]{2,1,0:T(8,128)(2,1)} collective-permute-done((bf16[4,32,1536]{2,1,0:T(8,128)(2,1)}, bf16[4,32,1536]{2,1,0:T(8,128)(2,1)}, u32[]{:S(2)}, u32[]{:S(2)}) %collective-permute-start.6) | collective-permute-done | bytes 393248 | tf_op jit(solution)/shard_map/ppermute | solution.py:408
  60.9 7.5 %collective-permute-done.8.refs_3_ = bf16[4,32,1536]{2,1,0:T(8,128)(2,1)} collective-permute-done((bf16[4,32,1536]{2,1,0:T(8,128)(2,1)}, bf16[4,32,1536]{2,1,0:T(8,128)(2,1)}, u32[]{:S(2)}, u32[]{:S(2)}) %collective-permute-start.8) | collective-permute-done | bytes 393248 | tf_op jit(solution)/shard_map/ppermute | solution.py:408
  68.4 7.0 %second_member.1 = (bf16[256,2048]{1,0:T(8,128)(2,1)S(1)}, bf16[256,2048]{1,0:T(8,128)(2,1)S(1)}) custom-call(s32[2]{0:T(128)S(1)} %pad_add_fusion.where_ref, s32[3,4]{1,0:T(4,128)S(1)} %bitcast.15, s32[1,256]{1,0:T(1,128)S(1)} %copy-done.9, bf16[4,32,1536]{2,1,0:T(8,128)(2,1)S(1)} %copy-done.6, bf16[4,32,1536]{2,1,0:T(8,128)(2,1)} %collective-permute-done.6.refs_1_, ...), custom_call_target="tpu_custom_call" | custom-call | tf_op jit(solution)/shard_map/second_member/pallas_call | solution.py:296
  75.5 0.7 dynamic-slice.3
  76.2 1.9 %collective-permute-done.12.oth_ref = bf16[256,2048]{1,0:T(8,128)(2,1)S(1)} collective-permute-done((bf16[256,2048]{1,0:T(8,128)(2,1)S(1)}, bf16[256,2048]{1,0:T(8,128)(2,1)S(1)}, u32[]{:S(2)}, u32[]{:S(2)}) %collective-permute-start.12) | collective-permute-done | bytes 1048608 | tf_op jit(solution)/shard_map/ppermute | solution.py:431
  78.1 3.1 %focus.1 = (bf16[2,256,1024]{2,1,0:T(8,128)(2,1)}, f32[2,64,1]{2,1,0:T(8,128)S(1)}) custom-call(s32[2]{0:T(128)S(1)} %pad_add_fusion.where_ref, bf16[256,2048]{1,0:T(8,128)(2,1)S(1)} %get-tuple-element.46.own_ref, bf16[256,2048]{1,0:T(8,128)(2,1)S(1)} %collective-permute-done.12.oth_ref, s32[1,1024]{1,0:T(1,128)S(1)} %bitcast.16), custom_call_target="tpu_custom_call" | custom-call | tf_op jit(solution)/shard_map/focus/pallas_call | solution.py:362
  81.4 11.2 %all_to_all.9 = f32[32,1,4]{2,1,0:T(1,128)S(1)} all-to-all(f32[32,1,4]{2,1,0:T(1,128)S(1)} %bitcast.18), channel_id=1, replica_groups=mesh['scene'=1,'panel'=16,'aper'=2] {'aper','panel'}, dimensions={0} | all-to-all | bytes 1024 | tf_op jit(solution)/shard_map/all_to_all | solution.py:435
  (35 shorter events, 1.5 us)
Async XLA Ops:
  0.6 48.0 %copy-start.2 = (bf16[1,2,16,32768]{3,2,1,0:T(8,128)(2,1)S(1)}, bf16[1,2,16,32768]{3,2,1,0:T(8,128)(2,1)}, u32[]{:S(2)}) copy-start(bf16[1,2,16,32768]{3,2,1,0:T(8,128)(2,1)} %param.14) | copy-start | bytes 6291460
  0.7 1.4 %copy-start.3 = (bf16[2,2,32,4096]{3,2,1,0:T(8,128)(2,1)S(1)}, bf16[2,2,32,4096]{3,2,1,0:T(8,128)(2,1)}, u32[]{:S(2)}) copy-start(bf16[2,2,32,4096]{3,2,1,0:T(8,128)(2,1)} %x_ref.1) | copy-start | bytes 3145732
  2.1 46.5 %copy-start.10 = (s32[1,3,4]{2,0,1:T(1,128)S(1)}, s32[1,3,4]{2,0,1:T(1,128)}, u32[]{:S(2)}) copy-start(s32[1,3,4]{2,0,1:T(1,128)} %param.10) | copy-start | bytes 148
  2.1 46.6 %copy-start.4 = (s32[1,32768]{1,0:T(1,128)S(1)}, s32[1,32768]{1,0:T(1,128)}, u32[]{:S(2)}) copy-start(s32[1,32768]{1,0:T(1,128)} %taps_ref.3) | copy-start | bytes 393220
  3.1 11.0 %collective-permute-start = (bf16[32,3072]{1,0:T(8,128)(2,1)S(1)}, bf16[32,3072]{1,0:T(8,128)(2,1)S(1)}, u32[]{:S(2)}, u32[]{:S(2)}) collective-permute-start(bf16[32,3072]{1,0:T(8,128)(2,1)S(1)} %get-tuple-element.31), channel_id=1, source_target_pairs={{0,8},{2,10},{4,12},{6,14},{8,16},{10,18},{12,20},{14,22},{16,24},... | collective-permute-start | bytes 589832 | tf_op jit(solution)/shard_map/ppermute | solution.py:400
  6.1 15.5 %collective-permute-start.1 = (bf16[32,3072]{1,0:T(8,128)(2,1)S(1)}, bf16[32,3072]{1,0:T(8,128)(2,1)S(1)}, u32[]{:S(2)}, u32[]{:S(2)}) collective-permute-start(bf16[32,3072]{1,0:T(8,128)(2,1)S(1)} %get-tuple-element.32), channel_id=1, source_target_pairs={{0,16},{2,18},{4,20},{6,22},{8,24},{10,26},{12,28},{14,30},{16,0},... | collective-permute-start | bytes 589832 | tf_op jit(solution)/shard_map/ppermute | solution.py:400
  8.7 12.9 %collective-permute-start.2 = (bf16[32,3072]{1,0:T(8,128)(2,1)S(1)}, bf16[32,3072]{1,0:T(8,128)(2,1)S(1)}, u32[]{:S(2)}, u32[]{:S(2)}) collective-permute-start(bf16[32,3072]{1,0:T(8,128)(2,1)S(1)} %get-tuple-element.33), channel_id=1, source_target_pairs={{0,24},{2,26},{4,28},{6,30},{8,0},{10,2},{12,4},{14,6},{16,8},{18,... | collective-permute-start | bytes 589832 | tf_op jit(solution)/shard_map/ppermute | solution.py:400
  23.2 23.9 %collective-permute-start.10 = (bf16[4,32,1536]{2,1,0:T(8,128)(2,1)S(1)}, bf16[4,32,1536]{2,1,0:T(8,128)(2,1)S(1)}, u32[]{:S(2)}, u32[]{:S(2)}) collective-permute-start(bf16[4,32,1536]{2,1,0:T(8,128)(2,1)S(1)} %get-tuple-element.44), channel_id=1, source_target_pairs={{0,4},{2,6},{4,0},{6,2},{8,12},{10,14},{12,8},{14,10},{16,20},{18,... | collective-permute-start | bytes 1179656 | tf_op jit(solution)/shard_map/ppermute | solution.py:408
  24.6 11.7 %collective-permute-start.3 = (bf16[32,3072]{1,0:T(8,128)(2,1)S(1)}, bf16[32,3072]{1,0:T(8,128)(2,1)S(1)}, u32[]{:S(2)}, u32[]{:S(2)}) collective-permute-start(bf16[32,3072]{1,0:T(8,128)(2,1)S(1)} %get-tuple-element.35), channel_id=1, source_target_pairs={{0,8},{2,10},{4,12},{6,14},{8,16},{10,18},{12,20},{14,22},{16,24},... | collective-permute-start | bytes 589832 | tf_op jit(solution)/shard_map/ppermute | solution.py:400
  29.3 13.3 %collective-permute-start.4 = (bf16[32,3072]{1,0:T(8,128)(2,1)S(1)}, bf16[32,3072]{1,0:T(8,128)(2,1)S(1)}, u32[]{:S(2)}, u32[]{:S(2)}) collective-permute-start(bf16[32,3072]{1,0:T(8,128)(2,1)S(1)} %get-tuple-element.36), channel_id=1, source_target_pairs={{0,16},{2,18},{4,20},{6,22},{8,24},{10,26},{12,28},{14,30},{16,0},... | collective-permute-start | bytes 589832 | tf_op jit(solution)/shard_map/ppermute | solution.py:400
  31.0 11.7 %collective-permute-start.5 = (bf16[32,3072]{1,0:T(8,128)(2,1)S(1)}, bf16[32,3072]{1,0:T(8,128)(2,1)S(1)}, u32[]{:S(2)}, u32[]{:S(2)}) collective-permute-start(bf16[32,3072]{1,0:T(8,128)(2,1)S(1)} %get-tuple-element.37), channel_id=1, source_target_pairs={{0,24},{2,26},{4,28},{6,30},{8,0},{10,2},{12,4},{14,6},{16,8},{18,... | collective-permute-start | bytes 589832 | tf_op jit(solution)/shard_map/ppermute | solution.py:400
  31.7 21.5 %collective-permute-start.11 = (bf16[4,32,1536]{2,1,0:T(8,128)(2,1)}, bf16[4,32,1536]{2,1,0:T(8,128)(2,1)S(1)}, u32[]{:S(2)}, u32[]{:S(2)}) collective-permute-start(bf16[4,32,1536]{2,1,0:T(8,128)(2,1)} %get-tuple-element.45), channel_id=1, source_target_pairs={{0,6},{2,4},{4,2},{6,0},{8,14},{10,12},{12,10},{14,8},{16,22},{18,... | collective-permute-start | bytes 1179656 | tf_op jit(solution)/shard_map/ppermute | solution.py:408
  36.3 16.9 %collective-permute-start.9 = (bf16[4,32,1536]{2,1,0:T(8,128)(2,1)}, bf16[4,32,1536]{2,1,0:T(8,128)(2,1)}, u32[]{:S(2)}, u32[]{:S(2)}) collective-permute-start(bf16[4,32,1536]{2,1,0:T(8,128)(2,1)} %get-tuple-element.43), channel_id=1, source_target_pairs={{0,2},{2,0},{4,6},{6,4},{8,10},{10,8},{12,14},{14,12},{16,18},{18,... | collective-permute-start | bytes 1179656 | tf_op jit(solution)/shard_map/ppermute | solution.py:408
  44.3 0.7 copy-start.5
  45.1 15.8 %collective-permute-start.6 = (bf16[4,32,1536]{2,1,0:T(8,128)(2,1)}, bf16[4,32,1536]{2,1,0:T(8,128)(2,1)}, u32[]{:S(2)}, u32[]{:S(2)}) collective-permute-start(bf16[4,32,1536]{2,1,0:T(8,128)(2,1)} %get-tuple-element.39), channel_id=1, source_target_pairs={{0,2},{2,0},{4,6},{6,4},{8,10},{10,8},{12,14},{14,12},{16,18},{18,... | collective-permute-start | bytes 1179656 | tf_op jit(solution)/shard_map/ppermute | solution.py:408
  46.6 14.3 %collective-permute-start.7 = (bf16[4,32,1536]{2,1,0:T(8,128)(2,1)}, bf16[4,32,1536]{2,1,0:T(8,128)(2,1)}, u32[]{:S(2)}, u32[]{:S(2)}) collective-permute-start(bf16[4,32,1536]{2,1,0:T(8,128)(2,1)} %get-tuple-element.40), channel_id=1, source_target_pairs={{0,4},{2,6},{4,0},{6,2},{8,12},{10,14},{12,8},{14,10},{16,20},{18,... | collective-permute-start | bytes 1179656 | tf_op jit(solution)/shard_map/ppermute | solution.py:408
  47.1 21.3 %collective-permute-start.8 = (bf16[4,32,1536]{2,1,0:T(8,128)(2,1)}, bf16[4,32,1536]{2,1,0:T(8,128)(2,1)}, u32[]{:S(2)}, u32[]{:S(2)}) collective-permute-start(bf16[4,32,1536]{2,1,0:T(8,128)(2,1)} %get-tuple-element.41), channel_id=1, source_target_pairs={{0,6},{2,4},{4,2},{6,0},{8,14},{10,12},{12,10},{14,8},{16,22},{18,... | collective-permute-start | bytes 1179656 | tf_op jit(solution)/shard_map/ppermute | solution.py:408
  50.2 3.0 %copy-start = (bf16[12,512,256]{2,1,0:T(8,128)(2,1)}, bf16[12,512,256]{2,1,0:T(8,128)(2,1)S(1)}, u32[]{:S(2)}) copy-start(bf16[12,512,256]{2,1,0:T(8,128)(2,1)S(1)} %build_angle.2.refs_5_.refs_7_) | copy-start | bytes 9437188
  50.2 1.3 %copy-start.7 = (bf16[1,3,2,16,512]{4,3,2,1,0:T(8,128)(2,1)S(1)}, bf16[1,3,2,16,512]{4,3,2,1,0:T(8,128)(2,1)}, u32[]{:S(2)}) copy-start(bf16[1,3,2,16,512]{4,3,2,1,0:T(8,128)(2,1)} %param.11) | copy-start | bytes 294916
  50.2 1.3 %copy-start.8 = (s32[1,3,512]{2,0,1:T(1,128)S(1)}, s32[1,3,512]{2,0,1:T(1,128)}, u32[]{:S(2)}) copy-start(s32[1,3,512]{2,0,1:T(1,128)} %param.9) | copy-start | bytes 18436
  50.2 3.0 %copy-start.9 = (s32[1,256]{1,0:T(1,128)S(1)}, s32[1,256]{1,0:T(1,128)}, u32[]{:S(2)}) copy-start(s32[1,256]{1,0:T(1,128)} %ab_ref.3) | copy-start | bytes 3076
  53.3 15.1 %copy-start.6 = (bf16[4,32,1536]{2,1,0:T(8,128)(2,1)S(1)}, bf16[4,32,1536]{2,1,0:T(8,128)(2,1)}, u32[]{:S(2)}) copy-start(bf16[4,32,1536]{2,1,0:T(8,128)(2,1)} %copy-done.5) | copy-start | bytes 1179652
  56.4 1.7 %copy-start.1 = (f32[512,1536]{1,0:T(8,128)}, f32[512,1536]{1,0:T(8,128)S(1)}, u32[]{:S(2)}) copy-start(f32[512,1536]{1,0:T(8,128)S(1)} %first_member.1.refs_4_) | copy-start | bytes 9437188
  75.4 2.7 %collective-permute-start.12 = (bf16[256,2048]{1,0:T(8,128)(2,1)S(1)}, bf16[256,2048]{1,0:T(8,128)(2,1)S(1)}, u32[]{:S(2)}, u32[]{:S(2)}) collective-permute-start(bf16[256,2048]{1,0:T(8,128)(2,1)S(1)} %get-tuple-element.47), channel_id=1, source_target_pairs={{0,1},{1,0},{2,3},{3,2},{4,5},{5,4},{6,7},{7,6},{8,9},{9,8},{10,11... | collective-permute-start | bytes 3145736 | tf_op jit(solution)/shard_map/ppermute | solution.py:431

commit v2 on v1

--- a/solution.py
+++ b/solution.py
@@ -1,5 +1,3 @@
-import functools
-
 import jax
 import jax.numpy as jnp
 from jax import lax
@@ -55,65 +53,68 @@
 
 SMEM = pl.BlockSpec(memory_space=pltpu.SMEM)
 VMEM = pl.BlockSpec(memory_space=pltpu.VMEM)
-
-
-def pack_planes(plan, where, subimages):
+ANY = pl.BlockSpec(memory_space=pltpu.HBM)
+
+
+def pack_own(plan, where, subimages):
     members = subimages.shape[0]
+    others = plan.planes - 1
 
     def body(where_ref, x_ref, *outs):
-        plane = where_ref[0] // plan.cells
-        for step in range(plan.planes):
-            start = plan.plane_start(lax.rem(plane + step, plan.planes))
-            for member in range(members):
-                out = outs[member * plan.planes + step]
-                for block in range(plan.plane_window):
-                    column = aligned(start + block, TILE)
-                    for part in range(2):
-                        at = block * PAIR + part * TILE
-                        out[:, at : at + TILE] = x_ref[
-                            member, part, :, pl.ds(column, TILE)
-                        ]
-
-    shape = jax.ShapeDtypeStruct((plan.rows, plan.plane_window * PAIR), BF16)
+        panel = where_ref[0]
+        plane = panel // plan.cells
+        cell = lax.rem(panel, plan.cells)
+        for step in range(1, plan.planes):
+            target = lax.rem(plane + step, plan.planes)
+            column = aligned(plan.plane_start(target), TILE)
+            outs[step - 1][...] = x_ref[
+                :, :, :, pl.ds(column, plan.plane_window * TILE)
+            ]
+        for flip in range(1, plan.cells):
+            target = plane * plan.cells + (cell ^ flip)
+            column = aligned(plan.panel_start(target), TILE)
+            outs[others + flip - 1][0] = x_ref[
+                :, :, :, pl.ds(column, plan.panel_window * TILE)
+            ]
+
+    lead = (members, 2, plan.rows)
+    far = jax.ShapeDtypeStruct(lead + (plan.plane_window * TILE,), BF16)
+    near = jax.ShapeDtypeStruct((1,) + lead + (plan.panel_window * TILE,), BF16)
     outs = pl.pallas_call(
         body,
-        out_shape=[shape] * (members * plan.planes),
+        out_shape=[far] * others + [near] * (plan.cells - 1),
         in_specs=[SMEM, VMEM],
-        out_specs=[VMEM] * (members * plan.planes),
-        compiler_params=params(),
-        name="pack_planes",
+        out_specs=[VMEM] * (others + plan.cells - 1),
+        compiler_params=params(),
+        name="pack_own",
     )(where, subimages)
-    return [
-        outs[member * plan.planes : (member + 1) * plan.planes]
-        for member in range(members)
-    ]
+    return outs[:others], outs[others:]
 
 
 def pack_panels(plan, where, received):
+    count = len(received)
+
     def body(where_ref, *refs):
-        ins = refs[: plan.planes]
-        outs = refs[plan.planes :]
+        ins, outs = refs[:count], refs[count:]
         panel = where_ref[0]
         plane = panel // plan.cells
         cell = lax.rem(panel, plan.cells)
         base = plan.plane_start(plane)
-        for flip in range(plan.cells):
-            other = plane * plan.cells + (cell ^ flip)
-            offset = plan.panel_start(other) - base
-            for step in range(plan.planes):
-                source = lax.rem(plane + plan.planes - step, plan.planes)
-                outs[flip][source] = ins[step][
-                    :, pl.ds(aligned(offset, PAIR), plan.panel_window * PAIR)
-                ]
-
+        for flip in range(1, plan.cells):
+            offset = plan.panel_start(plane * plan.cells + (cell ^ flip)) - base
+            columns = pl.ds(aligned(offset, TILE), plan.panel_window * TILE)
+            for at in range(count):
+                outs[flip - 1][at] = ins[at][:, :, :, columns]
+
+    lead = received[0].shape[:3]
     shape = jax.ShapeDtypeStruct(
-        (plan.planes, plan.rows, plan.panel_window * PAIR), BF16
+        (count,) + lead + (plan.panel_window * TILE,), BF16
     )
     return pl.pallas_call(
         body,
-        out_shape=[shape] * plan.cells,
-        in_specs=[SMEM] + [VMEM] * plan.planes,
-        out_specs=[VMEM] * plan.cells,
+        out_shape=[shape] * (plan.cells - 1),
+        in_specs=[SMEM] + [VMEM] * count,
+        out_specs=[VMEM] * (plan.cells - 1),
         compiler_params=params(),
         name="pack_panels",
     )(where, *received)
@@ -193,134 +194,152 @@
     )(taps.reshape(slots, 1, -1), weights)
 
 
-def range_step(plan, starts, matrices, source, target, blocks):
+def range_step(plan, starts, matrix, source, target, blocks):
     for j in range(plan.range_blocks):
         rows = pl.ds(aligned(starts(j), TILE), PAIR)
-        for block in range(blocks):
-            at = block * PAIR
-            res = jnp.dot(
-                matrices[0, j], source[rows, at : at + PAIR], preferred_element_type=F32
+        out = slice(j * TILE, (j + 1) * TILE)
+        for block in range(0, blocks, 2):
+            count = min(2, blocks - block)
+            of_real, of_imag = [
+                jnp.dot(
+                    matrix(j), source(part, rows, block, count), preferred_element_type=F32
+                )
+                for part in range(2)
+            ]
+            real = (of_real[:TILE] - of_imag[TILE:]).astype(BF16)
+            imag = (of_real[TILE:] + of_imag[:TILE]).astype(BF16)
+            for at in range(count):
+                lane = (block + at) * PAIR
+                piece = slice(at * TILE, (at + 1) * TILE)
+                target[out, lane : lane + TILE] = real[:, piece]
+                target[out, lane + TILE : lane + PAIR] = imag[:, piece]
+
+
+def merge(plan, where, groups, parts, held, rng_blocks, ang_blocks, rng_mats, ang_mats, last_mats):
+    half = plan.total_rows // 2
+    members = 2
+    cells, planes = plan.cells, plan.planes
+    width = plan.panel_window
+    mwidth = plan.merged_window
+    flips = cells - 1
+    n_parts = flips * len(groups)
+    n_in = n_parts + planes
+    flat = [part for per_flip in parts for part in per_flip] + list(held)
+
+    def body(where_ref, rb_ref, ab_ref, *refs):
+        ins = refs[:n_in]
+        rm_hbm, am_hbm, a2_hbm, own_ref, send_ref = refs[n_in : n_in + 5]
+        x_ref, z_ref, y_ref, s_ref, rm_ref, am_ref, a2_ref, sem, wsem = refs[n_in + 5 :]
+        panel = where_ref[0]
+        side = where_ref[1]
+        plane = panel // cells
+        cell = lax.rem(panel, cells)
+        loads = [[] for _ in range(members)]
+        own_at = plan.panel_start(panel)
+        for member in range(members):
+            for gi, group in enumerate(groups):
+                for at, step in enumerate(group):
+                    source = lax.rem(plane + planes - step, planes)
+                    for flip in range(cells):
+                        row = aligned(source * cells + (cell ^ flip), plan.rows)
+                        column = own_at - (plan.plane_start(plane) if step else 0)
+                        columns = pl.ds(aligned(column, TILE), width * TILE)
+                        loads[member].append(
+                            pltpu.make_async_copy(
+                                ins[gi * flips + flip - 1].at[at, member]
+                                if flip
+                                else ins[n_parts + step].at[member, :, :, columns],
+                                x_ref.at[member, :, pl.ds(row, plan.rows), :],
+                                sem.at[member, len(loads[member])],
+                            )
+                        )
+        weights = [
+            pltpu.make_async_copy(src, dst, wsem.at[i])
+            for i, (src, dst) in enumerate(
+                ((rm_hbm, rm_ref), (am_hbm, am_ref), (a2_hbm, a2_ref))
             )
-            real = res[:TILE, :TILE] - res[TILE:, TILE:]
-            imag = res[:TILE, TILE:] + res[TILE:, :TILE]
-            out = slice(j * TILE, (j + 1) * TILE)
-            target[out, at : at + TILE] = real.astype(BF16)
-            target[out, at + TILE : at + PAIR] = imag.astype(BF16)
-
-
-def gather_rows(plan, panel, parts, target):
-    cell = lax.rem(panel, plan.cells)
-    for flip in range(plan.cells):
-        source = cell ^ flip
-        for plane in range(plan.planes):
-            row = aligned(plane * plan.cells + source, plan.rows)
-            target[pl.ds(row, plan.rows), :] = parts[flip][plane]
-
-
-def first_member(plan, where, parts, rng_blocks, ang_blocks, rng_mats, ang_mats):
-    def body(where_ref, rb_ref, ab_ref, *refs):
-        ins = refs[: plan.cells]
-        rm_ref, am_ref, out_ref, x_ref, z_ref = refs[plan.cells :]
-        panel = where_ref[0]
-        gather_rows(plan, panel, ins, x_ref)
-        range_step(plan, lambda j: rb_ref[0, j], rm_ref, x_ref, z_ref, plan.panel_window)
+        ]
+        weights[0].start()
+        for member in range(members):
+            for load in loads[member]:
+                load.start()
+        weights[1].start()
+        weights[2].start()
+        weights[0].wait()
+        for member in range(members):
+            for load in loads[member]:
+                load.wait()
+            range_step(
+                plan,
+                lambda j: rb_ref[member, j],
+                lambda j: rm_ref[member, j],
+                lambda part, rows, block, count: x_ref[
+                    member, part, rows, block * TILE : (block + count) * TILE
+                ],
+                z_ref.at[member],
+                width,
+            )
         first = plan.merged_start(panel)
         base = plan.panel_start(panel)
-        for j in range(plan.merged_window):
-            start = ab_ref[0, first + j] - base
-            out_ref[:, j * PAIR : (j + 1) * PAIR] = jnp.dot(
-                z_ref[:, pl.ds(aligned(start, PAIR), 2 * PAIR)],
-                am_ref[j],
-                preferred_element_type=F32,
-            )
-
-    width = plan.panel_window * PAIR
-    mwidth = plan.merged_window * PAIR
-    return pl.pallas_call(
-        body,
-        out_shape=jax.ShapeDtypeStruct((plan.total_rows, mwidth), F32),
-        grid=(1,),
-        in_specs=[SMEM, SMEM, SMEM]
-        + [VMEM] * plan.cells
-        + [
-            pl.BlockSpec((1, plan.range_blocks, PAIR, PAIR), lambda i: (0, 0, 0, 0)),
-            pl.BlockSpec((plan.merged_window, 2 * PAIR, PAIR), lambda i: (0, 0, 0)),
-        ],
-        out_specs=VMEM,
-        scratch_shapes=[pltpu.VMEM((plan.total_rows, width), BF16)] * 2,
-        compiler_params=params(),
-        name="first_member",
-    )(where, rng_blocks, ang_blocks, *parts, rng_mats, ang_mats)
-
-
-def second_member(
-    plan, where, parts, partial, rng_blocks, ang_blocks, rng_mats, ang_mats, last_mats
-):
-    half = plan.total_rows // 2
-
-    def body(where_ref, rb_ref, ab_ref, *refs):
-        ins = refs[: plan.cells]
-        (m_ref, rm_ref, r2_ref, am_ref, a2_ref, own_ref, send_ref) = refs[
-            plan.cells : plan.cells + 7
-        ]
-        x_ref, z_ref, y_ref, s_ref = refs[plan.cells + 7 :]
-        panel = where_ref[0]
-        side = where_ref[1]
-        gather_rows(plan, panel, ins, x_ref)
-        range_step(plan, lambda j: rb_ref[1, j], rm_ref, x_ref, z_ref, plan.panel_window)
-        first = plan.merged_start(panel)
-        base = plan.panel_start(panel)
-        for j in range(plan.merged_window):
-            start = ab_ref[0, 2 * plan.in_blocks + first + j] - base
-            term = jnp.dot(
-                z_ref[:, pl.ds(aligned(start, PAIR), 2 * PAIR)],
-                am_ref[j],
-                preferred_element_type=F32,
-            )
-            at = slice(j * PAIR, (j + 1) * PAIR)
-            y_ref[:, at] = (m_ref[:, at] + term).astype(BF16)
-        range_step(plan, lambda j: rb_ref[2, j], r2_ref, y_ref, s_ref, plan.merged_window)
-        for j in range(plan.out_blocks):
-            place = 4 * plan.in_blocks + panel * plan.out_blocks + j
-            columns = pl.ds(aligned(ab_ref[0, place] - first, PAIR), 2 * PAIR)
-            for which, ref in ((1 - side, send_ref), (side, own_ref)):
+        weights[1].wait()
+        for j in range(mwidth):
+            terms = []
+            for member in range(members):
+                start = ab_ref[0, 2 * plan.in_blocks * member + first + j] - base
+                terms.append(
+                    jnp.dot(
+                        z_ref[member, :, pl.ds(aligned(start, PAIR), 2 * PAIR)],
+                        am_ref[member * mwidth + j],
+                        preferred_element_type=F32,
+                    )
+                )
+            total = (terms[0] + terms[1]).astype(BF16)
+            for part in range(2):
+                y_ref[part, :, j * TILE : (j + 1) * TILE] = total[
+                    :, part * TILE : (part + 1) * TILE
+                ]
+        range_step(
+            plan,
+            lambda j: rb_ref[2, j],
+            lambda j: rm_ref[2, j],
+            lambda part, rows, block, count: y_ref[
+                part, rows, block * TILE : (block + count) * TILE
+            ],
+            s_ref,
+            mwidth,
+        )
+        weights[2].wait()
+        for which, ref in ((1 - side, send_ref), (side, own_ref)):
+            for j in range(plan.out_blocks):
+                place = 4 * plan.in_blocks + panel * plan.out_blocks + j
+                columns = pl.ds(aligned(ab_ref[0, place] - first, PAIR), 2 * PAIR)
                 ref[:, j * PAIR : (j + 1) * PAIR] = jnp.dot(
                     s_ref[pl.ds(aligned(which, half), half), columns],
                     a2_ref[j],
                     preferred_element_type=F32,
                 ).astype(BF16)
 
-    width = plan.panel_window * PAIR
-    mwidth = plan.merged_window * PAIR
     shape = jax.ShapeDtypeStruct((half, plan.out_blocks * PAIR), BF16)
+    rows = plan.total_rows
     return pl.pallas_call(
         body,
         out_shape=[shape, shape],
-        grid=(1,),
-        in_specs=[SMEM, SMEM, SMEM]
-        + [VMEM] * (plan.cells + 1)
-        + [
-            pl.BlockSpec((1, plan.range_blocks, PAIR, PAIR), lambda i: (1, 0, 0, 0)),
-            pl.BlockSpec((1, plan.range_blocks, PAIR, PAIR), lambda i: (2, 0, 0, 0)),
-            pl.BlockSpec((plan.merged_window, 2 * PAIR, PAIR), lambda i: (1, 0, 0)),
-            VMEM,
+        in_specs=[SMEM, SMEM, SMEM] + [ANY] * (n_in + 3),
+        out_specs=[VMEM, VMEM],
+        scratch_shapes=[
+            pltpu.VMEM((members, 2, rows, width * TILE), BF16),
+            pltpu.VMEM((members, rows, width * PAIR), BF16),
+            pltpu.VMEM((2, rows, mwidth * TILE), BF16),
+            pltpu.VMEM((rows, mwidth * PAIR), BF16),
+            pltpu.VMEM(rng_mats.shape, BF16),
+            pltpu.VMEM(ang_mats.shape, BF16),
+            pltpu.VMEM(last_mats.shape, BF16),
+            pltpu.SemaphoreType.DMA((members, cells * planes)),
+            pltpu.SemaphoreType.DMA((3,)),
         ],
-        out_specs=[VMEM, VMEM],
-        scratch_shapes=[pltpu.VMEM((plan.total_rows, width), BF16)] * 2
-        + [pltpu.VMEM((plan.total_rows, mwidth), BF16)] * 2,
-        compiler_params=params(),
-        name="second_member",
-    )(
-        where,
-        rng_blocks,
-        ang_blocks,
-        *parts,
-        partial,
-        rng_mats,
-        rng_mats,
-        ang_mats,
-        last_mats,
-    )
+        compiler_params=params(),
+        name="merge",
+    )(where, rng_blocks, ang_blocks, *flat, rng_mats, ang_mats, last_mats)
 
 
 def focus(plan, where, own, other, owners, groups):
@@ -390,25 +409,34 @@
     def cell_flip(flip):
         return [(i, i ^ flip) for i in range(panels)]
 
-    sends = pack_planes(plan, where, subimages)
-    windows = []
-    after = None
-    for pieces in sends:
-        if after is not None:
-            pieces, _ = lax.optimization_barrier((pieces, after))
-        received = [pieces[0]] + [
-            lax.ppermute(pieces[step], "panel", plane_shift(step))
-            for step in range(1, plan.planes)
+    steps = [
+        sorted({step, plan.planes - step}) for step in range(1, plan.planes // 2 + 1)
+    ]
+    order = [[0]] + steps
+    far, near_parts = pack_own(plan, where, subimages)
+
+    def across(pieces):
+        return [
+            lax.ppermute(pieces[flip - 1], "panel", cell_flip(flip))
+            for flip in range(1, plan.cells)
         ]
-        after = received
-        parts = pack_panels(plan, where, received)
-        windows.append(
-            [parts[0]]
-            + [
-                lax.ppermute(parts[flip], "panel", cell_flip(flip))
-                for flip in range(1, plan.cells)
-            ]
-        )
+
+    parts = []
+    held = {0: subimages}
+    packed = near_parts
+    arrived = {
+        step: lax.ppermute(far[step - 1], "panel", plane_shift(step))
+        for group in steps
+        for step in group
+    }
+    for group in steps:
+        received = [arrived[step] for step in group]
+        parts.append(across(packed))
+        parts, received = lax.optimization_barrier((parts, received))
+        held.update(zip(group, received))
+        packed = pack_panels(plan, where, received)
+    parts.append(across(packed))
+    held = [held[step] for step in range(plan.planes)]
 
     first = plan.merged_start(panel)
     near = first + jnp.arange(plan.merged_window, dtype=jnp.int32)
@@ -422,11 +450,8 @@
     last_mats = build_angle(last_at, ang_taps, ang_weights[0])
     rng_mats = build_range(plan, rng_taps[0], rng_weights[0])
 
-    partial = first_member(
-        plan, where, windows[0], rng_blocks[0], ang_blocks, rng_mats, ang_mats
-    )
-    own, send = second_member(
-        plan, where, windows[1], partial, rng_blocks[0], ang_blocks, rng_mats, ang_mats, last_mats
+    own, send = merge(
+        plan, where, order, parts, held, rng_blocks[0], ang_blocks, rng_mats, ang_mats, last_mats
     )
     other = lax.ppermute(send, "aper", [(0, 1), (1, 0)])
     columns = plan.out_blocks * TILE

time: 93.4 us -> 89.5 us (0.958)
  starting transfers between devices: 22 us -> 16.7 us
  blocking collectives: 11.2 us -> 14.8 us
  waiting for transfers between devices: 31.8 us -> 30.1 us
  Pallas kernels: 21.8 us -> 20.3 us
  local copies, waits for them, and re-layouts: 4.6 us -> 5.85 us
    ppermute x12, starting transfers between devices: 22 us -> 16.6 us  [the longest x9 10.5 us: across(): lax.ppermute(pieces[flip - 1], 'panel', cell_flip(flip))]
    all_to_all x1, blocking collectives: 11.2 us -> 14.8 us  [shards(): lax.all_to_all(partials.reshape(2 * panels, GRP_DEV), ('aper', 'panel'),...]
    ppermute x12, waiting for transfers between devices: 29.9 us -> 27.9 us  [the longest x3 16 us: shards(): lax.ppermute(far[step - 1], 'panel', plane_shift(step))]
    pallas_call x5 -> x4, Pallas kernels: 14.3 us -> 12.8 us  [the longest x1 9.06 us: merge(): pl.pallas_call(body, out_shape=[shape, shape], in_specs=[SMEM, SMEM, SMEM...]
    unnamed x23 -> x31, local copies, waits for them, and re-layouts: 3.82 us -> 5.08 us
  transfers between devices with their start and end apart: 13 -> 13, of which waited for: 7 -> 7; matrix products, arithmetic and copies ran while one was open for 1% -> 1% of each run, Pallas kernels for 10% -> 7%
where the time goes in v2:
time: 89.5 us; the launch traced here: 89.3 us
  waiting for transfers between devices  30.1 us (34%)
  Pallas kernels  20.3 us (23%)
  starting transfers between devices  16.7 us (19%)
  blocking collectives  14.8 us (17%)
  local copies, waits for them, and re-layouts  5.85 us (7%)
    ppermute x3, waiting for transfers between devices, shards(): lax.ppermute(far[step - 1], 'panel', plane_shift(step))  16 us
    all_to_all x1, blocking collectives, shards(): lax.all_to_all(partials.reshape(2 * panels, GRP_DEV), ('aper', 'panel'),...  14.8 us
    ppermute x9, waiting for transfers between devices, across(): lax.ppermute(pieces[flip - 1], 'panel', cell_flip(flip))  11.9 us
    ppermute x9, starting transfers between devices, across(): lax.ppermute(pieces[flip - 1], 'panel', cell_flip(flip))  10.5 us
    pallas_call x1, Pallas kernels, merge(): pl.pallas_call(body, out_shape=[shape, shape], in_specs=[SMEM, SMEM, SMEM...  9.06 us
    ppermute x3, starting transfers between devices, shards(): lax.ppermute(far[step - 1], 'panel', plane_shift(step))  6.08 us
    unnamed x31, local copies, waits for them, and re-layouts  5.08 us
    pallas_call x1, Pallas kernels, focus(): pl.pallas_call(body, out_shape=[jax.ShapeDtypeStruct((2, half, columns),...  3.05 us
  transfers between devices with their start and end apart: 13, of which 7 were waited for; matrix products, arithmetic and copies ran while one was open for 1% of the time, Pallas kernels for 7%

profile of v2, /device:TPU:0, one launch (start us, length us, event | category | flops | bytes accessed | tf_op | source)
XLA Modules:
  0.0 89.3 jit_solution(741271921462692194)
XLA Ops:
  0.7 1.4 %copy-done.2 = bf16[2,2,32,4096]{3,2,1,0:T(8,128)(2,1)S(1)} copy-done((bf16[2,2,32,4096]{3,2,1,0:T(8,128)(2,1)S(1)}, bf16[2,2,32,4096]{3,2,1,0:T(8,128)(2,1)}, u32[]{:S(2)}) %copy-start.2) | copy-done | bytes 1048600
  2.1 1.4 %pack_own.1 = (bf16[2,2,32,1536]{3,2,1,0:T(8,128)(2,1)S(1)}, bf16[2,2,32,1536]{3,2,1,0:T(8,128)(2,1)}, bf16[2,2,32,1536]{3,2,1,0:T(8,128)(2,1)S(1)}, bf16[1,2,2,...) custom-call(s32[2]{0:T(128)S(1)} %pad_add_fusion.where_ref, ...), custom_call_target="tpu_custom_call" | custom-call | tf_op jit(solution)/shard_map/pack_own/pallas_call | solution.py:83
  3.5 3.0 %collective-permute-start.3 = (bf16[2,2,32,1536]{3,2,1,0:T(8,128)(2,1)S(1)}, bf16[2,2,32,1536]{3,2,1,0:T(8,128)(2,1)S(1)}, u32[]{:S(2)}, u32[]{:S(2)}) collective-permute-start(bf16[2,2,32,1536]{3,2,1,0:T(8,128)(2,1)S(1)} %get-tuple-element.33), channel_id=1, source_target_pairs={{0,8},{2,10},{4,12},{6,14},{8,16},{10,18},{12,20},{14,22},{16,24},... | collective-permute-start | bytes 1179656 | tf_op jit(solution)/shard_map/ppermute | solution.py:428
  6.5 2.0 %collective-permute-start.4 = (bf16[2,2,32,1536]{3,2,1,0:T(8,128)(2,1)S(1)}, bf16[2,2,32,1536]{3,2,1,0:T(8,128)(2,1)S(1)}, u32[]{:S(2)}, u32[]{:S(2)}) collective-permute-start(bf16[2,2,32,1536]{3,2,1,0:T(8,128)(2,1)S(1)} %get-tuple-element.34), channel_id=1, source_target_pairs={{0,24},{2,26},{4,28},{6,30},{8,0},{10,2},{12,4},{14,6},{16,8},{18,... | collective-permute-start | bytes 1179656 | tf_op jit(solution)/shard_map/ppermute | solution.py:428
  8.6 1.7 %collective-permute-start = (bf16[1,2,2,32,768]{4,3,2,1,0:T(8,128)(2,1)S(1)}, bf16[1,2,2,32,768]{4,3,2,1,0:T(8,128)(2,1)S(1)}, u32[]{:S(2)}, u32[]{:S(2)}) collective-permute-start(bf16[1,2,2,32,768]{4,3,2,1,0:T(8,128)(2,1)S(1)} %get-tuple-element.30), channel_id=1, source_target_pairs={{0,2},{2,0},{4,6},{6,4},{8,10},{10,8},{12,14},{14,12},{16,18},{18,... | collective-permute-start | bytes 589832 | tf_op jit(solution)/shard_map/ppermute | solution.py:420
  10.3 1.5 %collective-permute-start.1 = (bf16[1,2,2,32,768]{4,3,2,1,0:T(8,128)(2,1)S(1)}, bf16[1,2,2,32,768]{4,3,2,1,0:T(8,128)(2,1)S(1)}, u32[]{:S(2)}, u32[]{:S(2)}) collective-permute-start(bf16[1,2,2,32,768]{4,3,2,1,0:T(8,128)(2,1)S(1)} %get-tuple-element.31), channel_id=1, source_target_pairs={{0,4},{2,6},{4,0},{6,2},{8,12},{10,14},{12,8},{14,10},{16,20},{18,... | collective-permute-start | bytes 589832 | tf_op jit(solution)/shard_map/ppermute | solution.py:420
  12.0 4.3 %collective-permute-done.refs_0_ = bf16[1,2,2,32,768]{4,3,2,1,0:T(8,128)(2,1)S(1)} collective-permute-done((bf16[1,2,2,32,768]{4,3,2,1,0:T(8,128)(2,1)S(1)}, bf16[1,2,2,32,768]{4,3,2,1,0:T(8,128)(2,1)S(1)}, u32[]{:S(2)}, u32[]{:S(2)}) %collective-permute-start) | collective-permute-done | bytes 196640 | tf_op jit(solution)/shard_map/ppermute | solution.py:420
  16.4 0.7 copy-done.5
  17.1 1.0 %collective-permute-start.8 = (bf16[2,2,32,1536]{3,2,1,0:T(8,128)(2,1)}, bf16[2,2,32,1536]{3,2,1,0:T(8,128)(2,1)S(1)}, u32[]{:S(2)}, u32[]{:S(2)}) collective-permute-start(bf16[2,2,32,1536]{3,2,1,0:T(8,128)(2,1)} %get-tuple-element.43), channel_id=1, source_target_pairs={{0,16},{2,18},{4,20},{6,22},{8,24},{10,26},{12,28},{14,30},{16,0},... | collective-permute-start | bytes 1179656 | tf_op jit(solution)/shard_map/ppermute | solution.py:428
  18.1 2.3 %collective-permute-done.1.refs_1_ = bf16[1,2,2,32,768]{4,3,2,1,0:T(8,128)(2,1)S(1)} collective-permute-done((bf16[1,2,2,32,768]{4,3,2,1,0:T(8,128)(2,1)S(1)}, bf16[1,2,2,32,768]{4,3,2,1,0:T(8,128)(2,1)S(1)}, u32[]{:S(2)}, u32[]{:S(2)}) %collective-permute-start.1) | collective-permute-done | bytes 196640 | tf_op jit(solution)/shard_map/ppermute | solution.py:420
  20.3 0.7 copy-done.7
  21.0 0.7 copy-done.9
  21.7 3.8 %collective-permute-done.4.refs_1_.refs_12_ = bf16[2,2,32,1536]{3,2,1,0:T(8,128)(2,1)S(1)} collective-permute-done((bf16[2,2,32,1536]{3,2,1,0:T(8,128)(2,1)S(1)}, bf16[2,2,32,1536]{3,2,1,0:T(8,128)(2,1)S(1)}, u32[]{:S(2)}, u32[]{:S(2)}) %collective-permute-start.4) | collective-permute-done | bytes 393248 | tf_op jit(solution)/shard_map/ppermute | solution.py:428
  25.5 1.7 %pack_panels.2 = (bf16[2,2,2,32,768]{4,3,2,1,0:T(8,128)(2,1)}, bf16[2,2,2,32,768]{4,3,2,1,0:T(8,128)(2,1)}, bf16[2,2,2,32,768]{4,3,2,1,0:T(8,128)(2,1)}) custom-call(s32[2]{0:T(128)S(1)} %pad_add_fusion.where_ref, bf16[2,2,32,1536]{3,2,1,0:T(8,128)(2,1)S(1)} %collective-permute-done.3.refs_0_.refs_10_, ...), custom_call_target="tpu_custom_call" | custom-call | tf_op jit(solution)/shard_map/pack_panels/pallas_call | solution.py:113
  27.2 1.5 %collective-permute-start.5 = (bf16[2,2,2,32,768]{4,3,2,1,0:T(8,128)(2,1)}, bf16[2,2,2,32,768]{4,3,2,1,0:T(8,128)(2,1)}, u32[]{:S(2)}, u32[]{:S(2)}) collective-permute-start(bf16[2,2,2,32,768]{4,3,2,1,0:T(8,128)(2,1)} %get-tuple-element.40), channel_id=1, source_target_pairs={{0,2},{2,0},{4,6},{6,4},{8,10},{10,8},{12,14},{14,12},{16,18},{18,... | collective-permute-start | bytes 1179656 | tf_op jit(solution)/shard_map/ppermute | solution.py:420
  28.7 1.5 %collective-permute-start.6 = (bf16[2,2,2,32,768]{4,3,2,1,0:T(8,128)(2,1)}, bf16[2,2,2,32,768]{4,3,2,1,0:T(8,128)(2,1)}, u32[]{:S(2)}, u32[]{:S(2)}) collective-permute-start(bf16[2,2,2,32,768]{4,3,2,1,0:T(8,128)(2,1)} %get-tuple-element.41), channel_id=1, source_target_pairs={{0,4},{2,6},{4,0},{6,2},{8,12},{10,14},{12,8},{14,10},{16,20},{18,... | collective-permute-start | bytes 1179656 | tf_op jit(solution)/shard_map/ppermute | solution.py:420
  30.7 12.2 %collective-permute-done.8.refs_0_.refs_11_ = bf16[2,2,32,1536]{3,2,1,0:T(8,128)(2,1)S(1)} collective-permute-done((bf16[2,2,32,1536]{3,2,1,0:T(8,128)(2,1)}, bf16[2,2,32,1536]{3,2,1,0:T(8,128)(2,1)S(1)}, u32[]{:S(2)}, u32[]{:S(2)}) %collective-permute-start.8) | collective-permute-done | bytes 393248 | tf_op jit(solution)/shard_map/ppermute | solution.py:428
  42.9 4.6 %collective-permute-done.6.refs_4_ = bf16[2,2,2,32,768]{4,3,2,1,0:T(8,128)(2,1)} collective-permute-done((bf16[2,2,2,32,768]{4,3,2,1,0:T(8,128)(2,1)}, bf16[2,2,2,32,768]{4,3,2,1,0:T(8,128)(2,1)}, u32[]{:S(2)}, u32[]{:S(2)}) %collective-permute-start.6) | collective-permute-done | bytes 393248 | tf_op jit(solution)/shard_map/ppermute | solution.py:420
  47.6 0.6 pack_panels.3
  48.2 1.6 %collective-permute-start.10 = (bf16[1,2,2,32,768]{4,3,2,1,0:T(8,128)(2,1)S(1)}, bf16[1,2,2,32,768]{4,3,2,1,0:T(8,128)(2,1)S(1)}, u32[]{:S(2)}, u32[]{:S(2)}) collective-permute-start(bf16[1,2,2,32,768]{4,3,2,1,0:T(8,128)(2,1)S(1)} %get-tuple-element.52), channel_id=1, source_target_pairs={{0,4},{2,6},{4,0},{6,2},{8,12},{10,14},{12,8},{14,10},{16,20},{18,... | collective-permute-start | bytes 589832 | tf_op jit(solution)/shard_map/ppermute | solution.py:420
  49.8 1.2 %collective-permute-start.11 = (bf16[1,2,2,32,768]{4,3,2,1,0:T(8,128)(2,1)S(1)}, bf16[1,2,2,32,768]{4,3,2,1,0:T(8,128)(2,1)S(1)}, u32[]{:S(2)}, u32[]{:S(2)}) collective-permute-start(bf16[1,2,2,32,768]{4,3,2,1,0:T(8,128)(2,1)S(1)} %get-tuple-element.53), channel_id=1, source_target_pairs={{0,6},{2,4},{4,2},{6,0},{8,14},{10,12},{12,10},{14,8},{16,22},{18,... | collective-permute-start | bytes 589832 | tf_op jit(solution)/shard_map/ppermute | solution.py:420
  50.9 0.8 collective-permute-start.9
  51.8 1.5 %build_angle.2.refs_14_ = bf16[12,512,256]{2,1,0:T(8,128)(2,1)S(1)} custom-call(s32[12]{0:T(128)S(1)} %pad_add_fusion.1.blocks_ref, s32[1,32768]{1,0:T(1,128)S(1)} %copy-done.4, bf16[2,16,32768]{2,1,0:T(8,128)(2,1)S(1)} %bitcast.11), custom_call_target="tpu_custom_call" | custom-call | tf_op jit(solution)/shard_map/build_angle/pallas_call | solution.py:156
  53.4 1.6 %copy-done = bf16[12,512,256]{2,1,0:T(8,128)(2,1)} copy-done((bf16[12,512,256]{2,1,0:T(8,128)(2,1)}, bf16[12,512,256]{2,1,0:T(8,128)(2,1)S(1)}, u32[]{:S(2)}) %copy-start) | copy-done | bytes 3145752
  55.1 1.2 %build_angle.3.refs_15_ = bf16[8,512,256]{2,1,0:T(8,128)(2,1)S(1)} custom-call(s32[8]{0:T(128)S(1)} %iota_add_fusion.blocks_ref, s32[1,32768]{1,0:T(1,128)S(1)} %copy-done.4, bf16[2,16,32768]{2,1,0:T(8,128)(2,1)S(1)} %bitcast.12), custom_call_target="tpu_custom_call" | custom-call | tf_op jit(solution)/shard_map/build_angle/pallas_call | solution.py:156
  56.3 1.7 %build_range.1.refs_13_ = bf16[3,4,256,256]{3,2,1,0:T(8,128)(2,1)S(1)} custom-call(s32[3,1,512]{2,1,0:T(1,128)S(1)} %bitcast.16, bf16[3,2,16,512]{3,2,1,0:T(8,128)(2,1)S(1)} %bitcast.13), custom_call_target="tpu_custom_call" | custom-call | tf_op jit(solution)/shard_map/build_range/pallas_call | solution.py:183
  58.1 0.7 collective-permute-done.9.refs_6_
  58.7 9.1 %merge.1 = (bf16[256,2048]{1,0:T(8,128)(2,1)S(1)}, bf16[256,2048]{1,0:T(8,128)(2,1)}) custom-call(s32[2]{0:T(128)S(1)} %pad_add_fusion.where_ref, s32[3,4]{1,0:T(4,128)S(1)} %bitcast.15, s32[1,256]{1,0:T(1,128)S(1)} %copy-done.13, bf16[1,2,2,32,768]{4,3,2,1,0:T(8,128)(2,1)S(1)} %copy-done.6, bf16[1,2,2,32,768]{4,3,2,1,0:T(8,128)(2,1)S(1)} %copy-done.8, ...), custom_call_target="tpu_custom_call" | custom-call | tf_op jit(solution)/shard_map/merge/pallas_call | solution.py:324
  67.9 0.7 dynamic-slice.3
  68.6 2.2 %collective-permute-done.12.oth_ref = bf16[256,2048]{1,0:T(8,128)(2,1)S(1)} collective-permute-done((bf16[256,2048]{1,0:T(8,128)(2,1)}, bf16[256,2048]{1,0:T(8,128)(2,1)S(1)}, u32[]{:S(2)}, u32[]{:S(2)}) %collective-permute-start.12) | collective-permute-done | bytes 1048608 | tf_op jit(solution)/shard_map/ppermute | solution.py:456
  70.8 3.1 %focus.1 = (bf16[2,256,1024]{2,1,0:T(8,128)(2,1)}, f32[2,64,1]{2,1,0:T(8,128)S(1)}) custom-call(s32[2]{0:T(128)S(1)} %pad_add_fusion.where_ref, bf16[256,2048]{1,0:T(8,128)(2,1)S(1)} %get-tuple-element.54.own_ref, bf16[256,2048]{1,0:T(8,128)(2,1)S(1)} %collective-permute-done.12.oth_ref, s32[1,1024]{1,0:T(1,128)S(1)} %bitcast.14), custom_call_target="tpu_custom_call" | custom-call | tf_op jit(solution)/shard_map/focus/pallas_call | solution.py:381
  74.0 14.8 %all_to_all.9 = f32[32,1,4]{2,1,0:T(1,128)S(1)} all-to-all(f32[32,1,4]{2,1,0:T(1,128)S(1)} %bitcast.17), channel_id=1, replica_groups=mesh['scene'=1,'panel'=16,'aper'=2] {'aper','panel'}, dimensions={0} | all-to-all | bytes 1024 | tf_op jit(solution)/shard_map/all_to_all | solution.py:460
  (42 shorter events, 1.8 us)
Async XLA Ops:
  0.6 51.2 %copy-start.1 = (bf16[1,2,16,32768]{3,2,1,0:T(8,128)(2,1)S(1)}, bf16[1,2,16,32768]{3,2,1,0:T(8,128)(2,1)}, u32[]{:S(2)}) copy-start(bf16[1,2,16,32768]{3,2,1,0:T(8,128)(2,1)} %param.14) | copy-start | bytes 6291460
  0.7 1.4 %copy-start.2 = (bf16[2,2,32,4096]{3,2,1,0:T(8,128)(2,1)S(1)}, bf16[2,2,32,4096]{3,2,1,0:T(8,128)(2,1)}, u32[]{:S(2)}) copy-start(bf16[2,2,32,4096]{3,2,1,0:T(8,128)(2,1)} %refs_9_.1) | copy-start | bytes 3145732
  2.1 49.7 %copy-start.4 = (s32[1,32768]{1,0:T(1,128)S(1)}, s32[1,32768]{1,0:T(1,128)}, u32[]{:S(2)}) copy-start(s32[1,32768]{1,0:T(1,128)} %taps_ref.3) | copy-start | bytes 393220
  3.5 18.2 %collective-permute-start.3 = (bf16[2,2,32,1536]{3,2,1,0:T(8,128)(2,1)S(1)}, bf16[2,2,32,1536]{3,2,1,0:T(8,128)(2,1)S(1)}, u32[]{:S(2)}, u32[]{:S(2)}) collective-permute-start(bf16[2,2,32,1536]{3,2,1,0:T(8,128)(2,1)S(1)} %get-tuple-element.33), channel_id=1, source_target_pairs={{0,8},{2,10},{4,12},{6,14},{8,16},{10,18},{12,20},{14,22},{16,24},... | collective-permute-start | bytes 1179656 | tf_op jit(solution)/shard_map/ppermute | solution.py:428
  6.5 19.0 %collective-permute-start.4 = (bf16[2,2,32,1536]{3,2,1,0:T(8,128)(2,1)S(1)}, bf16[2,2,32,1536]{3,2,1,0:T(8,128)(2,1)S(1)}, u32[]{:S(2)}, u32[]{:S(2)}) collective-permute-start(bf16[2,2,32,1536]{3,2,1,0:T(8,128)(2,1)S(1)} %get-tuple-element.34), channel_id=1, source_target_pairs={{0,24},{2,26},{4,28},{6,30},{8,0},{10,2},{12,4},{14,6},{16,8},{18,... | collective-permute-start | bytes 1179656 | tf_op jit(solution)/shard_map/ppermute | solution.py:428
  8.6 7.8 %collective-permute-start = (bf16[1,2,2,32,768]{4,3,2,1,0:T(8,128)(2,1)S(1)}, bf16[1,2,2,32,768]{4,3,2,1,0:T(8,128)(2,1)S(1)}, u32[]{:S(2)}, u32[]{:S(2)}) collective-permute-start(bf16[1,2,2,32,768]{4,3,2,1,0:T(8,128)(2,1)S(1)} %get-tuple-element.30), channel_id=1, source_target_pairs={{0,2},{2,0},{4,6},{6,4},{8,10},{10,8},{12,14},{14,12},{16,18},{18,... | collective-permute-start | bytes 589832 | tf_op jit(solution)/shard_map/ppermute | solution.py:420
  10.3 10.1 %collective-permute-start.1 = (bf16[1,2,2,32,768]{4,3,2,1,0:T(8,128)(2,1)S(1)}, bf16[1,2,2,32,768]{4,3,2,1,0:T(8,128)(2,1)S(1)}, u32[]{:S(2)}, u32[]{:S(2)}) collective-permute-start(bf16[1,2,2,32,768]{4,3,2,1,0:T(8,128)(2,1)S(1)} %get-tuple-element.31), channel_id=1, source_target_pairs={{0,4},{2,6},{4,0},{6,2},{8,12},{10,14},{12,8},{14,10},{16,20},{18,... | collective-permute-start | bytes 589832 | tf_op jit(solution)/shard_map/ppermute | solution.py:420
  11.8 9.3 %collective-permute-start.2 = (bf16[1,2,2,32,768]{4,3,2,1,0:T(8,128)(2,1)S(1)}, bf16[1,2,2,32,768]{4,3,2,1,0:T(8,128)(2,1)S(1)}, u32[]{:S(2)}, u32[]{:S(2)}) collective-permute-start(bf16[1,2,2,32,768]{4,3,2,1,0:T(8,128)(2,1)S(1)} %get-tuple-element.32), channel_id=1, source_target_pairs={{0,6},{2,4},{4,2},{6,0},{8,14},{10,12},{12,10},{14,8},{16,22},{18,... | collective-permute-start | bytes 589832 | tf_op jit(solution)/shard_map/ppermute | solution.py:420
  16.4 0.7 copy-start.5
  17.1 25.9 %collective-permute-start.8 = (bf16[2,2,32,1536]{3,2,1,0:T(8,128)(2,1)}, bf16[2,2,32,1536]{3,2,1,0:T(8,128)(2,1)S(1)}, u32[]{:S(2)}, u32[]{:S(2)}) collective-permute-start(bf16[2,2,32,1536]{3,2,1,0:T(8,128)(2,1)} %get-tuple-element.43), channel_id=1, source_target_pairs={{0,16},{2,18},{4,20},{6,22},{8,24},{10,26},{12,28},{14,30},{16,0},... | collective-permute-start | bytes 1179656 | tf_op jit(solution)/shard_map/ppermute | solution.py:428
  20.3 0.7 copy-start.7
  21.0 0.7 copy-start.9
  27.2 15.7 %collective-permute-start.5 = (bf16[2,2,2,32,768]{4,3,2,1,0:T(8,128)(2,1)}, bf16[2,2,2,32,768]{4,3,2,1,0:T(8,128)(2,1)}, u32[]{:S(2)}, u32[]{:S(2)}) collective-permute-start(bf16[2,2,2,32,768]{4,3,2,1,0:T(8,128)(2,1)} %get-tuple-element.40), channel_id=1, source_target_pairs={{0,2},{2,0},{4,6},{6,4},{8,10},{10,8},{12,14},{14,12},{16,18},{18,... | collective-permute-start | bytes 1179656 | tf_op jit(solution)/shard_map/ppermute | solution.py:420
  28.7 18.9 %collective-permute-start.6 = (bf16[2,2,2,32,768]{4,3,2,1,0:T(8,128)(2,1)}, bf16[2,2,2,32,768]{4,3,2,1,0:T(8,128)(2,1)}, u32[]{:S(2)}, u32[]{:S(2)}) collective-permute-start(bf16[2,2,2,32,768]{4,3,2,1,0:T(8,128)(2,1)} %get-tuple-element.41), channel_id=1, source_target_pairs={{0,4},{2,6},{4,0},{6,2},{8,12},{10,14},{12,8},{14,10},{16,20},{18,... | collective-permute-start | bytes 1179656 | tf_op jit(solution)/shard_map/ppermute | solution.py:420
  30.2 17.4 %collective-permute-start.7 = (bf16[2,2,2,32,768]{4,3,2,1,0:T(8,128)(2,1)}, bf16[2,2,2,32,768]{4,3,2,1,0:T(8,128)(2,1)}, u32[]{:S(2)}, u32[]{:S(2)}) collective-permute-start(bf16[2,2,2,32,768]{4,3,2,1,0:T(8,128)(2,1)} %get-tuple-element.42), channel_id=1, source_target_pairs={{0,6},{2,4},{4,2},{6,0},{8,14},{10,12},{12,10},{14,8},{16,22},{18,... | collective-permute-start | bytes 1179656 | tf_op jit(solution)/shard_map/ppermute | solution.py:420
  48.2 9.9 %collective-permute-start.10 = (bf16[1,2,2,32,768]{4,3,2,1,0:T(8,128)(2,1)S(1)}, bf16[1,2,2,32,768]{4,3,2,1,0:T(8,128)(2,1)S(1)}, u32[]{:S(2)}, u32[]{:S(2)}) collective-permute-start(bf16[1,2,2,32,768]{4,3,2,1,0:T(8,128)(2,1)S(1)} %get-tuple-element.52), channel_id=1, source_target_pairs={{0,4},{2,6},{4,0},{6,2},{8,12},{10,14},{12,8},{14,10},{16,20},{18,... | collective-permute-start | bytes 589832 | tf_op jit(solution)/shard_map/ppermute | solution.py:420
  49.8 8.3 %collective-permute-start.11 = (bf16[1,2,2,32,768]{4,3,2,1,0:T(8,128)(2,1)S(1)}, bf16[1,2,2,32,768]{4,3,2,1,0:T(8,128)(2,1)S(1)}, u32[]{:S(2)}, u32[]{:S(2)}) collective-permute-start(bf16[1,2,2,32,768]{4,3,2,1,0:T(8,128)(2,1)S(1)} %get-tuple-element.53), channel_id=1, source_target_pairs={{0,6},{2,4},{4,2},{6,0},{8,14},{10,12},{12,10},{14,8},{16,22},{18,... | collective-permute-start | bytes 589832 | tf_op jit(solution)/shard_map/ppermute | solution.py:420
  50.9 7.8 %collective-permute-start.9 = (bf16[1,2,2,32,768]{4,3,2,1,0:T(8,128)(2,1)S(1)}, bf16[1,2,2,32,768]{4,3,2,1,0:T(8,128)(2,1)S(1)}, u32[]{:S(2)}, u32[]{:S(2)}) collective-permute-start(bf16[1,2,2,32,768]{4,3,2,1,0:T(8,128)(2,1)S(1)} %get-tuple-element.51), channel_id=1, source_target_pairs={{0,2},{2,0},{4,6},{6,4},{8,10},{10,8},{12,14},{14,12},{16,18},{18,... | collective-permute-start | bytes 589832 | tf_op jit(solution)/shard_map/ppermute | solution.py:420
  53.3 1.6 %copy-start = (bf16[12,512,256]{2,1,0:T(8,128)(2,1)}, bf16[12,512,256]{2,1,0:T(8,128)(2,1)S(1)}, u32[]{:S(2)}) copy-start(bf16[12,512,256]{2,1,0:T(8,128)(2,1)S(1)} %build_angle.2.refs_14_) | copy-start | bytes 9437188
  55.0 1.3 %copy-start.14 = (s32[1,3,4]{2,0,1:T(1,128)S(1)}, s32[1,3,4]{2,0,1:T(1,128)}, u32[]{:S(2)}) copy-start(s32[1,3,4]{2,0,1:T(1,128)} %param.10) | copy-start | bytes 148
  55.0 1.3 %copy-start.11 = (bf16[1,3,2,16,512]{4,3,2,1,0:T(8,128)(2,1)S(1)}, bf16[1,3,2,16,512]{4,3,2,1,0:T(8,128)(2,1)}, u32[]{:S(2)}) copy-start(bf16[1,3,2,16,512]{4,3,2,1,0:T(8,128)(2,1)} %param.11) | copy-start | bytes 294916
  55.0 1.3 %copy-start.12 = (s32[1,3,512]{2,0,1:T(1,128)S(1)}, s32[1,3,512]{2,0,1:T(1,128)}, u32[]{:S(2)}) copy-start(s32[1,3,512]{2,0,1:T(1,128)} %param.9) | copy-start | bytes 18436
  55.0 3.7 %copy-start.3 = (bf16[2,2,32,4096]{3,2,1,0:T(8,128)(2,1)S(1)}, bf16[2,2,32,4096]{3,2,1,0:T(8,128)(2,1)}, u32[]{:S(2)}) copy-start(bf16[2,2,32,4096]{3,2,1,0:T(8,128)(2,1)} %refs_9_.1) | copy-start | bytes 3145732
  55.0 3.7 %copy-start.6 = (bf16[1,2,2,32,768]{4,3,2,1,0:T(8,128)(2,1)S(1)}, bf16[1,2,2,32,768]{4,3,2,1,0:T(8,128)(2,1)}, u32[]{:S(2)}) copy-start(bf16[1,2,2,32,768]{4,3,2,1,0:T(8,128)(2,1)} %copy-done.5) | copy-start | bytes 589828
  55.0 3.7 %copy-start.8 = (bf16[1,2,2,32,768]{4,3,2,1,0:T(8,128)(2,1)S(1)}, bf16[1,2,2,32,768]{4,3,2,1,0:T(8,128)(2,1)}, u32[]{:S(2)}) copy-start(bf16[1,2,2,32,768]{4,3,2,1,0:T(8,128)(2,1)} %copy-done.7) | copy-start | bytes 589828
  55.0 3.7 %copy-start.10 = (bf16[1,2,2,32,768]{4,3,2,1,0:T(8,128)(2,1)S(1)}, bf16[1,2,2,32,768]{4,3,2,1,0:T(8,128)(2,1)}, u32[]{:S(2)}) copy-start(bf16[1,2,2,32,768]{4,3,2,1,0:T(8,128)(2,1)} %copy-done.9) | copy-start | bytes 589828
  55.0 3.7 %copy-start.13 = (s32[1,256]{1,0:T(1,128)S(1)}, s32[1,256]{1,0:T(1,128)}, u32[]{:S(2)}) copy-start(s32[1,256]{1,0:T(1,128)} %ab_ref.1) | copy-start | bytes 3076
  67.8 2.9 %collective-permute-start.12 = (bf16[256,2048]{1,0:T(8,128)(2,1)}, bf16[256,2048]{1,0:T(8,128)(2,1)S(1)}, u32[]{:S(2)}, u32[]{:S(2)}) collective-permute-start(bf16[256,2048]{1,0:T(8,128)(2,1)} %get-tuple-element.55), channel_id=1, source_target_pairs={{0,1},{1,0},{2,3},{3,2},{4,5},{5,4},{6,7},{7,6},{8,9},{9,8},{10,11... | collective-permute-start | bytes 3145736 | tf_op jit(solution)/shard_map/ppermute | solution.py:456

commit v3 on v2

--- a/solution.py
+++ b/solution.py
@@ -9,6 +9,7 @@
 PAIR = 2 * TILE
 TAPS = 16
 GRP_DEV = 4
+STRIP = 32
 F32 = jnp.float32
 BF16 = jnp.bfloat16
 VMEM_BYTES = 44 * 1024 * 1024
@@ -53,7 +54,7 @@
 
 SMEM = pl.BlockSpec(memory_space=pltpu.SMEM)
 VMEM = pl.BlockSpec(memory_space=pltpu.VMEM)
-ANY = pl.BlockSpec(memory_space=pltpu.HBM)
+ANY = pl.BlockSpec(memory_space=pl.ANY)
 
 
 def pack_own(plan, where, subimages):
@@ -234,41 +235,42 @@
         side = where_ref[1]
         plane = panel // cells
         cell = lax.rem(panel, cells)
-        loads = [[] for _ in range(members)]
         own_at = plan.panel_start(panel)
+        loads = []
+        for step in range(planes):
+            row = aligned(lax.rem(plane + planes - step, planes) * cells + cell, plan.rows)
+            column = own_at - (plan.plane_start(plane) if step else 0)
+            loads.append(
+                pltpu.make_async_copy(
+                    ins[n_parts + step].at[
+                        :, :, :, pl.ds(aligned(column, TILE), width * TILE)
+                    ],
+                    x_ref.at[:, :, pl.ds(row, plan.rows), :],
+                    sem.at[step],
+                )
+            )
+        weights = [
+            pltpu.make_async_copy(rm_hbm.at[slot], rm_ref.at[slot], wsem.at[slot])
+            for slot in range(3)
+        ] + [
+            pltpu.make_async_copy(am_hbm, am_ref, wsem.at[3]),
+            pltpu.make_async_copy(a2_hbm, a2_ref, wsem.at[4]),
+        ]
+        weights[0].start()
+        for load in loads:
+            load.start()
+        for at in (1, 3, 2, 4):
+            weights[at].start()
+        for load in loads:
+            load.wait()
         for member in range(members):
             for gi, group in enumerate(groups):
                 for at, step in enumerate(group):
-                    source = lax.rem(plane + planes - step, planes)
-                    for flip in range(cells):
-                        row = aligned(source * cells + (cell ^ flip), plan.rows)
-                        column = own_at - (plan.plane_start(plane) if step else 0)
-                        columns = pl.ds(aligned(column, TILE), width * TILE)
-                        loads[member].append(
-                            pltpu.make_async_copy(
-                                ins[gi * flips + flip - 1].at[at, member]
-                                if flip
-                                else ins[n_parts + step].at[member, :, :, columns],
-                                x_ref.at[member, :, pl.ds(row, plan.rows), :],
-                                sem.at[member, len(loads[member])],
-                            )
-                        )
-        weights = [
-            pltpu.make_async_copy(src, dst, wsem.at[i])
-            for i, (src, dst) in enumerate(
-                ((rm_hbm, rm_ref), (am_hbm, am_ref), (a2_hbm, a2_ref))
-            )
-        ]
-        weights[0].start()
-        for member in range(members):
-            for load in loads[member]:
-                load.start()
-        weights[1].start()
-        weights[2].start()
-        weights[0].wait()
-        for member in range(members):
-            for load in loads[member]:
-                load.wait()
+                    source = lax.rem(plane + planes - step, planes) * cells
+                    for flip in range(1, cells):
+                        rows = pl.ds(aligned(source + (cell ^ flip), plan.rows), plan.rows)
+                        x_ref[member, :, rows, :] = ins[gi * flips + flip - 1][at, member]
+            weights[member].wait()
             range_step(
                 plan,
                 lambda j: rb_ref[member, j],
@@ -281,7 +283,7 @@
             )
         first = plan.merged_start(panel)
         base = plan.panel_start(panel)
-        weights[1].wait()
+        weights[3].wait()
         for j in range(mwidth):
             terms = []
             for member in range(members):
@@ -298,6 +300,7 @@
                 y_ref[part, :, j * TILE : (j + 1) * TILE] = total[
                     :, part * TILE : (part + 1) * TILE
                 ]
+        weights[2].wait()
         range_step(
             plan,
             lambda j: rb_ref[2, j],
@@ -308,7 +311,7 @@
             s_ref,
             mwidth,
         )
-        weights[2].wait()
+        weights[4].wait()
         for which, ref in ((1 - side, send_ref), (side, own_ref)):
             for j in range(plan.out_blocks):
                 place = 4 * plan.in_blocks + panel * plan.out_blocks + j
@@ -324,7 +327,7 @@
     return pl.pallas_call(
         body,
         out_shape=[shape, shape],
-        in_specs=[SMEM, SMEM, SMEM] + [ANY] * (n_in + 3),
+        in_specs=[SMEM, SMEM, SMEM] + [VMEM] * n_parts + [ANY] * (planes + 3),
         out_specs=[VMEM, VMEM],
         scratch_shapes=[
             pltpu.VMEM((members, 2, rows, width * TILE), BF16),
@@ -334,8 +337,8 @@
             pltpu.VMEM(rng_mats.shape, BF16),
             pltpu.VMEM(ang_mats.shape, BF16),
             pltpu.VMEM(last_mats.shape, BF16),
-            pltpu.SemaphoreType.DMA((members, cells * planes)),
-            pltpu.SemaphoreType.DMA((3,)),
+            pltpu.SemaphoreType.DMA((planes,)),
+            pltpu.SemaphoreType.DMA((5,)),
         ],
         compiler_params=params(),
         name="merge",
@@ -346,28 +349,43 @@
     half = plan.total_rows // 2
     columns = plan.out_blocks * TILE
 
-    def body(where_ref, own_ref, oth_ref, owners_ref, image_ref, grad_ref):
+    def body(
+        where_ref, own_ref, oth_ref, owners_ref, image_ref, grad_ref, held_ref, sem
+    ):
         side = where_ref[1]
-        row = lax.broadcasted_iota(jnp.int32, (half, TILE), 0) + side * half
-        weight = 1.0 + 2.0 * row.astype(F32) / (plan.total_rows - 1)
+        row = lax.broadcasted_iota(jnp.int32, (STRIP, TILE), 0) + side * half
         mine, theirs = [], []
+        stores = []
         for j in range(plan.out_blocks):
             at = j * PAIR
-            own_re = own_ref[:, at : at + TILE].astype(F32)
-            own_im = own_ref[:, at + TILE : at + PAIR].astype(F32)
-            oth_re = oth_ref[:, at : at + TILE].astype(F32)
-            oth_im = oth_ref[:, at + TILE : at + PAIR].astype(F32)
-            re = own_re + oth_re
-            im = own_im + oth_im
-            image_ref[0, :, j * TILE : (j + 1) * TILE] = re.astype(BF16)
-            image_ref[1, :, j * TILE : (j + 1) * TILE] = im.astype(BF16)
-            power = weight * (re * re + im * im)
-            mine.append(
-                jnp.sum(power * (re * own_re + im * own_im), axis=0, keepdims=True)
+            sums = [jnp.zeros((8, TILE), F32)] * 2
+            for top in range(0, half, STRIP):
+                strip = slice(top, top + STRIP)
+                weight = 1.0 + 2.0 * (row + top).astype(F32) / (plan.total_rows - 1)
+                own_re = own_ref[strip, at : at + TILE].astype(F32)
+                own_im = own_ref[strip, at + TILE : at + PAIR].astype(F32)
+                oth_re = oth_ref[strip, at : at + TILE].astype(F32)
+                oth_im = oth_ref[strip, at + TILE : at + PAIR].astype(F32)
+                re = own_re + oth_re
+                im = own_im + oth_im
+                held_ref[0, strip, j * TILE : (j + 1) * TILE] = re.astype(BF16)
+                held_ref[1, strip, j * TILE : (j + 1) * TILE] = im.astype(BF16)
+                power = weight * (re * re + im * im)
+                for which, (a, b) in enumerate(((own_re, own_im), (oth_re, oth_im))):
+                    term = power * (re * a + im * b)
+                    sums[which] = sums[which] + jnp.sum(
+                        term.reshape(STRIP // 8, 8, TILE), axis=0
+                    )
+            stores.append(
+                pltpu.make_async_copy(
+                    held_ref.at[:, :, j * TILE : (j + 1) * TILE],
+                    image_ref.at[:, :, j * TILE : (j + 1) * TILE],
+                    sem.at[j],
+                )
             )
-            theirs.append(
-                jnp.sum(power * (re * oth_re + im * oth_im), axis=0, keepdims=True)
-            )
+            stores[-1].start()
+            mine.append(jnp.sum(sums[0], axis=0, keepdims=True))
+            theirs.append(jnp.sum(sums[1], axis=0, keepdims=True))
         mine = jnp.concatenate(mine, axis=1) / plan.total_rows
         theirs = jnp.concatenate(theirs, axis=1) / plan.total_rows
         zeroth = jnp.where(side == 0, mine, theirs)
@@ -377,6 +395,8 @@
         )
         for q, slope in ((0, zeroth), (1, oneth)):
             grad_ref[q] = jnp.sum(jnp.where(marks, slope, 0.0), axis=1, keepdims=True)
+        for store in stores:
+            store.wait()
 
     return pl.pallas_call(
         body,
@@ -385,7 +405,11 @@
             jax.ShapeDtypeStruct((2, groups, 1), F32),
         ],
         in_specs=[SMEM, VMEM, VMEM, VMEM],
-        out_specs=[VMEM, VMEM],
+        out_specs=[ANY, VMEM],
+        scratch_shapes=[
+            pltpu.VMEM((2, half, columns), BF16),
+            pltpu.SemaphoreType.DMA((plan.out_blocks,)),
+        ],
         compiler_params=params(),
         name="focus",
     )(where, own, other, owners)
@@ -432,7 +456,9 @@
     for group in steps:
         received = [arrived[step] for step in group]
         parts.append(across(packed))
-        parts, received = lax.optimization_barrier((parts, received))
+        tied = [parts[-1][0]] if len(parts) > 1 else parts[-1]
+        tied, received = lax.optimization_barrier((tied, received))
+        parts[-1][: len(tied)] = tied
         held.update(zip(group, received))
         packed = pack_panels(plan, where, received)
     parts.append(across(packed))

time: 89.5 us -> 82.7 us (0.924)
  blocking collectives: 14.8 us -> 11.8 us
  waiting for transfers between devices: 30.1 us -> 27.4 us
  Pallas kernels: 20.3 us -> 19.1 us
    all_to_all x1, blocking collectives: 14.8 us -> 11.8 us  [shards(): lax.all_to_all(partials.reshape(2 * panels, GRP_DEV), ('aper', 'panel'),...]
    ppermute x9, waiting for transfers between devices: 11.9 us -> 9.16 us  [across(): lax.ppermute(pieces[flip - 1], 'panel', cell_flip(flip))]
  transfers between devices with their start and end apart: 13 -> 13, of which waited for: 7 -> 7; matrix products, arithmetic and copies ran while one was open for 1% -> 1% of each run, Pallas kernels for 7% -> 8%
where the time goes in v3:
time: 82.7 us; the launch traced here: 82.5 us
  waiting for transfers between devices  27.4 us (33%)
  Pallas kernels  19.1 us (23%)
  starting transfers between devices  16.7 us (20%)
  blocking collectives  11.8 us (14%)
  local copies, waits for them, and re-layouts  5.85 us (7%)
  between operations  0.85 us (1%)
    ppermute x3, waiting for transfers between devices, shards(): lax.ppermute(far[step - 1], 'panel', plane_shift(step))  16.1 us
    all_to_all x1, blocking collectives, shards(): lax.all_to_all(partials.reshape(2 * panels, GRP_DEV), ('aper', 'panel'),...  11.8 us
    ppermute x9, starting transfers between devices, across(): lax.ppermute(pieces[flip - 1], 'panel', cell_flip(flip))  10.5 us
    ppermute x9, waiting for transfers between devices, across(): lax.ppermute(pieces[flip - 1], 'panel', cell_flip(flip))  9.16 us
    pallas_call x1, Pallas kernels, merge(): pl.pallas_call(body, out_shape=[shape, shape], in_specs=[SMEM, SMEM, SMEM...  8.51 us
    ppermute x3, starting transfers between devices, shards(): lax.ppermute(far[step - 1], 'panel', plane_shift(step))  6.08 us
    unnamed x31, local copies, waits for them, and re-layouts  5.08 us
    pallas_call x2, Pallas kernels, build_angle(): pl.pallas_call(body, out_shape=jax.ShapeDtypeStruct((count, 2 * PAIR, PAI...  2.73 us
  transfers between devices with their start and end apart: 13, of which 7 were waited for; matrix products, arithmetic and copies ran while one was open for 1% of the time, Pallas kernels for 8%

profile of v3, /device:TPU:0, one launch (start us, length us, event | category | flops | bytes accessed | tf_op | source)
XLA Modules:
  0.0 82.5 jit_solution(16182386355998222504)
XLA Ops:
  0.7 1.4 %copy-done.2 = bf16[2,2,32,4096]{3,2,1,0:T(8,128)(2,1)S(1)} copy-done((bf16[2,2,32,4096]{3,2,1,0:T(8,128)(2,1)S(1)}, bf16[2,2,32,4096]{3,2,1,0:T(8,128)(2,1)}, u32[]{:S(2)}) %copy-start.2) | copy-done | bytes 1048600
  2.1 1.4 %pack_own.1 = (bf16[2,2,32,1536]{3,2,1,0:T(8,128)(2,1)S(1)}, bf16[2,2,32,1536]{3,2,1,0:T(8,128)(2,1)}, bf16[2,2,32,1536]{3,2,1,0:T(8,128)(2,1)S(1)}, bf16[1,2,2,...) custom-call(s32[2]{0:T(128)S(1)} %pad_add_fusion.where_ref, ...), custom_call_target="tpu_custom_call" | custom-call | tf_op jit(solution)/shard_map/pack_own/pallas_call | solution.py:84
  3.5 3.0 %collective-permute-start.3 = (bf16[2,2,32,1536]{3,2,1,0:T(8,128)(2,1)S(1)}, bf16[2,2,32,1536]{3,2,1,0:T(8,128)(2,1)S(1)}, u32[]{:S(2)}, u32[]{:S(2)}) collective-permute-start(bf16[2,2,32,1536]{3,2,1,0:T(8,128)(2,1)S(1)} %get-tuple-element.28), channel_id=1, source_target_pairs={{0,8},{2,10},{4,12},{6,14},{8,16},{10,18},{12,20},{14,22},{16,24},... | collective-permute-start | bytes 1179656 | tf_op jit(solution)/shard_map/ppermute | solution.py:452
  6.5 2.0 %collective-permute-start.4 = (bf16[2,2,32,1536]{3,2,1,0:T(8,128)(2,1)S(1)}, bf16[2,2,32,1536]{3,2,1,0:T(8,128)(2,1)S(1)}, u32[]{:S(2)}, u32[]{:S(2)}) collective-permute-start(bf16[2,2,32,1536]{3,2,1,0:T(8,128)(2,1)S(1)} %get-tuple-element.29), channel_id=1, source_target_pairs={{0,24},{2,26},{4,28},{6,30},{8,0},{10,2},{12,4},{14,6},{16,8},{18,... | collective-permute-start | bytes 1179656 | tf_op jit(solution)/shard_map/ppermute | solution.py:452
  8.6 1.7 %collective-permute-start = (bf16[1,2,2,32,768]{4,3,2,1,0:T(8,128)(2,1)S(1)}, bf16[1,2,2,32,768]{4,3,2,1,0:T(8,128)(2,1)S(1)}, u32[]{:S(2)}, u32[]{:S(2)}) collective-permute-start(bf16[1,2,2,32,768]{4,3,2,1,0:T(8,128)(2,1)S(1)} %get-tuple-element.25), channel_id=1, source_target_pairs={{0,2},{2,0},{4,6},{6,4},{8,10},{10,8},{12,14},{14,12},{16,18},{18,... | collective-permute-start | bytes 589832 | tf_op jit(solution)/shard_map/ppermute | solution.py:444
  10.3 1.5 %collective-permute-start.1 = (bf16[1,2,2,32,768]{4,3,2,1,0:T(8,128)(2,1)S(1)}, bf16[1,2,2,32,768]{4,3,2,1,0:T(8,128)(2,1)S(1)}, u32[]{:S(2)}, u32[]{:S(2)}) collective-permute-start(bf16[1,2,2,32,768]{4,3,2,1,0:T(8,128)(2,1)S(1)} %get-tuple-element.26), channel_id=1, source_target_pairs={{0,4},{2,6},{4,0},{6,2},{8,12},{10,14},{12,8},{14,10},{16,20},{18,... | collective-permute-start | bytes 589832 | tf_op jit(solution)/shard_map/ppermute | solution.py:444
  12.0 4.3 %collective-permute-done.refs_0_ = bf16[1,2,2,32,768]{4,3,2,1,0:T(8,128)(2,1)S(1)} collective-permute-done((bf16[1,2,2,32,768]{4,3,2,1,0:T(8,128)(2,1)S(1)}, bf16[1,2,2,32,768]{4,3,2,1,0:T(8,128)(2,1)S(1)}, u32[]{:S(2)}, u32[]{:S(2)}) %collective-permute-start) | collective-permute-done | bytes 196640 | tf_op jit(solution)/shard_map/ppermute | solution.py:444
  16.4 0.7 copy-done.5
  17.1 1.0 %collective-permute-start.6 = (bf16[2,2,32,1536]{3,2,1,0:T(8,128)(2,1)}, bf16[2,2,32,1536]{3,2,1,0:T(8,128)(2,1)S(1)}, u32[]{:S(2)}, u32[]{:S(2)}) collective-permute-start(bf16[2,2,32,1536]{3,2,1,0:T(8,128)(2,1)} %get-tuple-element.36), channel_id=1, source_target_pairs={{0,16},{2,18},{4,20},{6,22},{8,24},{10,26},{12,28},{14,30},{16,0},... | collective-permute-start | bytes 1179656 | tf_op jit(solution)/shard_map/ppermute | solution.py:452
  18.1 2.3 %collective-permute-done.1.refs_1_ = bf16[1,2,2,32,768]{4,3,2,1,0:T(8,128)(2,1)S(1)} collective-permute-done((bf16[1,2,2,32,768]{4,3,2,1,0:T(8,128)(2,1)S(1)}, bf16[1,2,2,32,768]{4,3,2,1,0:T(8,128)(2,1)S(1)}, u32[]{:S(2)}, u32[]{:S(2)}) %collective-permute-start.1) | collective-permute-done | bytes 196640 | tf_op jit(solution)/shard_map/ppermute | solution.py:444
  20.3 0.7 copy-done.7
  21.0 0.7 copy-done.9
  21.7 3.8 %collective-permute-done.4.refs_1_.refs_12_ = bf16[2,2,32,1536]{3,2,1,0:T(8,128)(2,1)S(1)} collective-permute-done((bf16[2,2,32,1536]{3,2,1,0:T(8,128)(2,1)S(1)}, bf16[2,2,32,1536]{3,2,1,0:T(8,128)(2,1)S(1)}, u32[]{:S(2)}, u32[]{:S(2)}) %collective-permute-start.4) | collective-permute-done | bytes 393248 | tf_op jit(solution)/shard_map/ppermute | solution.py:452
  25.5 1.7 %pack_panels.2 = (bf16[2,2,2,32,768]{4,3,2,1,0:T(8,128)(2,1)}, bf16[2,2,2,32,768]{4,3,2,1,0:T(8,128)(2,1)}, bf16[2,2,2,32,768]{4,3,2,1,0:T(8,128)(2,1)}) custom-call(s32[2]{0:T(128)S(1)} %pad_add_fusion.where_ref, bf16[2,2,32,1536]{3,2,1,0:T(8,128)(2,1)S(1)} %collective-permute-done.3.refs_0_.refs_10_, ...), custom_call_target="tpu_custom_call" | custom-call | tf_op jit(solution)/shard_map/pack_panels/pallas_call | solution.py:114
  27.2 1.5 %collective-permute-start.5 = (bf16[2,2,2,32,768]{4,3,2,1,0:T(8,128)(2,1)}, bf16[2,2,2,32,768]{4,3,2,1,0:T(8,128)(2,1)}, u32[]{:S(2)}, u32[]{:S(2)}) collective-permute-start(bf16[2,2,2,32,768]{4,3,2,1,0:T(8,128)(2,1)} %get-tuple-element.35), channel_id=1, source_target_pairs={{0,2},{2,0},{4,6},{6,4},{8,10},{10,8},{12,14},{14,12},{16,18},{18,... | collective-permute-start | bytes 1179656 | tf_op jit(solution)/shard_map/ppermute | solution.py:444
  28.7 1.5 %collective-permute-start.7 = (bf16[2,2,2,32,768]{4,3,2,1,0:T(8,128)(2,1)}, bf16[2,2,2,32,768]{4,3,2,1,0:T(8,128)(2,1)}, u32[]{:S(2)}, u32[]{:S(2)}) collective-permute-start(bf16[2,2,2,32,768]{4,3,2,1,0:T(8,128)(2,1)} %get-tuple-element.38), channel_id=1, source_target_pairs={{0,4},{2,6},{4,0},{6,2},{8,12},{10,14},{12,8},{14,10},{16,20},{18,... | collective-permute-start | bytes 1179656 | tf_op jit(solution)/shard_map/ppermute | solution.py:444
  30.7 12.3 %collective-permute-done.6.refs_0_.refs_11_ = bf16[2,2,32,1536]{3,2,1,0:T(8,128)(2,1)S(1)} collective-permute-done((bf16[2,2,32,1536]{3,2,1,0:T(8,128)(2,1)}, bf16[2,2,32,1536]{3,2,1,0:T(8,128)(2,1)S(1)}, u32[]{:S(2)}, u32[]{:S(2)}) %collective-permute-start.6) | collective-permute-done | bytes 393248 | tf_op jit(solution)/shard_map/ppermute | solution.py:452
  42.9 0.6 pack_panels.3
  43.5 1.6 %collective-permute-start.10 = (bf16[1,2,2,32,768]{4,3,2,1,0:T(8,128)(2,1)S(1)}, bf16[1,2,2,32,768]{4,3,2,1,0:T(8,128)(2,1)S(1)}, u32[]{:S(2)}, u32[]{:S(2)}) collective-permute-start(bf16[1,2,2,32,768]{4,3,2,1,0:T(8,128)(2,1)S(1)} %get-tuple-element.42), channel_id=1, source_target_pairs={{0,4},{2,6},{4,0},{6,2},{8,12},{10,14},{12,8},{14,10},{16,20},{18,... | collective-permute-start | bytes 589832 | tf_op jit(solution)/shard_map/ppermute | solution.py:444
  45.1 1.4 %collective-permute-start.11 = (bf16[1,2,2,32,768]{4,3,2,1,0:T(8,128)(2,1)S(1)}, bf16[1,2,2,32,768]{4,3,2,1,0:T(8,128)(2,1)S(1)}, u32[]{:S(2)}, u32[]{:S(2)}) collective-permute-start(bf16[1,2,2,32,768]{4,3,2,1,0:T(8,128)(2,1)S(1)} %get-tuple-element.43), channel_id=1, source_target_pairs={{0,6},{2,4},{4,2},{6,0},{8,14},{10,12},{12,10},{14,8},{16,22},{18,... | collective-permute-start | bytes 589832 | tf_op jit(solution)/shard_map/ppermute | solution.py:444
  46.6 0.5 collective-permute-start.9
  47.2 1.5 %build_angle.2.refs_14_ = bf16[12,512,256]{2,1,0:T(8,128)(2,1)S(1)} custom-call(s32[12]{0:T(128)S(1)} %pad_add_fusion.1.blocks_ref, s32[1,32768]{1,0:T(1,128)S(1)} %copy-done.4, bf16[2,16,32768]{2,1,0:T(8,128)(2,1)S(1)} %bitcast.11), custom_call_target="tpu_custom_call" | custom-call | tf_op jit(solution)/shard_map/build_angle/pallas_call | solution.py:157
  48.7 1.6 %copy-done = bf16[12,512,256]{2,1,0:T(8,128)(2,1)} copy-done((bf16[12,512,256]{2,1,0:T(8,128)(2,1)}, bf16[12,512,256]{2,1,0:T(8,128)(2,1)S(1)}, u32[]{:S(2)}) %copy-start) | copy-done | bytes 3145752
  50.4 1.2 %build_angle.3.refs_15_ = bf16[8,512,256]{2,1,0:T(8,128)(2,1)S(1)} custom-call(s32[8]{0:T(128)S(1)} %iota_add_fusion.blocks_ref, s32[1,32768]{1,0:T(1,128)S(1)} %copy-done.4, bf16[2,16,32768]{2,1,0:T(8,128)(2,1)S(1)} %bitcast.12), custom_call_target="tpu_custom_call" | custom-call | tf_op jit(solution)/shard_map/build_angle/pallas_call | solution.py:157
  51.7 1.7 %build_range.1.refs_13_ = bf16[3,4,256,256]{3,2,1,0:T(8,128)(2,1)S(1)} custom-call(s32[3,1,512]{2,1,0:T(1,128)S(1)} %bitcast.16, bf16[3,2,16,512]{3,2,1,0:T(8,128)(2,1)S(1)} %bitcast.13), custom_call_target="tpu_custom_call" | custom-call | tf_op jit(solution)/shard_map/build_range/pallas_call | solution.py:184
  53.4 2.4 %collective-permute-done.10.refs_7_ = bf16[1,2,2,32,768]{4,3,2,1,0:T(8,128)(2,1)S(1)} collective-permute-done((bf16[1,2,2,32,768]{4,3,2,1,0:T(8,128)(2,1)S(1)}, bf16[1,2,2,32,768]{4,3,2,1,0:T(8,128)(2,1)S(1)}, u32[]{:S(2)}, u32[]{:S(2)}) %collective-permute-start.10) | collective-permute-done | bytes 196640 | tf_op jit(solution)/shard_map/ppermute | solution.py:444
  56.0 8.5 %merge.1 = (bf16[256,2048]{1,0:T(8,128)(2,1)S(1)}, bf16[256,2048]{1,0:T(8,128)(2,1)}) custom-call(s32[2]{0:T(128)S(1)} %pad_add_fusion.where_ref, s32[3,4]{1,0:T(4,128)S(1)} %bitcast.15, s32[1,256]{1,0:T(1,128)S(1)} %copy-done.13, bf16[1,2,2,32,768]{4,3,2,1,0:T(8,128)(2,1)S(1)} %copy-done.6, bf16[1,2,2,32,768]{4,3,2,1,0:T(8,128)(2,1)S(1)} %copy-done.8, ...), custom_call_target="tpu_custom_call" | custom-call | tf_op jit(solution)/shard_map/merge/pallas_call | solution.py:327
  64.6 0.7 dynamic-slice.3
  65.3 2.2 %collective-permute-done.12.oth_ref = bf16[256,2048]{1,0:T(8,128)(2,1)S(1)} collective-permute-done((bf16[256,2048]{1,0:T(8,128)(2,1)}, bf16[256,2048]{1,0:T(8,128)(2,1)S(1)}, u32[]{:S(2)}, u32[]{:S(2)}) %collective-permute-start.12) | collective-permute-done | bytes 1048608 | tf_op jit(solution)/shard_map/ppermute | solution.py:482
  67.5 2.4 %focus.1 = (bf16[2,256,1024]{2,1,0:T(8,128)(2,1)}, f32[2,64,1]{2,1,0:T(8,128)S(1)}) custom-call(s32[2]{0:T(128)S(1)} %pad_add_fusion.where_ref, bf16[256,2048]{1,0:T(8,128)(2,1)S(1)} %get-tuple-element.44.own_ref, bf16[256,2048]{1,0:T(8,128)(2,1)S(1)} %collective-permute-done.12.oth_ref, s32[1,1024]{1,0:T(1,128)S(1)} %bitcast.14), custom_call_target="tpu_custom_call" | custom-call | tf_op jit(solution)/shard_map/focus/pallas_call | solution.py:401
  70.1 11.8 %all_to_all.9 = f32[32,1,4]{2,1,0:T(1,128)S(1)} all-to-all(f32[32,1,4]{2,1,0:T(1,128)S(1)} %bitcast.17), channel_id=1, replica_groups=mesh['scene'=1,'panel'=16,'aper'=2] {'aper','panel'}, dimensions={0} | all-to-all | bytes 1024 | tf_op jit(solution)/shard_map/all_to_all | solution.py:486
  81.9 0.6 reduce_sum.9
  (42 shorter events, 1.3 us)
Async XLA Ops:
  0.6 46.6 %copy-start.1 = (bf16[1,2,16,32768]{3,2,1,0:T(8,128)(2,1)S(1)}, bf16[1,2,16,32768]{3,2,1,0:T(8,128)(2,1)}, u32[]{:S(2)}) copy-start(bf16[1,2,16,32768]{3,2,1,0:T(8,128)(2,1)} %param.14) | copy-start | bytes 6291460
  0.7 1.4 %copy-start.2 = (bf16[2,2,32,4096]{3,2,1,0:T(8,128)(2,1)S(1)}, bf16[2,2,32,4096]{3,2,1,0:T(8,128)(2,1)}, u32[]{:S(2)}) copy-start(bf16[2,2,32,4096]{3,2,1,0:T(8,128)(2,1)} %refs_9_.1) | copy-start | bytes 3145732
  2.1 45.1 %copy-start.4 = (s32[1,32768]{1,0:T(1,128)S(1)}, s32[1,32768]{1,0:T(1,128)}, u32[]{:S(2)}) copy-start(s32[1,32768]{1,0:T(1,128)} %taps_ref.3) | copy-start | bytes 393220
  3.5 18.2 %collective-permute-start.3 = (bf16[2,2,32,1536]{3,2,1,0:T(8,128)(2,1)S(1)}, bf16[2,2,32,1536]{3,2,1,0:T(8,128)(2,1)S(1)}, u32[]{:S(2)}, u32[]{:S(2)}) collective-permute-start(bf16[2,2,32,1536]{3,2,1,0:T(8,128)(2,1)S(1)} %get-tuple-element.28), channel_id=1, source_target_pairs={{0,8},{2,10},{4,12},{6,14},{8,16},{10,18},{12,20},{14,22},{16,24},... | collective-permute-start | bytes 1179656 | tf_op jit(solution)/shard_map/ppermute | solution.py:452
  6.5 19.0 %collective-permute-start.4 = (bf16[2,2,32,1536]{3,2,1,0:T(8,128)(2,1)S(1)}, bf16[2,2,32,1536]{3,2,1,0:T(8,128)(2,1)S(1)}, u32[]{:S(2)}, u32[]{:S(2)}) collective-permute-start(bf16[2,2,32,1536]{3,2,1,0:T(8,128)(2,1)S(1)} %get-tuple-element.29), channel_id=1, source_target_pairs={{0,24},{2,26},{4,28},{6,30},{8,0},{10,2},{12,4},{14,6},{16,8},{18,... | collective-permute-start | bytes 1179656 | tf_op jit(solution)/shard_map/ppermute | solution.py:452
  8.6 7.8 %collective-permute-start = (bf16[1,2,2,32,768]{4,3,2,1,0:T(8,128)(2,1)S(1)}, bf16[1,2,2,32,768]{4,3,2,1,0:T(8,128)(2,1)S(1)}, u32[]{:S(2)}, u32[]{:S(2)}) collective-permute-start(bf16[1,2,2,32,768]{4,3,2,1,0:T(8,128)(2,1)S(1)} %get-tuple-element.25), channel_id=1, source_target_pairs={{0,2},{2,0},{4,6},{6,4},{8,10},{10,8},{12,14},{14,12},{16,18},{18,... | collective-permute-start | bytes 589832 | tf_op jit(solution)/shard_map/ppermute | solution.py:444
  10.3 10.1 %collective-permute-start.1 = (bf16[1,2,2,32,768]{4,3,2,1,0:T(8,128)(2,1)S(1)}, bf16[1,2,2,32,768]{4,3,2,1,0:T(8,128)(2,1)S(1)}, u32[]{:S(2)}, u32[]{:S(2)}) collective-permute-start(bf16[1,2,2,32,768]{4,3,2,1,0:T(8,128)(2,1)S(1)} %get-tuple-element.26), channel_id=1, source_target_pairs={{0,4},{2,6},{4,0},{6,2},{8,12},{10,14},{12,8},{14,10},{16,20},{18,... | collective-permute-start | bytes 589832 | tf_op jit(solution)/shard_map/ppermute | solution.py:444
  11.8 9.3 %collective-permute-start.2 = (bf16[1,2,2,32,768]{4,3,2,1,0:T(8,128)(2,1)S(1)}, bf16[1,2,2,32,768]{4,3,2,1,0:T(8,128)(2,1)S(1)}, u32[]{:S(2)}, u32[]{:S(2)}) collective-permute-start(bf16[1,2,2,32,768]{4,3,2,1,0:T(8,128)(2,1)S(1)} %get-tuple-element.27), channel_id=1, source_target_pairs={{0,6},{2,4},{4,2},{6,0},{8,14},{10,12},{12,10},{14,8},{16,22},{18,... | collective-permute-start | bytes 589832 | tf_op jit(solution)/shard_map/ppermute | solution.py:444
  16.4 0.7 copy-start.5
  17.1 25.9 %collective-permute-start.6 = (bf16[2,2,32,1536]{3,2,1,0:T(8,128)(2,1)}, bf16[2,2,32,1536]{3,2,1,0:T(8,128)(2,1)S(1)}, u32[]{:S(2)}, u32[]{:S(2)}) collective-permute-start(bf16[2,2,32,1536]{3,2,1,0:T(8,128)(2,1)} %get-tuple-element.36), channel_id=1, source_target_pairs={{0,16},{2,18},{4,20},{6,22},{8,24},{10,26},{12,28},{14,30},{16,0},... | collective-permute-start | bytes 1179656 | tf_op jit(solution)/shard_map/ppermute | solution.py:452
  20.3 0.7 copy-start.7
  21.0 0.7 copy-start.9
  27.2 15.8 %collective-permute-start.5 = (bf16[2,2,2,32,768]{4,3,2,1,0:T(8,128)(2,1)}, bf16[2,2,2,32,768]{4,3,2,1,0:T(8,128)(2,1)}, u32[]{:S(2)}, u32[]{:S(2)}) collective-permute-start(bf16[2,2,2,32,768]{4,3,2,1,0:T(8,128)(2,1)} %get-tuple-element.35), channel_id=1, source_target_pairs={{0,2},{2,0},{4,6},{6,4},{8,10},{10,8},{12,14},{14,12},{16,18},{18,... | collective-permute-start | bytes 1179656 | tf_op jit(solution)/shard_map/ppermute | solution.py:444
  28.7 24.7 %collective-permute-start.7 = (bf16[2,2,2,32,768]{4,3,2,1,0:T(8,128)(2,1)}, bf16[2,2,2,32,768]{4,3,2,1,0:T(8,128)(2,1)}, u32[]{:S(2)}, u32[]{:S(2)}) collective-permute-start(bf16[2,2,2,32,768]{4,3,2,1,0:T(8,128)(2,1)} %get-tuple-element.38), channel_id=1, source_target_pairs={{0,4},{2,6},{4,0},{6,2},{8,12},{10,14},{12,8},{14,10},{16,20},{18,... | collective-permute-start | bytes 1179656 | tf_op jit(solution)/shard_map/ppermute | solution.py:444
  30.2 23.2 %collective-permute-start.8 = (bf16[2,2,2,32,768]{4,3,2,1,0:T(8,128)(2,1)}, bf16[2,2,2,32,768]{4,3,2,1,0:T(8,128)(2,1)}, u32[]{:S(2)}, u32[]{:S(2)}) collective-permute-start(bf16[2,2,2,32,768]{4,3,2,1,0:T(8,128)(2,1)} %get-tuple-element.39), channel_id=1, source_target_pairs={{0,6},{2,4},{4,2},{6,0},{8,14},{10,12},{12,10},{14,8},{16,22},{18,... | collective-permute-start | bytes 1179656 | tf_op jit(solution)/shard_map/ppermute | solution.py:444
  43.5 12.3 %collective-permute-start.10 = (bf16[1,2,2,32,768]{4,3,2,1,0:T(8,128)(2,1)S(1)}, bf16[1,2,2,32,768]{4,3,2,1,0:T(8,128)(2,1)S(1)}, u32[]{:S(2)}, u32[]{:S(2)}) collective-permute-start(bf16[1,2,2,32,768]{4,3,2,1,0:T(8,128)(2,1)S(1)} %get-tuple-element.42), channel_id=1, source_target_pairs={{0,4},{2,6},{4,0},{6,2},{8,12},{10,14},{12,8},{14,10},{16,20},{18,... | collective-permute-start | bytes 589832 | tf_op jit(solution)/shard_map/ppermute | solution.py:444
  45.1 10.7 %collective-permute-start.11 = (bf16[1,2,2,32,768]{4,3,2,1,0:T(8,128)(2,1)S(1)}, bf16[1,2,2,32,768]{4,3,2,1,0:T(8,128)(2,1)S(1)}, u32[]{:S(2)}, u32[]{:S(2)}) collective-permute-start(bf16[1,2,2,32,768]{4,3,2,1,0:T(8,128)(2,1)S(1)} %get-tuple-element.43), channel_id=1, source_target_pairs={{0,6},{2,4},{4,2},{6,0},{8,14},{10,12},{12,10},{14,8},{16,22},{18,... | collective-permute-start | bytes 589832 | tf_op jit(solution)/shard_map/ppermute | solution.py:444
  46.6 9.4 %collective-permute-start.9 = (bf16[1,2,2,32,768]{4,3,2,1,0:T(8,128)(2,1)S(1)}, bf16[1,2,2,32,768]{4,3,2,1,0:T(8,128)(2,1)S(1)}, u32[]{:S(2)}, u32[]{:S(2)}) collective-permute-start(bf16[1,2,2,32,768]{4,3,2,1,0:T(8,128)(2,1)S(1)} %get-tuple-element.41), channel_id=1, source_target_pairs={{0,2},{2,0},{4,6},{6,4},{8,10},{10,8},{12,14},{14,12},{16,18},{18,... | collective-permute-start | bytes 589832 | tf_op jit(solution)/shard_map/ppermute | solution.py:444
  48.7 1.6 %copy-start = (bf16[12,512,256]{2,1,0:T(8,128)(2,1)}, bf16[12,512,256]{2,1,0:T(8,128)(2,1)S(1)}, u32[]{:S(2)}) copy-start(bf16[12,512,256]{2,1,0:T(8,128)(2,1)S(1)} %build_angle.2.refs_14_) | copy-start | bytes 9437188
  50.4 1.3 %copy-start.14 = (s32[1,3,4]{2,0,1:T(1,128)S(1)}, s32[1,3,4]{2,0,1:T(1,128)}, u32[]{:S(2)}) copy-start(s32[1,3,4]{2,0,1:T(1,128)} %param.10) | copy-start | bytes 148
  50.4 1.3 %copy-start.11 = (bf16[1,3,2,16,512]{4,3,2,1,0:T(8,128)(2,1)S(1)}, bf16[1,3,2,16,512]{4,3,2,1,0:T(8,128)(2,1)}, u32[]{:S(2)}) copy-start(bf16[1,3,2,16,512]{4,3,2,1,0:T(8,128)(2,1)} %param.11) | copy-start | bytes 294916
  50.4 1.3 %copy-start.12 = (s32[1,3,512]{2,0,1:T(1,128)S(1)}, s32[1,3,512]{2,0,1:T(1,128)}, u32[]{:S(2)}) copy-start(s32[1,3,512]{2,0,1:T(1,128)} %param.9) | copy-start | bytes 18436
  50.4 5.6 %copy-start.3 = (bf16[2,2,32,4096]{3,2,1,0:T(8,128)(2,1)S(1)}, bf16[2,2,32,4096]{3,2,1,0:T(8,128)(2,1)}, u32[]{:S(2)}) copy-start(bf16[2,2,32,4096]{3,2,1,0:T(8,128)(2,1)} %refs_9_.1) | copy-start | bytes 3145732
  50.4 5.6 %copy-start.6 = (bf16[1,2,2,32,768]{4,3,2,1,0:T(8,128)(2,1)S(1)}, bf16[1,2,2,32,768]{4,3,2,1,0:T(8,128)(2,1)}, u32[]{:S(2)}) copy-start(bf16[1,2,2,32,768]{4,3,2,1,0:T(8,128)(2,1)} %copy-done.5) | copy-start | bytes 589828
  50.4 5.6 %copy-start.8 = (bf16[1,2,2,32,768]{4,3,2,1,0:T(8,128)(2,1)S(1)}, bf16[1,2,2,32,768]{4,3,2,1,0:T(8,128)(2,1)}, u32[]{:S(2)}) copy-start(bf16[1,2,2,32,768]{4,3,2,1,0:T(8,128)(2,1)} %copy-done.7) | copy-start | bytes 589828
  50.4 5.6 %copy-start.10 = (bf16[1,2,2,32,768]{4,3,2,1,0:T(8,128)(2,1)S(1)}, bf16[1,2,2,32,768]{4,3,2,1,0:T(8,128)(2,1)}, u32[]{:S(2)}) copy-start(bf16[1,2,2,32,768]{4,3,2,1,0:T(8,128)(2,1)} %copy-done.9) | copy-start | bytes 589828
  50.4 5.6 %copy-start.13 = (s32[1,256]{1,0:T(1,128)S(1)}, s32[1,256]{1,0:T(1,128)}, u32[]{:S(2)}) copy-start(s32[1,256]{1,0:T(1,128)} %ab_ref.1) | copy-start | bytes 3076
  64.5 2.9 %collective-permute-start.12 = (bf16[256,2048]{1,0:T(8,128)(2,1)}, bf16[256,2048]{1,0:T(8,128)(2,1)S(1)}, u32[]{:S(2)}, u32[]{:S(2)}) collective-permute-start(bf16[256,2048]{1,0:T(8,128)(2,1)} %get-tuple-element.45), channel_id=1, source_target_pairs={{0,1},{1,0},{2,3},{3,2},{4,5},{5,4},{6,7},{7,6},{8,9},{9,8},{10,11... | collective-permute-start | bytes 3145736 | tf_op jit(solution)/shard_map/ppermute | solution.py:482

commit v4 on v3

--- a/solution.py
+++ b/solution.py
@@ -57,35 +57,31 @@
 ANY = pl.BlockSpec(memory_space=pl.ANY)
 
 
-def pack_own(plan, where, subimages):
+def pack_own(plan, where, subimages, steps, flips):
     members = subimages.shape[0]
-    others = plan.planes - 1
+    others = len(steps)
 
     def body(where_ref, x_ref, *outs):
         panel = where_ref[0]
         plane = panel // plan.cells
         cell = lax.rem(panel, plan.cells)
-        for step in range(1, plan.planes):
+        for at, step in enumerate(steps):
             target = lax.rem(plane + step, plan.planes)
             column = aligned(plan.plane_start(target), TILE)
-            outs[step - 1][...] = x_ref[
-                :, :, :, pl.ds(column, plan.plane_window * TILE)
-            ]
-        for flip in range(1, plan.cells):
+            outs[at][...] = x_ref[:, :, :, pl.ds(column, plan.plane_window * TILE)]
+        for at, flip in enumerate(flips):
             target = plane * plan.cells + (cell ^ flip)
             column = aligned(plan.panel_start(target), TILE)
-            outs[others + flip - 1][0] = x_ref[
-                :, :, :, pl.ds(column, plan.panel_window * TILE)
-            ]
+            outs[others + at][0] = x_ref[:, :, :, pl.ds(column, plan.panel_window * TILE)]
 
     lead = (members, 2, plan.rows)
     far = jax.ShapeDtypeStruct(lead + (plan.plane_window * TILE,), BF16)
     near = jax.ShapeDtypeStruct((1,) + lead + (plan.panel_window * TILE,), BF16)
     outs = pl.pallas_call(
         body,
-        out_shape=[far] * others + [near] * (plan.cells - 1),
+        out_shape=[far] * others + [near] * len(flips),
         in_specs=[SMEM, VMEM],
-        out_specs=[VMEM] * (others + plan.cells - 1),
+        out_specs=[VMEM] * (others + len(flips)),
         compiler_params=params(),
         name="pack_own",
     )(where, subimages)
@@ -437,7 +433,10 @@
         sorted({step, plan.planes - step}) for step in range(1, plan.planes // 2 + 1)
     ]
     order = [[0]] + steps
-    far, near_parts = pack_own(plan, where, subimages)
+    rest = [step for group in steps[1:] for step in group]
+    soon, _ = pack_own(plan, where, subimages, steps[0], [])
+    later, near_parts = pack_own(plan, where, subimages, rest, range(1, plan.cells))
+    far = dict(zip(steps[0] + rest, list(soon) + list(later)))
 
     def across(pieces):
         return [
@@ -449,7 +448,7 @@
     held = {0: subimages}
     packed = near_parts
     arrived = {
-        step: lax.ppermute(far[step - 1], "panel", plane_shift(step))
+        step: lax.ppermute(far[step], "panel", plane_shift(step))
         for group in steps
         for step in group
     }

time: 82.7 us -> 81.3 us (0.983)
  waiting for transfers between devices: 27.4 us -> 26 us
    ppermute x3, waiting for transfers between devices: 16.1 us -> 14.7 us  [shards(): lax.ppermute(far[step], 'panel', plane_shift(step))]
    pallas_call x1 -> x2, Pallas kernels: 1.42 us -> 1.97 us  [pack_own(): pl.pallas_call(body, out_shape=[far] * others + [near] * len(flips), in_s...]
  transfers between devices with their start and end apart: 13 -> 13, of which waited for: 7 -> 7; matrix products, arithmetic and copies ran while one was open for 1% -> 1% of each run, Pallas kernels for 8% -> 10%
where the time goes in v4:
time: 81.3 us; the launch traced here: 81.1 us
  waiting for transfers between devices  26 us (32%)
  Pallas kernels  19.6 us (24%)
  starting transfers between devices  16.7 us (21%)
  blocking collectives  11.3 us (14%)
  local copies, waits for them, and re-layouts  5.73 us (7%)
  between operations  0.85 us (1%)
    ppermute x3, waiting for transfers between devices, shards(): lax.ppermute(far[step], 'panel', plane_shift(step))  14.7 us
    all_to_all x1, blocking collectives, shards(): lax.all_to_all(partials.reshape(2 * panels, GRP_DEV), ('aper', 'panel'),...  11.3 us
    ppermute x9, starting transfers between devices, across(): lax.ppermute(pieces[flip - 1], 'panel', cell_flip(flip))  10.5 us
    ppermute x9, waiting for transfers between devices, across(): lax.ppermute(pieces[flip - 1], 'panel', cell_flip(flip))  9.22 us
    pallas_call x1, Pallas kernels, merge(): pl.pallas_call(body, out_shape=[shape, shape], in_specs=[SMEM, SMEM, SMEM...  8.51 us
    ppermute x3, starting transfers between devices, shards(): lax.ppermute(far[step], 'panel', plane_shift(step))  6.13 us
    unnamed x31, local copies, waits for them, and re-layouts  4.95 us
    pallas_call x2, Pallas kernels, build_angle(): pl.pallas_call(body, out_shape=jax.ShapeDtypeStruct((count, 2 * PAIR, PAI...  2.73 us
  transfers between devices with their start and end apart: 13, of which 7 were waited for; matrix products, arithmetic and copies ran while one was open for 1% of the time, Pallas kernels for 10%

profile of v4, /device:TPU:0, one launch (start us, length us, event | category | flops | bytes accessed | tf_op | source)
XLA Modules:
  0.0 81.1 jit_solution(12822341629286387770)
XLA Ops:
  0.7 1.2 %copy-done.1 = bf16[2,2,32,4096]{3,2,1,0:T(8,128)(2,1)S(1)} copy-done((bf16[2,2,32,4096]{3,2,1,0:T(8,128)(2,1)S(1)}, bf16[2,2,32,4096]{3,2,1,0:T(8,128)(2,1)}, u32[]{:S(2)}) %copy-start.1) | copy-done | bytes 1048600
  1.9 0.6 pack_own.3
  2.6 3.1 %collective-permute-start.3 = (bf16[2,2,32,1536]{3,2,1,0:T(8,128)(2,1)S(1)}, bf16[2,2,32,1536]{3,2,1,0:T(8,128)(2,1)S(1)}, u32[]{:S(2)}, u32[]{:S(2)}) collective-permute-start(bf16[2,2,32,1536]{3,2,1,0:T(8,128)(2,1)S(1)} %get-tuple-element.28), channel_id=1, source_target_pairs={{0,8},{2,10},{4,12},{6,14},{8,16},{10,18},{12,20},{14,22},{16,24},... | collective-permute-start | bytes 1179656 | tf_op jit(solution)/shard_map/ppermute | solution.py:451
  5.6 2.1 %collective-permute-start.4 = (bf16[2,2,32,1536]{3,2,1,0:T(8,128)(2,1)S(1)}, bf16[2,2,32,1536]{3,2,1,0:T(8,128)(2,1)S(1)}, u32[]{:S(2)}, u32[]{:S(2)}) collective-permute-start(bf16[2,2,32,1536]{3,2,1,0:T(8,128)(2,1)S(1)} %get-tuple-element.29), channel_id=1, source_target_pairs={{0,24},{2,26},{4,28},{6,30},{8,0},{10,2},{12,4},{14,6},{16,8},{18,... | collective-permute-start | bytes 1179656 | tf_op jit(solution)/shard_map/ppermute | solution.py:451
  7.7 1.4 %pack_own.2 = (bf16[2,2,32,1536]{3,2,1,0:T(8,128)(2,1)}, bf16[1,2,2,32,768]{4,3,2,1,0:T(8,128)(2,1)S(1)}, bf16[1,2,2,32,768]{4,3,2,1,0:T(8,128)(2,1)S(1)}, bf16[1,2,2,32,768]{4,3,2,1,0:T(8,128)(2,1)S(1)}) custom-call(s32[2]{0:T(128)S(1)} %pad_add_fusion.where_ref, bf16[2,2,32,4096]{3,2,1,0:T(8,128)(2,1)S(1)} %copy-done.1), custom_call_target="tpu_custom_call" | custom-call | tf_op jit(solution)/shard_map/pack_own/pallas_call | solution.py:80
  9.1 1.6 %collective-permute-start = (bf16[1,2,2,32,768]{4,3,2,1,0:T(8,128)(2,1)S(1)}, bf16[1,2,2,32,768]{4,3,2,1,0:T(8,128)(2,1)S(1)}, u32[]{:S(2)}, u32[]{:S(2)}) collective-permute-start(bf16[1,2,2,32,768]{4,3,2,1,0:T(8,128)(2,1)S(1)} %get-tuple-element.25), channel_id=1, source_target_pairs={{0,2},{2,0},{4,6},{6,4},{8,10},{10,8},{12,14},{14,12},{16,18},{18,... | collective-permute-start | bytes 589832 | tf_op jit(solution)/shard_map/ppermute | solution.py:443
  10.7 1.5 %collective-permute-start.1 = (bf16[1,2,2,32,768]{4,3,2,1,0:T(8,128)(2,1)S(1)}, bf16[1,2,2,32,768]{4,3,2,1,0:T(8,128)(2,1)S(1)}, u32[]{:S(2)}, u32[]{:S(2)}) collective-permute-start(bf16[1,2,2,32,768]{4,3,2,1,0:T(8,128)(2,1)S(1)} %get-tuple-element.26), channel_id=1, source_target_pairs={{0,4},{2,6},{4,0},{6,2},{8,12},{10,14},{12,8},{14,10},{16,20},{18,... | collective-permute-start | bytes 589832 | tf_op jit(solution)/shard_map/ppermute | solution.py:443
  12.6 4.3 %collective-permute-done.refs_0_ = bf16[1,2,2,32,768]{4,3,2,1,0:T(8,128)(2,1)S(1)} collective-permute-done((bf16[1,2,2,32,768]{4,3,2,1,0:T(8,128)(2,1)S(1)}, bf16[1,2,2,32,768]{4,3,2,1,0:T(8,128)(2,1)S(1)}, u32[]{:S(2)}, u32[]{:S(2)}) %collective-permute-start) | collective-permute-done | bytes 196640 | tf_op jit(solution)/shard_map/ppermute | solution.py:443
  16.9 0.7 copy-done.5
  17.6 1.0 %collective-permute-start.6 = (bf16[2,2,32,1536]{3,2,1,0:T(8,128)(2,1)}, bf16[2,2,32,1536]{3,2,1,0:T(8,128)(2,1)S(1)}, u32[]{:S(2)}, u32[]{:S(2)}) collective-permute-start(bf16[2,2,32,1536]{3,2,1,0:T(8,128)(2,1)} %get-tuple-element.36), channel_id=1, source_target_pairs={{0,16},{2,18},{4,20},{6,22},{8,24},{10,26},{12,28},{14,30},{16,0},... | collective-permute-start | bytes 1179656 | tf_op jit(solution)/shard_map/ppermute | solution.py:451
  18.6 2.3 %collective-permute-done.1.refs_1_ = bf16[1,2,2,32,768]{4,3,2,1,0:T(8,128)(2,1)S(1)} collective-permute-done((bf16[1,2,2,32,768]{4,3,2,1,0:T(8,128)(2,1)S(1)}, bf16[1,2,2,32,768]{4,3,2,1,0:T(8,128)(2,1)S(1)}, u32[]{:S(2)}, u32[]{:S(2)}) %collective-permute-start.1) | collective-permute-done | bytes 196640 | tf_op jit(solution)/shard_map/ppermute | solution.py:443
  20.9 0.7 copy-done.7
  21.6 0.7 copy-done.9
  22.3 2.4 %collective-permute-done.4.refs_1_.refs_12_ = bf16[2,2,32,1536]{3,2,1,0:T(8,128)(2,1)S(1)} collective-permute-done((bf16[2,2,32,1536]{3,2,1,0:T(8,128)(2,1)S(1)}, bf16[2,2,32,1536]{3,2,1,0:T(8,128)(2,1)S(1)}, u32[]{:S(2)}, u32[]{:S(2)}) %collective-permute-start.4) | collective-permute-done | bytes 393248 | tf_op jit(solution)/shard_map/ppermute | solution.py:451
  24.6 1.6 %pack_panels.2 = (bf16[2,2,2,32,768]{4,3,2,1,0:T(8,128)(2,1)}, bf16[2,2,2,32,768]{4,3,2,1,0:T(8,128)(2,1)}, bf16[2,2,2,32,768]{4,3,2,1,0:T(8,128)(2,1)}) custom-call(s32[2]{0:T(128)S(1)} %pad_add_fusion.where_ref, bf16[2,2,32,1536]{3,2,1,0:T(8,128)(2,1)S(1)} %collective-permute-done.3.refs_0_.refs_10_, ...), custom_call_target="tpu_custom_call" | custom-call | tf_op jit(solution)/shard_map/pack_panels/pallas_call | solution.py:110
  26.3 1.5 %collective-permute-start.5 = (bf16[2,2,2,32,768]{4,3,2,1,0:T(8,128)(2,1)}, bf16[2,2,2,32,768]{4,3,2,1,0:T(8,128)(2,1)}, u32[]{:S(2)}, u32[]{:S(2)}) collective-permute-start(bf16[2,2,2,32,768]{4,3,2,1,0:T(8,128)(2,1)} %get-tuple-element.35), channel_id=1, source_target_pairs={{0,2},{2,0},{4,6},{6,4},{8,10},{10,8},{12,14},{14,12},{16,18},{18,... | collective-permute-start | bytes 1179656 | tf_op jit(solution)/shard_map/ppermute | solution.py:443
  27.8 1.5 %collective-permute-start.7 = (bf16[2,2,2,32,768]{4,3,2,1,0:T(8,128)(2,1)}, bf16[2,2,2,32,768]{4,3,2,1,0:T(8,128)(2,1)}, u32[]{:S(2)}, u32[]{:S(2)}) collective-permute-start(bf16[2,2,2,32,768]{4,3,2,1,0:T(8,128)(2,1)} %get-tuple-element.38), channel_id=1, source_target_pairs={{0,4},{2,6},{4,0},{6,2},{8,12},{10,14},{12,8},{14,10},{16,20},{18,... | collective-permute-start | bytes 1179656 | tf_op jit(solution)/shard_map/ppermute | solution.py:443
  29.8 12.3 %collective-permute-done.6.refs_0_.refs_11_ = bf16[2,2,32,1536]{3,2,1,0:T(8,128)(2,1)S(1)} collective-permute-done((bf16[2,2,32,1536]{3,2,1,0:T(8,128)(2,1)}, bf16[2,2,32,1536]{3,2,1,0:T(8,128)(2,1)S(1)}, u32[]{:S(2)}, u32[]{:S(2)}) %collective-permute-start.6) | collective-permute-done | bytes 393248 | tf_op jit(solution)/shard_map/ppermute | solution.py:451
  42.1 0.6 pack_panels.3
  42.7 1.6 %collective-permute-start.10 = (bf16[1,2,2,32,768]{4,3,2,1,0:T(8,128)(2,1)S(1)}, bf16[1,2,2,32,768]{4,3,2,1,0:T(8,128)(2,1)S(1)}, u32[]{:S(2)}, u32[]{:S(2)}) collective-permute-start(bf16[1,2,2,32,768]{4,3,2,1,0:T(8,128)(2,1)S(1)} %get-tuple-element.42), channel_id=1, source_target_pairs={{0,4},{2,6},{4,0},{6,2},{8,12},{10,14},{12,8},{14,10},{16,20},{18,... | collective-permute-start | bytes 589832 | tf_op jit(solution)/shard_map/ppermute | solution.py:443
  44.2 1.4 %collective-permute-start.11 = (bf16[1,2,2,32,768]{4,3,2,1,0:T(8,128)(2,1)S(1)}, bf16[1,2,2,32,768]{4,3,2,1,0:T(8,128)(2,1)S(1)}, u32[]{:S(2)}, u32[]{:S(2)}) collective-permute-start(bf16[1,2,2,32,768]{4,3,2,1,0:T(8,128)(2,1)S(1)} %get-tuple-element.43), channel_id=1, source_target_pairs={{0,6},{2,4},{4,2},{6,0},{8,14},{10,12},{12,10},{14,8},{16,22},{18,... | collective-permute-start | bytes 589832 | tf_op jit(solution)/shard_map/ppermute | solution.py:443
  46.3 1.5 %build_angle.2.refs_14_ = bf16[12,512,256]{2,1,0:T(8,128)(2,1)S(1)} custom-call(s32[12]{0:T(128)S(1)} %pad_add_fusion.1.blocks_ref, s32[1,32768]{1,0:T(1,128)S(1)} %copy-done.4, bf16[2,16,32768]{2,1,0:T(8,128)(2,1)S(1)} %bitcast.11), custom_call_target="tpu_custom_call" | custom-call | tf_op jit(solution)/shard_map/build_angle/pallas_call | solution.py:153
  47.8 1.6 %copy-done = bf16[12,512,256]{2,1,0:T(8,128)(2,1)} copy-done((bf16[12,512,256]{2,1,0:T(8,128)(2,1)}, bf16[12,512,256]{2,1,0:T(8,128)(2,1)S(1)}, u32[]{:S(2)}) %copy-start) | copy-done | bytes 3145752
  49.5 1.2 %build_angle.3.refs_15_ = bf16[8,512,256]{2,1,0:T(8,128)(2,1)S(1)} custom-call(s32[8]{0:T(128)S(1)} %iota_add_fusion.blocks_ref, s32[1,32768]{1,0:T(1,128)S(1)} %copy-done.4, bf16[2,16,32768]{2,1,0:T(8,128)(2,1)S(1)} %bitcast.12), custom_call_target="tpu_custom_call" | custom-call | tf_op jit(solution)/shard_map/build_angle/pallas_call | solution.py:153
  50.8 1.7 %build_range.1.refs_13_ = bf16[3,4,256,256]{3,2,1,0:T(8,128)(2,1)S(1)} custom-call(s32[3,1,512]{2,1,0:T(1,128)S(1)} %bitcast.16, bf16[3,2,16,512]{3,2,1,0:T(8,128)(2,1)S(1)} %bitcast.13), custom_call_target="tpu_custom_call" | custom-call | tf_op jit(solution)/shard_map/build_range/pallas_call | solution.py:180
  52.5 2.4 %collective-permute-done.10.refs_7_ = bf16[1,2,2,32,768]{4,3,2,1,0:T(8,128)(2,1)S(1)} collective-permute-done((bf16[1,2,2,32,768]{4,3,2,1,0:T(8,128)(2,1)S(1)}, bf16[1,2,2,32,768]{4,3,2,1,0:T(8,128)(2,1)S(1)}, u32[]{:S(2)}, u32[]{:S(2)}) %collective-permute-start.10) | collective-permute-done | bytes 196640 | tf_op jit(solution)/shard_map/ppermute | solution.py:443
  55.1 8.5 %merge.1 = (bf16[256,2048]{1,0:T(8,128)(2,1)S(1)}, bf16[256,2048]{1,0:T(8,128)(2,1)}) custom-call(s32[2]{0:T(128)S(1)} %pad_add_fusion.where_ref, s32[3,4]{1,0:T(4,128)S(1)} %bitcast.15, s32[1,256]{1,0:T(1,128)S(1)} %copy-done.13, bf16[1,2,2,32,768]{4,3,2,1,0:T(8,128)(2,1)S(1)} %copy-done.6, bf16[1,2,2,32,768]{4,3,2,1,0:T(8,128)(2,1)S(1)} %copy-done.8, ...), custom_call_target="tpu_custom_call" | custom-call | tf_op jit(solution)/shard_map/merge/pallas_call | solution.py:323
  63.7 0.7 dynamic-slice.3
  64.4 2.2 %collective-permute-done.12.oth_ref = bf16[256,2048]{1,0:T(8,128)(2,1)S(1)} collective-permute-done((bf16[256,2048]{1,0:T(8,128)(2,1)}, bf16[256,2048]{1,0:T(8,128)(2,1)S(1)}, u32[]{:S(2)}, u32[]{:S(2)}) %collective-permute-start.12) | collective-permute-done | bytes 1048608 | tf_op jit(solution)/shard_map/ppermute | solution.py:481
  66.6 2.4 %focus.1 = (bf16[2,256,1024]{2,1,0:T(8,128)(2,1)}, f32[2,64,1]{2,1,0:T(8,128)S(1)}) custom-call(s32[2]{0:T(128)S(1)} %pad_add_fusion.where_ref, bf16[256,2048]{1,0:T(8,128)(2,1)S(1)} %get-tuple-element.44.own_ref, bf16[256,2048]{1,0:T(8,128)(2,1)S(1)} %collective-permute-done.12.oth_ref, s32[1,1024]{1,0:T(1,128)S(1)} %bitcast.14), custom_call_target="tpu_custom_call" | custom-call | tf_op jit(solution)/shard_map/focus/pallas_call | solution.py:397
  69.2 11.3 %all_to_all.9 = f32[32,1,4]{2,1,0:T(1,128)S(1)} all-to-all(f32[32,1,4]{2,1,0:T(1,128)S(1)} %bitcast.17), channel_id=1, replica_groups=mesh['scene'=1,'panel'=16,'aper'=2] {'aper','panel'}, dimensions={0} | all-to-all | bytes 1024 | tf_op jit(solution)/shard_map/all_to_all | solution.py:485
  80.5 0.6 reduce_sum.9
  (43 shorter events, 1.9 us)
Async XLA Ops:
  0.7 1.2 %copy-start.1 = (bf16[2,2,32,4096]{3,2,1,0:T(8,128)(2,1)S(1)}, bf16[2,2,32,4096]{3,2,1,0:T(8,128)(2,1)}, u32[]{:S(2)}) copy-start(bf16[2,2,32,4096]{3,2,1,0:T(8,128)(2,1)} %refs_9_.1) | copy-start | bytes 3145732
  1.9 44.4 %copy-start.3 = (bf16[1,2,16,32768]{3,2,1,0:T(8,128)(2,1)S(1)}, bf16[1,2,16,32768]{3,2,1,0:T(8,128)(2,1)}, u32[]{:S(2)}) copy-start(bf16[1,2,16,32768]{3,2,1,0:T(8,128)(2,1)} %param.14) | copy-start | bytes 6291460
  1.9 44.4 %copy-start.4 = (s32[1,32768]{1,0:T(1,128)S(1)}, s32[1,32768]{1,0:T(1,128)}, u32[]{:S(2)}) copy-start(s32[1,32768]{1,0:T(1,128)} %taps_ref.3) | copy-start | bytes 393220
  2.6 19.7 %collective-permute-start.3 = (bf16[2,2,32,1536]{3,2,1,0:T(8,128)(2,1)S(1)}, bf16[2,2,32,1536]{3,2,1,0:T(8,128)(2,1)S(1)}, u32[]{:S(2)}, u32[]{:S(2)}) collective-permute-start(bf16[2,2,32,1536]{3,2,1,0:T(8,128)(2,1)S(1)} %get-tuple-element.28), channel_id=1, source_target_pairs={{0,8},{2,10},{4,12},{6,14},{8,16},{10,18},{12,20},{14,22},{16,24},... | collective-permute-start | bytes 1179656 | tf_op jit(solution)/shard_map/ppermute | solution.py:451
  5.6 19.0 %collective-permute-start.4 = (bf16[2,2,32,1536]{3,2,1,0:T(8,128)(2,1)S(1)}, bf16[2,2,32,1536]{3,2,1,0:T(8,128)(2,1)S(1)}, u32[]{:S(2)}, u32[]{:S(2)}) collective-permute-start(bf16[2,2,32,1536]{3,2,1,0:T(8,128)(2,1)S(1)} %get-tuple-element.29), channel_id=1, source_target_pairs={{0,24},{2,26},{4,28},{6,30},{8,0},{10,2},{12,4},{14,6},{16,8},{18,... | collective-permute-start | bytes 1179656 | tf_op jit(solution)/shard_map/ppermute | solution.py:451
  9.1 7.8 %collective-permute-start = (bf16[1,2,2,32,768]{4,3,2,1,0:T(8,128)(2,1)S(1)}, bf16[1,2,2,32,768]{4,3,2,1,0:T(8,128)(2,1)S(1)}, u32[]{:S(2)}, u32[]{:S(2)}) collective-permute-start(bf16[1,2,2,32,768]{4,3,2,1,0:T(8,128)(2,1)S(1)} %get-tuple-element.25), channel_id=1, source_target_pairs={{0,2},{2,0},{4,6},{6,4},{8,10},{10,8},{12,14},{14,12},{16,18},{18,... | collective-permute-start | bytes 589832 | tf_op jit(solution)/shard_map/ppermute | solution.py:443
  10.7 10.1 %collective-permute-start.1 = (bf16[1,2,2,32,768]{4,3,2,1,0:T(8,128)(2,1)S(1)}, bf16[1,2,2,32,768]{4,3,2,1,0:T(8,128)(2,1)S(1)}, u32[]{:S(2)}, u32[]{:S(2)}) collective-permute-start(bf16[1,2,2,32,768]{4,3,2,1,0:T(8,128)(2,1)S(1)} %get-tuple-element.26), channel_id=1, source_target_pairs={{0,4},{2,6},{4,0},{6,2},{8,12},{10,14},{12,8},{14,10},{16,20},{18,... | collective-permute-start | bytes 589832 | tf_op jit(solution)/shard_map/ppermute | solution.py:443
  12.3 9.3 %collective-permute-start.2 = (bf16[1,2,2,32,768]{4,3,2,1,0:T(8,128)(2,1)S(1)}, bf16[1,2,2,32,768]{4,3,2,1,0:T(8,128)(2,1)S(1)}, u32[]{:S(2)}, u32[]{:S(2)}) collective-permute-start(bf16[1,2,2,32,768]{4,3,2,1,0:T(8,128)(2,1)S(1)} %get-tuple-element.27), channel_id=1, source_target_pairs={{0,6},{2,4},{4,2},{6,0},{8,14},{10,12},{12,10},{14,8},{16,22},{18,... | collective-permute-start | bytes 589832 | tf_op jit(solution)/shard_map/ppermute | solution.py:443
  16.9 0.7 copy-start.5
  17.6 24.4 %collective-permute-start.6 = (bf16[2,2,32,1536]{3,2,1,0:T(8,128)(2,1)}, bf16[2,2,32,1536]{3,2,1,0:T(8,128)(2,1)S(1)}, u32[]{:S(2)}, u32[]{:S(2)}) collective-permute-start(bf16[2,2,32,1536]{3,2,1,0:T(8,128)(2,1)} %get-tuple-element.36), channel_id=1, source_target_pairs={{0,16},{2,18},{4,20},{6,22},{8,24},{10,26},{12,28},{14,30},{16,0},... | collective-permute-start | bytes 1179656 | tf_op jit(solution)/shard_map/ppermute | solution.py:451
  20.9 0.7 copy-start.7
  21.6 0.7 copy-start.9
  26.3 15.8 %collective-permute-start.5 = (bf16[2,2,2,32,768]{4,3,2,1,0:T(8,128)(2,1)}, bf16[2,2,2,32,768]{4,3,2,1,0:T(8,128)(2,1)}, u32[]{:S(2)}, u32[]{:S(2)}) collective-permute-start(bf16[2,2,2,32,768]{4,3,2,1,0:T(8,128)(2,1)} %get-tuple-element.35), channel_id=1, source_target_pairs={{0,2},{2,0},{4,6},{6,4},{8,10},{10,8},{12,14},{14,12},{16,18},{18,... | collective-permute-start | bytes 1179656 | tf_op jit(solution)/shard_map/ppermute | solution.py:443
  27.8 24.8 %collective-permute-start.7 = (bf16[2,2,2,32,768]{4,3,2,1,0:T(8,128)(2,1)}, bf16[2,2,2,32,768]{4,3,2,1,0:T(8,128)(2,1)}, u32[]{:S(2)}, u32[]{:S(2)}) collective-permute-start(bf16[2,2,2,32,768]{4,3,2,1,0:T(8,128)(2,1)} %get-tuple-element.38), channel_id=1, source_target_pairs={{0,4},{2,6},{4,0},{6,2},{8,12},{10,14},{12,8},{14,10},{16,20},{18,... | collective-permute-start | bytes 1179656 | tf_op jit(solution)/shard_map/ppermute | solution.py:443
  29.3 23.2 %collective-permute-start.8 = (bf16[2,2,2,32,768]{4,3,2,1,0:T(8,128)(2,1)}, bf16[2,2,2,32,768]{4,3,2,1,0:T(8,128)(2,1)}, u32[]{:S(2)}, u32[]{:S(2)}) collective-permute-start(bf16[2,2,2,32,768]{4,3,2,1,0:T(8,128)(2,1)} %get-tuple-element.39), channel_id=1, source_target_pairs={{0,6},{2,4},{4,2},{6,0},{8,14},{10,12},{12,10},{14,8},{16,22},{18,... | collective-permute-start | bytes 1179656 | tf_op jit(solution)/shard_map/ppermute | solution.py:443
  42.7 12.3 %collective-permute-start.10 = (bf16[1,2,2,32,768]{4,3,2,1,0:T(8,128)(2,1)S(1)}, bf16[1,2,2,32,768]{4,3,2,1,0:T(8,128)(2,1)S(1)}, u32[]{:S(2)}, u32[]{:S(2)}) collective-permute-start(bf16[1,2,2,32,768]{4,3,2,1,0:T(8,128)(2,1)S(1)} %get-tuple-element.42), channel_id=1, source_target_pairs={{0,4},{2,6},{4,0},{6,2},{8,12},{10,14},{12,8},{14,10},{16,20},{18,... | collective-permute-start | bytes 589832 | tf_op jit(solution)/shard_map/ppermute | solution.py:443
  44.2 10.7 %collective-permute-start.11 = (bf16[1,2,2,32,768]{4,3,2,1,0:T(8,128)(2,1)S(1)}, bf16[1,2,2,32,768]{4,3,2,1,0:T(8,128)(2,1)S(1)}, u32[]{:S(2)}, u32[]{:S(2)}) collective-permute-start(bf16[1,2,2,32,768]{4,3,2,1,0:T(8,128)(2,1)S(1)} %get-tuple-element.43), channel_id=1, source_target_pairs={{0,6},{2,4},{4,2},{6,0},{8,14},{10,12},{12,10},{14,8},{16,22},{18,... | collective-permute-start | bytes 589832 | tf_op jit(solution)/shard_map/ppermute | solution.py:443
  45.7 9.4 %collective-permute-start.9 = (bf16[1,2,2,32,768]{4,3,2,1,0:T(8,128)(2,1)S(1)}, bf16[1,2,2,32,768]{4,3,2,1,0:T(8,128)(2,1)S(1)}, u32[]{:S(2)}, u32[]{:S(2)}) collective-permute-start(bf16[1,2,2,32,768]{4,3,2,1,0:T(8,128)(2,1)S(1)} %get-tuple-element.41), channel_id=1, source_target_pairs={{0,2},{2,0},{4,6},{6,4},{8,10},{10,8},{12,14},{14,12},{16,18},{18,... | collective-permute-start | bytes 589832 | tf_op jit(solution)/shard_map/ppermute | solution.py:443
  47.8 1.6 %copy-start = (bf16[12,512,256]{2,1,0:T(8,128)(2,1)}, bf16[12,512,256]{2,1,0:T(8,128)(2,1)S(1)}, u32[]{:S(2)}) copy-start(bf16[12,512,256]{2,1,0:T(8,128)(2,1)S(1)} %build_angle.2.refs_14_) | copy-start | bytes 9437188
  49.5 1.3 %copy-start.14 = (s32[1,3,4]{2,0,1:T(1,128)S(1)}, s32[1,3,4]{2,0,1:T(1,128)}, u32[]{:S(2)}) copy-start(s32[1,3,4]{2,0,1:T(1,128)} %param.10) | copy-start | bytes 148
  49.5 1.3 %copy-start.11 = (bf16[1,3,2,16,512]{4,3,2,1,0:T(8,128)(2,1)S(1)}, bf16[1,3,2,16,512]{4,3,2,1,0:T(8,128)(2,1)}, u32[]{:S(2)}) copy-start(bf16[1,3,2,16,512]{4,3,2,1,0:T(8,128)(2,1)} %param.11) | copy-start | bytes 294916
  49.5 1.3 %copy-start.12 = (s32[1,3,512]{2,0,1:T(1,128)S(1)}, s32[1,3,512]{2,0,1:T(1,128)}, u32[]{:S(2)}) copy-start(s32[1,3,512]{2,0,1:T(1,128)} %param.9) | copy-start | bytes 18436
  49.5 5.6 %copy-start.2 = (bf16[2,2,32,4096]{3,2,1,0:T(8,128)(2,1)S(1)}, bf16[2,2,32,4096]{3,2,1,0:T(8,128)(2,1)}, u32[]{:S(2)}) copy-start(bf16[2,2,32,4096]{3,2,1,0:T(8,128)(2,1)} %refs_9_.1) | copy-start | bytes 3145732
  49.5 5.6 %copy-start.6 = (bf16[1,2,2,32,768]{4,3,2,1,0:T(8,128)(2,1)S(1)}, bf16[1,2,2,32,768]{4,3,2,1,0:T(8,128)(2,1)}, u32[]{:S(2)}) copy-start(bf16[1,2,2,32,768]{4,3,2,1,0:T(8,128)(2,1)} %copy-done.5) | copy-start | bytes 589828
  49.5 5.6 %copy-start.8 = (bf16[1,2,2,32,768]{4,3,2,1,0:T(8,128)(2,1)S(1)}, bf16[1,2,2,32,768]{4,3,2,1,0:T(8,128)(2,1)}, u32[]{:S(2)}) copy-start(bf16[1,2,2,32,768]{4,3,2,1,0:T(8,128)(2,1)} %copy-done.7) | copy-start | bytes 589828
  49.5 5.6 %copy-start.10 = (bf16[1,2,2,32,768]{4,3,2,1,0:T(8,128)(2,1)S(1)}, bf16[1,2,2,32,768]{4,3,2,1,0:T(8,128)(2,1)}, u32[]{:S(2)}) copy-start(bf16[1,2,2,32,768]{4,3,2,1,0:T(8,128)(2,1)} %copy-done.9) | copy-start | bytes 589828
  49.5 5.6 %copy-start.13 = (s32[1,256]{1,0:T(1,128)S(1)}, s32[1,256]{1,0:T(1,128)}, u32[]{:S(2)}) copy-start(s32[1,256]{1,0:T(1,128)} %ab_ref.1) | copy-start | bytes 3076
  63.6 2.9 %collective-permute-start.12 = (bf16[256,2048]{1,0:T(8,128)(2,1)}, bf16[256,2048]{1,0:T(8,128)(2,1)S(1)}, u32[]{:S(2)}, u32[]{:S(2)}) collective-permute-start(bf16[256,2048]{1,0:T(8,128)(2,1)} %get-tuple-element.45), channel_id=1, source_target_pairs={{0,1},{1,0},{2,3},{3,2},{4,5},{5,4},{6,7},{7,6},{8,9},{9,8},{10,11... | collective-permute-start | bytes 3145736 | tf_op jit(solution)/shard_map/ppermute | solution.py:481

commit v5 on v4

--- a/solution.py
+++ b/solution.py
@@ -226,7 +226,7 @@
     def body(where_ref, rb_ref, ab_ref, *refs):
         ins = refs[:n_in]
         rm_hbm, am_hbm, a2_hbm, own_ref, send_ref = refs[n_in : n_in + 5]
-        x_ref, z_ref, y_ref, s_ref, rm_ref, am_ref, a2_ref, sem, wsem = refs[n_in + 5 :]
+        x_ref, z_ref, y_ref, s_ref, rm_ref, am_ref, a2_ref, sem, wsem, o_ref, osem = refs[n_in + 5 :]
         panel = where_ref[0]
         side = where_ref[1]
         plane = panel // cells
@@ -257,8 +257,6 @@
             load.start()
         for at in (1, 3, 2, 4):
             weights[at].start()
-        for load in loads:
-            load.wait()
         for member in range(members):
             for gi, group in enumerate(groups):
                 for at, step in enumerate(group):
@@ -266,6 +264,9 @@
                     for flip in range(1, cells):
                         rows = pl.ds(aligned(source + (cell ^ flip), plan.rows), plan.rows)
                         x_ref[member, :, rows, :] = ins[gi * flips + flip - 1][at, member]
+            if member == 0:
+                for load in loads:
+                    load.wait()
             weights[member].wait()
             range_step(
                 plan,
@@ -308,15 +309,27 @@
             mwidth,
         )
         weights[4].wait()
-        for which, ref in ((1 - side, send_ref), (side, own_ref)):
+        stores = []
+        for turn, (which, ref) in enumerate(((1 - side, send_ref), (side, own_ref))):
             for j in range(plan.out_blocks):
                 place = 4 * plan.in_blocks + panel * plan.out_blocks + j
                 columns = pl.ds(aligned(ab_ref[0, place] - first, PAIR), 2 * PAIR)
-                ref[:, j * PAIR : (j + 1) * PAIR] = jnp.dot(
+                out = slice(j * PAIR, (j + 1) * PAIR)
+                o_ref[turn, :, out] = jnp.dot(
                     s_ref[pl.ds(aligned(which, half), half), columns],
                     a2_ref[j],
                     preferred_element_type=F32,
                 ).astype(BF16)
+                if j % 4 == 3:
+                    four = slice((j - 3) * PAIR, (j + 1) * PAIR)
+                    stores.append(
+                        pltpu.make_async_copy(
+                            o_ref.at[turn, :, four], ref.at[:, four], osem.at[len(stores)]
+                        )
+                    )
+                    stores[-1].start()
+        for store in stores:
+            store.wait()
 
     shape = jax.ShapeDtypeStruct((half, plan.out_blocks * PAIR), BF16)
     rows = plan.total_rows
@@ -324,7 +337,7 @@
         body,
         out_shape=[shape, shape],
         in_specs=[SMEM, SMEM, SMEM] + [VMEM] * n_parts + [ANY] * (planes + 3),
-        out_specs=[VMEM, VMEM],
+        out_specs=[ANY, ANY],
         scratch_shapes=[
             pltpu.VMEM((members, 2, rows, width * TILE), BF16),
             pltpu.VMEM((members, rows, width * PAIR), BF16),
@@ -335,6 +348,8 @@
             pltpu.VMEM(last_mats.shape, BF16),
             pltpu.SemaphoreType.DMA((planes,)),
             pltpu.SemaphoreType.DMA((5,)),
+            pltpu.VMEM((2,) + shape.shape, BF16),
+            pltpu.SemaphoreType.DMA((plan.out_blocks // 2,)),
         ],
         compiler_params=params(),
         name="merge",

time: 81.3 us -> 81 us (level)
  no operation moved by 1% of the time
where the time goes in v5:
time: 81 us; the launch traced here: 80.8 us
  waiting for transfers between devices  26 us (32%)
  Pallas kernels  19.3 us (24%)
  starting transfers between devices  16.7 us (21%)
  blocking collectives  11.3 us (14%)
  local copies, waits for them, and re-layouts  5.73 us (7%)
  between operations  0.85 us (1%)
  other arithmetic  0.81 us (1%)
    ppermute x3, waiting for transfers between devices, shards(): lax.ppermute(far[step], 'panel', plane_shift(step))  14.7 us
    all_to_all x1, blocking collectives, shards(): lax.all_to_all(partials.reshape(2 * panels, GRP_DEV), ('aper', 'panel'),...  11.3 us
    ppermute x9, starting transfers between devices, across(): lax.ppermute(pieces[flip - 1], 'panel', cell_flip(flip))  10.5 us
    ppermute x9, waiting for transfers between devices, across(): lax.ppermute(pieces[flip - 1], 'panel', cell_flip(flip))  9.22 us
    pallas_call x1, Pallas kernels, merge(): pl.pallas_call(body, out_shape=[shape, shape], in_specs=[SMEM, SMEM, SMEM...  8.24 us
    ppermute x3, starting transfers between devices, shards(): lax.ppermute(far[step], 'panel', plane_shift(step))  6.13 us
    unnamed x31, local copies, waits for them, and re-layouts  4.95 us
    pallas_call x2, Pallas kernels, build_angle(): pl.pallas_call(body, out_shape=jax.ShapeDtypeStruct((count, 2 * PAIR, PAI...  2.73 us
  transfers between devices with their start and end apart: 13, of which 7 were waited for; matrix products, arithmetic and copies ran while one was open for 1% of the time, Pallas kernels for 10%

profile of v5, /device:TPU:0, one launch (start us, length us, event | category | flops | bytes accessed | tf_op | source)
XLA Modules:
  0.0 80.8 jit_solution(14033896222726830575)
XLA Ops:
  0.7 1.2 %copy-done.1 = bf16[2,2,32,4096]{3,2,1,0:T(8,128)(2,1)S(1)} copy-done((bf16[2,2,32,4096]{3,2,1,0:T(8,128)(2,1)S(1)}, bf16[2,2,32,4096]{3,2,1,0:T(8,128)(2,1)}, u32[]{:S(2)}) %copy-start.1) | copy-done | bytes 1048600
  1.9 0.6 pack_own.3
  2.6 3.1 %collective-permute-start.3 = (bf16[2,2,32,1536]{3,2,1,0:T(8,128)(2,1)S(1)}, bf16[2,2,32,1536]{3,2,1,0:T(8,128)(2,1)S(1)}, u32[]{:S(2)}, u32[]{:S(2)}) collective-permute-start(bf16[2,2,32,1536]{3,2,1,0:T(8,128)(2,1)S(1)} %get-tuple-element.28), channel_id=1, source_target_pairs={{0,8},{2,10},{4,12},{6,14},{8,16},{10,18},{12,20},{14,22},{16,24},... | collective-permute-start | bytes 1179656 | tf_op jit(solution)/shard_map/ppermute | solution.py:466
  5.6 2.1 %collective-permute-start.4 = (bf16[2,2,32,1536]{3,2,1,0:T(8,128)(2,1)S(1)}, bf16[2,2,32,1536]{3,2,1,0:T(8,128)(2,1)S(1)}, u32[]{:S(2)}, u32[]{:S(2)}) collective-permute-start(bf16[2,2,32,1536]{3,2,1,0:T(8,128)(2,1)S(1)} %get-tuple-element.29), channel_id=1, source_target_pairs={{0,24},{2,26},{4,28},{6,30},{8,0},{10,2},{12,4},{14,6},{16,8},{18,... | collective-permute-start | bytes 1179656 | tf_op jit(solution)/shard_map/ppermute | solution.py:466
  7.7 1.4 %pack_own.2 = (bf16[2,2,32,1536]{3,2,1,0:T(8,128)(2,1)}, bf16[1,2,2,32,768]{4,3,2,1,0:T(8,128)(2,1)S(1)}, bf16[1,2,2,32,768]{4,3,2,1,0:T(8,128)(2,1)S(1)}, bf16[1,2,2,32,768]{4,3,2,1,0:T(8,128)(2,1)S(1)}) custom-call(s32[2]{0:T(128)S(1)} %pad_add_fusion.where_ref, bf16[2,2,32,4096]{3,2,1,0:T(8,128)(2,1)S(1)} %copy-done.1), custom_call_target="tpu_custom_call" | custom-call | tf_op jit(solution)/shard_map/pack_own/pallas_call | solution.py:80
  9.1 1.6 %collective-permute-start = (bf16[1,2,2,32,768]{4,3,2,1,0:T(8,128)(2,1)S(1)}, bf16[1,2,2,32,768]{4,3,2,1,0:T(8,128)(2,1)S(1)}, u32[]{:S(2)}, u32[]{:S(2)}) collective-permute-start(bf16[1,2,2,32,768]{4,3,2,1,0:T(8,128)(2,1)S(1)} %get-tuple-element.25), channel_id=1, source_target_pairs={{0,2},{2,0},{4,6},{6,4},{8,10},{10,8},{12,14},{14,12},{16,18},{18,... | collective-permute-start | bytes 589832 | tf_op jit(solution)/shard_map/ppermute | solution.py:458
  10.7 1.5 %collective-permute-start.1 = (bf16[1,2,2,32,768]{4,3,2,1,0:T(8,128)(2,1)S(1)}, bf16[1,2,2,32,768]{4,3,2,1,0:T(8,128)(2,1)S(1)}, u32[]{:S(2)}, u32[]{:S(2)}) collective-permute-start(bf16[1,2,2,32,768]{4,3,2,1,0:T(8,128)(2,1)S(1)} %get-tuple-element.26), channel_id=1, source_target_pairs={{0,4},{2,6},{4,0},{6,2},{8,12},{10,14},{12,8},{14,10},{16,20},{18,... | collective-permute-start | bytes 589832 | tf_op jit(solution)/shard_map/ppermute | solution.py:458
  12.6 4.3 %collective-permute-done.refs_0_ = bf16[1,2,2,32,768]{4,3,2,1,0:T(8,128)(2,1)S(1)} collective-permute-done((bf16[1,2,2,32,768]{4,3,2,1,0:T(8,128)(2,1)S(1)}, bf16[1,2,2,32,768]{4,3,2,1,0:T(8,128)(2,1)S(1)}, u32[]{:S(2)}, u32[]{:S(2)}) %collective-permute-start) | collective-permute-done | bytes 196640 | tf_op jit(solution)/shard_map/ppermute | solution.py:458
  16.9 0.7 copy-done.5
  17.6 1.0 %collective-permute-start.6 = (bf16[2,2,32,1536]{3,2,1,0:T(8,128)(2,1)}, bf16[2,2,32,1536]{3,2,1,0:T(8,128)(2,1)S(1)}, u32[]{:S(2)}, u32[]{:S(2)}) collective-permute-start(bf16[2,2,32,1536]{3,2,1,0:T(8,128)(2,1)} %get-tuple-element.36), channel_id=1, source_target_pairs={{0,16},{2,18},{4,20},{6,22},{8,24},{10,26},{12,28},{14,30},{16,0},... | collective-permute-start | bytes 1179656 | tf_op jit(solution)/shard_map/ppermute | solution.py:466
  18.6 2.3 %collective-permute-done.1.refs_1_ = bf16[1,2,2,32,768]{4,3,2,1,0:T(8,128)(2,1)S(1)} collective-permute-done((bf16[1,2,2,32,768]{4,3,2,1,0:T(8,128)(2,1)S(1)}, bf16[1,2,2,32,768]{4,3,2,1,0:T(8,128)(2,1)S(1)}, u32[]{:S(2)}, u32[]{:S(2)}) %collective-permute-start.1) | collective-permute-done | bytes 196640 | tf_op jit(solution)/shard_map/ppermute | solution.py:458
  20.9 0.7 copy-done.7
  21.6 0.7 copy-done.9
  22.3 2.4 %collective-permute-done.4.refs_1_.refs_12_ = bf16[2,2,32,1536]{3,2,1,0:T(8,128)(2,1)S(1)} collective-permute-done((bf16[2,2,32,1536]{3,2,1,0:T(8,128)(2,1)S(1)}, bf16[2,2,32,1536]{3,2,1,0:T(8,128)(2,1)S(1)}, u32[]{:S(2)}, u32[]{:S(2)}) %collective-permute-start.4) | collective-permute-done | bytes 393248 | tf_op jit(solution)/shard_map/ppermute | solution.py:466
  24.6 1.6 %pack_panels.2 = (bf16[2,2,2,32,768]{4,3,2,1,0:T(8,128)(2,1)}, bf16[2,2,2,32,768]{4,3,2,1,0:T(8,128)(2,1)}, bf16[2,2,2,32,768]{4,3,2,1,0:T(8,128)(2,1)}) custom-call(s32[2]{0:T(128)S(1)} %pad_add_fusion.where_ref, bf16[2,2,32,1536]{3,2,1,0:T(8,128)(2,1)S(1)} %collective-permute-done.3.refs_0_.refs_10_, ...), custom_call_target="tpu_custom_call" | custom-call | tf_op jit(solution)/shard_map/pack_panels/pallas_call | solution.py:110
  26.3 1.5 %collective-permute-start.5 = (bf16[2,2,2,32,768]{4,3,2,1,0:T(8,128)(2,1)}, bf16[2,2,2,32,768]{4,3,2,1,0:T(8,128)(2,1)}, u32[]{:S(2)}, u32[]{:S(2)}) collective-permute-start(bf16[2,2,2,32,768]{4,3,2,1,0:T(8,128)(2,1)} %get-tuple-element.35), channel_id=1, source_target_pairs={{0,2},{2,0},{4,6},{6,4},{8,10},{10,8},{12,14},{14,12},{16,18},{18,... | collective-permute-start | bytes 1179656 | tf_op jit(solution)/shard_map/ppermute | solution.py:458
  27.8 1.5 %collective-permute-start.7 = (bf16[2,2,2,32,768]{4,3,2,1,0:T(8,128)(2,1)}, bf16[2,2,2,32,768]{4,3,2,1,0:T(8,128)(2,1)}, u32[]{:S(2)}, u32[]{:S(2)}) collective-permute-start(bf16[2,2,2,32,768]{4,3,2,1,0:T(8,128)(2,1)} %get-tuple-element.38), channel_id=1, source_target_pairs={{0,4},{2,6},{4,0},{6,2},{8,12},{10,14},{12,8},{14,10},{16,20},{18,... | collective-permute-start | bytes 1179656 | tf_op jit(solution)/shard_map/ppermute | solution.py:458
  29.8 12.3 %collective-permute-done.6.refs_0_.refs_11_ = bf16[2,2,32,1536]{3,2,1,0:T(8,128)(2,1)S(1)} collective-permute-done((bf16[2,2,32,1536]{3,2,1,0:T(8,128)(2,1)}, bf16[2,2,32,1536]{3,2,1,0:T(8,128)(2,1)S(1)}, u32[]{:S(2)}, u32[]{:S(2)}) %collective-permute-start.6) | collective-permute-done | bytes 393248 | tf_op jit(solution)/shard_map/ppermute | solution.py:466
  42.1 0.6 pack_panels.3
  42.7 1.6 %collective-permute-start.10 = (bf16[1,2,2,32,768]{4,3,2,1,0:T(8,128)(2,1)S(1)}, bf16[1,2,2,32,768]{4,3,2,1,0:T(8,128)(2,1)S(1)}, u32[]{:S(2)}, u32[]{:S(2)}) collective-permute-start(bf16[1,2,2,32,768]{4,3,2,1,0:T(8,128)(2,1)S(1)} %get-tuple-element.42), channel_id=1, source_target_pairs={{0,4},{2,6},{4,0},{6,2},{8,12},{10,14},{12,8},{14,10},{16,20},{18,... | collective-permute-start | bytes 589832 | tf_op jit(solution)/shard_map/ppermute | solution.py:458
  44.2 1.4 %collective-permute-start.11 = (bf16[1,2,2,32,768]{4,3,2,1,0:T(8,128)(2,1)S(1)}, bf16[1,2,2,32,768]{4,3,2,1,0:T(8,128)(2,1)S(1)}, u32[]{:S(2)}, u32[]{:S(2)}) collective-permute-start(bf16[1,2,2,32,768]{4,3,2,1,0:T(8,128)(2,1)S(1)} %get-tuple-element.43), channel_id=1, source_target_pairs={{0,6},{2,4},{4,2},{6,0},{8,14},{10,12},{12,10},{14,8},{16,22},{18,... | collective-permute-start | bytes 589832 | tf_op jit(solution)/shard_map/ppermute | solution.py:458
  46.3 1.5 %build_angle.2.refs_14_ = bf16[12,512,256]{2,1,0:T(8,128)(2,1)S(1)} custom-call(s32[12]{0:T(128)S(1)} %pad_add_fusion.1.blocks_ref, s32[1,32768]{1,0:T(1,128)S(1)} %copy-done.4, bf16[2,16,32768]{2,1,0:T(8,128)(2,1)S(1)} %bitcast.11), custom_call_target="tpu_custom_call" | custom-call | tf_op jit(solution)/shard_map/build_angle/pallas_call | solution.py:153
  47.8 1.6 %copy-done = bf16[12,512,256]{2,1,0:T(8,128)(2,1)} copy-done((bf16[12,512,256]{2,1,0:T(8,128)(2,1)}, bf16[12,512,256]{2,1,0:T(8,128)(2,1)S(1)}, u32[]{:S(2)}) %copy-start) | copy-done | bytes 3145752
  49.5 1.2 %build_angle.3.refs_15_ = bf16[8,512,256]{2,1,0:T(8,128)(2,1)S(1)} custom-call(s32[8]{0:T(128)S(1)} %iota_add_fusion.blocks_ref, s32[1,32768]{1,0:T(1,128)S(1)} %copy-done.4, bf16[2,16,32768]{2,1,0:T(8,128)(2,1)S(1)} %bitcast.12), custom_call_target="tpu_custom_call" | custom-call | tf_op jit(solution)/shard_map/build_angle/pallas_call | solution.py:153
  50.8 1.7 %build_range.1.refs_13_ = bf16[3,4,256,256]{3,2,1,0:T(8,128)(2,1)S(1)} custom-call(s32[3,1,512]{2,1,0:T(1,128)S(1)} %bitcast.16, bf16[3,2,16,512]{3,2,1,0:T(8,128)(2,1)S(1)} %bitcast.13), custom_call_target="tpu_custom_call" | custom-call | tf_op jit(solution)/shard_map/build_range/pallas_call | solution.py:180
  52.5 2.4 %collective-permute-done.10.refs_7_ = bf16[1,2,2,32,768]{4,3,2,1,0:T(8,128)(2,1)S(1)} collective-permute-done((bf16[1,2,2,32,768]{4,3,2,1,0:T(8,128)(2,1)S(1)}, bf16[1,2,2,32,768]{4,3,2,1,0:T(8,128)(2,1)S(1)}, u32[]{:S(2)}, u32[]{:S(2)}) %collective-permute-start.10) | collective-permute-done | bytes 196640 | tf_op jit(solution)/shard_map/ppermute | solution.py:458
  55.1 8.2 %merge.1 = (bf16[256,2048]{1,0:T(8,128)(2,1)S(1)}, bf16[256,2048]{1,0:T(8,128)(2,1)}) custom-call(s32[2]{0:T(128)S(1)} %pad_add_fusion.where_ref, s32[3,4]{1,0:T(4,128)S(1)} %bitcast.15, s32[1,256]{1,0:T(1,128)S(1)} %copy-done.13, bf16[1,2,2,32,768]{4,3,2,1,0:T(8,128)(2,1)S(1)} %copy-done.6, bf16[1,2,2,32,768]{4,3,2,1,0:T(8,128)(2,1)S(1)} %copy-done.8, ...), custom_call_target="tpu_custom_call" | custom-call | tf_op jit(solution)/shard_map/merge/pallas_call | solution.py:336
  63.5 0.7 dynamic-slice.3
  64.2 2.2 %collective-permute-done.12.oth_ref = bf16[256,2048]{1,0:T(8,128)(2,1)S(1)} collective-permute-done((bf16[256,2048]{1,0:T(8,128)(2,1)}, bf16[256,2048]{1,0:T(8,128)(2,1)S(1)}, u32[]{:S(2)}, u32[]{:S(2)}) %collective-permute-start.12) | collective-permute-done | bytes 1048608 | tf_op jit(solution)/shard_map/ppermute | solution.py:496
  66.3 2.4 %focus.1 = (bf16[2,256,1024]{2,1,0:T(8,128)(2,1)}, f32[2,64,1]{2,1,0:T(8,128)S(1)}) custom-call(s32[2]{0:T(128)S(1)} %pad_add_fusion.where_ref, bf16[256,2048]{1,0:T(8,128)(2,1)S(1)} %get-tuple-element.44.own_ref, bf16[256,2048]{1,0:T(8,128)(2,1)S(1)} %collective-permute-done.12.oth_ref, s32[1,1024]{1,0:T(1,128)S(1)} %bitcast.14), custom_call_target="tpu_custom_call" | custom-call | tf_op jit(solution)/shard_map/focus/pallas_call | solution.py:412
  68.9 11.3 %all_to_all.9 = f32[32,1,4]{2,1,0:T(1,128)S(1)} all-to-all(f32[32,1,4]{2,1,0:T(1,128)S(1)} %bitcast.17), channel_id=1, replica_groups=mesh['scene'=1,'panel'=16,'aper'=2] {'aper','panel'}, dimensions={0} | all-to-all | bytes 1024 | tf_op jit(solution)/shard_map/all_to_all | solution.py:500
  80.2 0.6 reduce_sum.9
  (43 shorter events, 1.9 us)
Async XLA Ops:
  0.7 1.2 %copy-start.1 = (bf16[2,2,32,4096]{3,2,1,0:T(8,128)(2,1)S(1)}, bf16[2,2,32,4096]{3,2,1,0:T(8,128)(2,1)}, u32[]{:S(2)}) copy-start(bf16[2,2,32,4096]{3,2,1,0:T(8,128)(2,1)} %refs_9_.1) | copy-start | bytes 3145732
  1.9 44.4 %copy-start.3 = (bf16[1,2,16,32768]{3,2,1,0:T(8,128)(2,1)S(1)}, bf16[1,2,16,32768]{3,2,1,0:T(8,128)(2,1)}, u32[]{:S(2)}) copy-start(bf16[1,2,16,32768]{3,2,1,0:T(8,128)(2,1)} %param.14) | copy-start | bytes 6291460
  1.9 44.4 %copy-start.4 = (s32[1,32768]{1,0:T(1,128)S(1)}, s32[1,32768]{1,0:T(1,128)}, u32[]{:S(2)}) copy-start(s32[1,32768]{1,0:T(1,128)} %taps_ref.3) | copy-start | bytes 393220
  2.6 19.7 %collective-permute-start.3 = (bf16[2,2,32,1536]{3,2,1,0:T(8,128)(2,1)S(1)}, bf16[2,2,32,1536]{3,2,1,0:T(8,128)(2,1)S(1)}, u32[]{:S(2)}, u32[]{:S(2)}) collective-permute-start(bf16[2,2,32,1536]{3,2,1,0:T(8,128)(2,1)S(1)} %get-tuple-element.28), channel_id=1, source_target_pairs={{0,8},{2,10},{4,12},{6,14},{8,16},{10,18},{12,20},{14,22},{16,24},... | collective-permute-start | bytes 1179656 | tf_op jit(solution)/shard_map/ppermute | solution.py:466
  5.6 19.0 %collective-permute-start.4 = (bf16[2,2,32,1536]{3,2,1,0:T(8,128)(2,1)S(1)}, bf16[2,2,32,1536]{3,2,1,0:T(8,128)(2,1)S(1)}, u32[]{:S(2)}, u32[]{:S(2)}) collective-permute-start(bf16[2,2,32,1536]{3,2,1,0:T(8,128)(2,1)S(1)} %get-tuple-element.29), channel_id=1, source_target_pairs={{0,24},{2,26},{4,28},{6,30},{8,0},{10,2},{12,4},{14,6},{16,8},{18,... | collective-permute-start | bytes 1179656 | tf_op jit(solution)/shard_map/ppermute | solution.py:466
  9.1 7.8 %collective-permute-start = (bf16[1,2,2,32,768]{4,3,2,1,0:T(8,128)(2,1)S(1)}, bf16[1,2,2,32,768]{4,3,2,1,0:T(8,128)(2,1)S(1)}, u32[]{:S(2)}, u32[]{:S(2)}) collective-permute-start(bf16[1,2,2,32,768]{4,3,2,1,0:T(8,128)(2,1)S(1)} %get-tuple-element.25), channel_id=1, source_target_pairs={{0,2},{2,0},{4,6},{6,4},{8,10},{10,8},{12,14},{14,12},{16,18},{18,... | collective-permute-start | bytes 589832 | tf_op jit(solution)/shard_map/ppermute | solution.py:458
  10.7 10.1 %collective-permute-start.1 = (bf16[1,2,2,32,768]{4,3,2,1,0:T(8,128)(2,1)S(1)}, bf16[1,2,2,32,768]{4,3,2,1,0:T(8,128)(2,1)S(1)}, u32[]{:S(2)}, u32[]{:S(2)}) collective-permute-start(bf16[1,2,2,32,768]{4,3,2,1,0:T(8,128)(2,1)S(1)} %get-tuple-element.26), channel_id=1, source_target_pairs={{0,4},{2,6},{4,0},{6,2},{8,12},{10,14},{12,8},{14,10},{16,20},{18,... | collective-permute-start | bytes 589832 | tf_op jit(solution)/shard_map/ppermute | solution.py:458
  12.3 9.3 %collective-permute-start.2 = (bf16[1,2,2,32,768]{4,3,2,1,0:T(8,128)(2,1)S(1)}, bf16[1,2,2,32,768]{4,3,2,1,0:T(8,128)(2,1)S(1)}, u32[]{:S(2)}, u32[]{:S(2)}) collective-permute-start(bf16[1,2,2,32,768]{4,3,2,1,0:T(8,128)(2,1)S(1)} %get-tuple-element.27), channel_id=1, source_target_pairs={{0,6},{2,4},{4,2},{6,0},{8,14},{10,12},{12,10},{14,8},{16,22},{18,... | collective-permute-start | bytes 589832 | tf_op jit(solution)/shard_map/ppermute | solution.py:458
  16.9 0.7 copy-start.5
  17.6 24.4 %collective-permute-start.6 = (bf16[2,2,32,1536]{3,2,1,0:T(8,128)(2,1)}, bf16[2,2,32,1536]{3,2,1,0:T(8,128)(2,1)S(1)}, u32[]{:S(2)}, u32[]{:S(2)}) collective-permute-start(bf16[2,2,32,1536]{3,2,1,0:T(8,128)(2,1)} %get-tuple-element.36), channel_id=1, source_target_pairs={{0,16},{2,18},{4,20},{6,22},{8,24},{10,26},{12,28},{14,30},{16,0},... | collective-permute-start | bytes 1179656 | tf_op jit(solution)/shard_map/ppermute | solution.py:466
  20.9 0.7 copy-start.7
  21.6 0.7 copy-start.9
  26.3 15.8 %collective-permute-start.5 = (bf16[2,2,2,32,768]{4,3,2,1,0:T(8,128)(2,1)}, bf16[2,2,2,32,768]{4,3,2,1,0:T(8,128)(2,1)}, u32[]{:S(2)}, u32[]{:S(2)}) collective-permute-start(bf16[2,2,2,32,768]{4,3,2,1,0:T(8,128)(2,1)} %get-tuple-element.35), channel_id=1, source_target_pairs={{0,2},{2,0},{4,6},{6,4},{8,10},{10,8},{12,14},{14,12},{16,18},{18,... | collective-permute-start | bytes 1179656 | tf_op jit(solution)/shard_map/ppermute | solution.py:458
  27.8 24.8 %collective-permute-start.7 = (bf16[2,2,2,32,768]{4,3,2,1,0:T(8,128)(2,1)}, bf16[2,2,2,32,768]{4,3,2,1,0:T(8,128)(2,1)}, u32[]{:S(2)}, u32[]{:S(2)}) collective-permute-start(bf16[2,2,2,32,768]{4,3,2,1,0:T(8,128)(2,1)} %get-tuple-element.38), channel_id=1, source_target_pairs={{0,4},{2,6},{4,0},{6,2},{8,12},{10,14},{12,8},{14,10},{16,20},{18,... | collective-permute-start | bytes 1179656 | tf_op jit(solution)/shard_map/ppermute | solution.py:458
  29.3 23.2 %collective-permute-start.8 = (bf16[2,2,2,32,768]{4,3,2,1,0:T(8,128)(2,1)}, bf16[2,2,2,32,768]{4,3,2,1,0:T(8,128)(2,1)}, u32[]{:S(2)}, u32[]{:S(2)}) collective-permute-start(bf16[2,2,2,32,768]{4,3,2,1,0:T(8,128)(2,1)} %get-tuple-element.39), channel_id=1, source_target_pairs={{0,6},{2,4},{4,2},{6,0},{8,14},{10,12},{12,10},{14,8},{16,22},{18,... | collective-permute-start | bytes 1179656 | tf_op jit(solution)/shard_map/ppermute | solution.py:458
  42.7 12.3 %collective-permute-start.10 = (bf16[1,2,2,32,768]{4,3,2,1,0:T(8,128)(2,1)S(1)}, bf16[1,2,2,32,768]{4,3,2,1,0:T(8,128)(2,1)S(1)}, u32[]{:S(2)}, u32[]{:S(2)}) collective-permute-start(bf16[1,2,2,32,768]{4,3,2,1,0:T(8,128)(2,1)S(1)} %get-tuple-element.42), channel_id=1, source_target_pairs={{0,4},{2,6},{4,0},{6,2},{8,12},{10,14},{12,8},{14,10},{16,20},{18,... | collective-permute-start | bytes 589832 | tf_op jit(solution)/shard_map/ppermute | solution.py:458
  44.2 10.7 %collective-permute-start.11 = (bf16[1,2,2,32,768]{4,3,2,1,0:T(8,128)(2,1)S(1)}, bf16[1,2,2,32,768]{4,3,2,1,0:T(8,128)(2,1)S(1)}, u32[]{:S(2)}, u32[]{:S(2)}) collective-permute-start(bf16[1,2,2,32,768]{4,3,2,1,0:T(8,128)(2,1)S(1)} %get-tuple-element.43), channel_id=1, source_target_pairs={{0,6},{2,4},{4,2},{6,0},{8,14},{10,12},{12,10},{14,8},{16,22},{18,... | collective-permute-start | bytes 589832 | tf_op jit(solution)/shard_map/ppermute | solution.py:458
  45.7 9.4 %collective-permute-start.9 = (bf16[1,2,2,32,768]{4,3,2,1,0:T(8,128)(2,1)S(1)}, bf16[1,2,2,32,768]{4,3,2,1,0:T(8,128)(2,1)S(1)}, u32[]{:S(2)}, u32[]{:S(2)}) collective-permute-start(bf16[1,2,2,32,768]{4,3,2,1,0:T(8,128)(2,1)S(1)} %get-tuple-element.41), channel_id=1, source_target_pairs={{0,2},{2,0},{4,6},{6,4},{8,10},{10,8},{12,14},{14,12},{16,18},{18,... | collective-permute-start | bytes 589832 | tf_op jit(solution)/shard_map/ppermute | solution.py:458
  47.8 1.6 %copy-start = (bf16[12,512,256]{2,1,0:T(8,128)(2,1)}, bf16[12,512,256]{2,1,0:T(8,128)(2,1)S(1)}, u32[]{:S(2)}) copy-start(bf16[12,512,256]{2,1,0:T(8,128)(2,1)S(1)} %build_angle.2.refs_14_) | copy-start | bytes 9437188
  49.5 1.3 %copy-start.14 = (s32[1,3,4]{2,0,1:T(1,128)S(1)}, s32[1,3,4]{2,0,1:T(1,128)}, u32[]{:S(2)}) copy-start(s32[1,3,4]{2,0,1:T(1,128)} %param.10) | copy-start | bytes 148
  49.5 1.3 %copy-start.11 = (bf16[1,3,2,16,512]{4,3,2,1,0:T(8,128)(2,1)S(1)}, bf16[1,3,2,16,512]{4,3,2,1,0:T(8,128)(2,1)}, u32[]{:S(2)}) copy-start(bf16[1,3,2,16,512]{4,3,2,1,0:T(8,128)(2,1)} %param.11) | copy-start | bytes 294916
  49.5 1.3 %copy-start.12 = (s32[1,3,512]{2,0,1:T(1,128)S(1)}, s32[1,3,512]{2,0,1:T(1,128)}, u32[]{:S(2)}) copy-start(s32[1,3,512]{2,0,1:T(1,128)} %param.9) | copy-start | bytes 18436
  49.5 5.6 %copy-start.2 = (bf16[2,2,32,4096]{3,2,1,0:T(8,128)(2,1)S(1)}, bf16[2,2,32,4096]{3,2,1,0:T(8,128)(2,1)}, u32[]{:S(2)}) copy-start(bf16[2,2,32,4096]{3,2,1,0:T(8,128)(2,1)} %refs_9_.1) | copy-start | bytes 3145732
  49.5 5.6 %copy-start.6 = (bf16[1,2,2,32,768]{4,3,2,1,0:T(8,128)(2,1)S(1)}, bf16[1,2,2,32,768]{4,3,2,1,0:T(8,128)(2,1)}, u32[]{:S(2)}) copy-start(bf16[1,2,2,32,768]{4,3,2,1,0:T(8,128)(2,1)} %copy-done.5) | copy-start | bytes 589828
  49.5 5.6 %copy-start.8 = (bf16[1,2,2,32,768]{4,3,2,1,0:T(8,128)(2,1)S(1)}, bf16[1,2,2,32,768]{4,3,2,1,0:T(8,128)(2,1)}, u32[]{:S(2)}) copy-start(bf16[1,2,2,32,768]{4,3,2,1,0:T(8,128)(2,1)} %copy-done.7) | copy-start | bytes 589828
  49.5 5.6 %copy-start.10 = (bf16[1,2,2,32,768]{4,3,2,1,0:T(8,128)(2,1)S(1)}, bf16[1,2,2,32,768]{4,3,2,1,0:T(8,128)(2,1)}, u32[]{:S(2)}) copy-start(bf16[1,2,2,32,768]{4,3,2,1,0:T(8,128)(2,1)} %copy-done.9) | copy-start | bytes 589828
  49.5 5.6 %copy-start.13 = (s32[1,256]{1,0:T(1,128)S(1)}, s32[1,256]{1,0:T(1,128)}, u32[]{:S(2)}) copy-start(s32[1,256]{1,0:T(1,128)} %ab_ref.1) | copy-start | bytes 3076
  63.4 2.9 %collective-permute-start.12 = (bf16[256,2048]{1,0:T(8,128)(2,1)}, bf16[256,2048]{1,0:T(8,128)(2,1)S(1)}, u32[]{:S(2)}, u32[]{:S(2)}) collective-permute-start(bf16[256,2048]{1,0:T(8,128)(2,1)} %get-tuple-element.45), channel_id=1, source_target_pairs={{0,1},{1,0},{2,3},{3,2},{4,5},{5,4},{6,7},{7,6},{8,9},{9,8},{10,11... | collective-permute-start | bytes 3145736 | tf_op jit(solution)/shard_map/ppermute | solution.py:496

commit v6 on v5

--- a/solution.py
+++ b/solution.py
@@ -450,7 +450,8 @@
     order = [[0]] + steps
     rest = [step for group in steps[1:] for step in group]
     soon, _ = pack_own(plan, where, subimages, steps[0], [])
-    later, near_parts = pack_own(plan, where, subimages, rest, range(1, plan.cells))
+    _, near_parts = pack_own(plan, where, subimages, [], range(1, plan.cells))
+    later, _ = pack_own(plan, where, subimages, rest, [])
     far = dict(zip(steps[0] + rest, list(soon) + list(later)))
 
     def across(pieces):

time: 81 us -> 81.2 us (level)
    ppermute x9, waiting for transfers between devices: 9.22 us -> 7.88 us  [across(): lax.ppermute(pieces[flip - 1], 'panel', cell_flip(flip))]
    pallas_call x2 -> x3, Pallas kernels: 1.97 us -> 2.54 us  [pack_own(): pl.pallas_call(body, out_shape=[far] * others + [near] * len(flips), in_s...]
  transfers between devices with their start and end apart: 13 -> 13, of which waited for: 7 -> 7; matrix products, arithmetic and copies ran while one was open for 1% -> 1% of each run, Pallas kernels for 10% -> 11%
where the time goes in v6:
time: 81.2 us; the launch traced here: 81 us
  waiting for transfers between devices  25.4 us (31%)
  Pallas kernels  19.9 us (25%)
  starting transfers between devices  16.8 us (21%)
  blocking collectives  11.5 us (14%)
  local copies, waits for them, and re-layouts  5.73 us (7%)
  between operations  0.87 us (1%)
    ppermute x3, waiting for transfers between devices, shards(): lax.ppermute(far[step], 'panel', plane_shift(step))  15.4 us
    all_to_all x1, blocking collectives, shards(): lax.all_to_all(partials.reshape(2 * panels, GRP_DEV), ('aper', 'panel'),...  11.5 us
    ppermute x9, starting transfers between devices, across(): lax.ppermute(pieces[flip - 1], 'panel', cell_flip(flip))  10.6 us
    pallas_call x1, Pallas kernels, merge(): pl.pallas_call(body, out_shape=[shape, shape], in_specs=[SMEM, SMEM, SMEM...  8.24 us
    ppermute x9, waiting for transfers between devices, across(): lax.ppermute(pieces[flip - 1], 'panel', cell_flip(flip))  7.88 us
    ppermute x3, starting transfers between devices, shards(): lax.ppermute(far[step], 'panel', plane_shift(step))  6.13 us
    unnamed x31, local copies, waits for them, and re-layouts  4.96 us
    pallas_call x2, Pallas kernels, build_angle(): pl.pallas_call(body, out_shape=jax.ShapeDtypeStruct((count, 2 * PAIR, PAI...  2.73 us
  transfers between devices with their start and end apart: 13, of which 7 were waited for; matrix products, arithmetic and copies ran while one was open for 1% of the time, Pallas kernels for 11%

profile of v6, /device:TPU:0, one launch (start us, length us, event | category | flops | bytes accessed | tf_op | source)
XLA Modules:
  0.0 81.0 jit_solution(13434082633912613443)
XLA Ops:
  0.7 1.2 %copy-done = bf16[2,2,32,4096]{3,2,1,0:T(8,128)(2,1)S(1)} copy-done((bf16[2,2,32,4096]{3,2,1,0:T(8,128)(2,1)S(1)}, bf16[2,2,32,4096]{3,2,1,0:T(8,128)(2,1)}, u32[]{:S(2)}) %copy-start) | copy-done | bytes 1048600
  1.9 0.6 pack_own.4
  2.6 3.1 %collective-permute-start.3 = (bf16[2,2,32,1536]{3,2,1,0:T(8,128)(2,1)S(1)}, bf16[2,2,32,1536]{3,2,1,0:T(8,128)(2,1)S(1)}, u32[]{:S(2)}, u32[]{:S(2)}) collective-permute-start(bf16[2,2,32,1536]{3,2,1,0:T(8,128)(2,1)S(1)} %get-tuple-element.27), channel_id=1, source_target_pairs={{0,8},{2,10},{4,12},{6,14},{8,16},{10,18},{12,20},{14,22},{16,24},... | collective-permute-start | bytes 1179656 | tf_op jit(solution)/shard_map/ppermute | solution.py:467
  5.7 2.1 %collective-permute-start.4 = (bf16[2,2,32,1536]{3,2,1,0:T(8,128)(2,1)S(1)}, bf16[2,2,32,1536]{3,2,1,0:T(8,128)(2,1)S(1)}, u32[]{:S(2)}, u32[]{:S(2)}) collective-permute-start(bf16[2,2,32,1536]{3,2,1,0:T(8,128)(2,1)S(1)} %get-tuple-element.28), channel_id=1, source_target_pairs={{0,24},{2,26},{4,28},{6,30},{8,0},{10,2},{12,4},{14,6},{16,8},{18,... | collective-permute-start | bytes 1179656 | tf_op jit(solution)/shard_map/ppermute | solution.py:467
  7.7 0.6 pack_own.3
  8.3 1.7 %collective-permute-start = (bf16[1,2,2,32,768]{4,3,2,1,0:T(8,128)(2,1)S(1)}, bf16[1,2,2,32,768]{4,3,2,1,0:T(8,128)(2,1)S(1)}, u32[]{:S(2)}, u32[]{:S(2)}) collective-permute-start(bf16[1,2,2,32,768]{4,3,2,1,0:T(8,128)(2,1)S(1)} %get-tuple-element.24), channel_id=1, source_target_pairs={{0,2},{2,0},{4,6},{6,4},{8,10},{10,8},{12,14},{14,12},{16,18},{18,... | collective-permute-start | bytes 589832 | tf_op jit(solution)/shard_map/ppermute | solution.py:459
  10.1 1.5 %collective-permute-start.1 = (bf16[1,2,2,32,768]{4,3,2,1,0:T(8,128)(2,1)S(1)}, bf16[1,2,2,32,768]{4,3,2,1,0:T(8,128)(2,1)S(1)}, u32[]{:S(2)}, u32[]{:S(2)}) collective-permute-start(bf16[1,2,2,32,768]{4,3,2,1,0:T(8,128)(2,1)S(1)} %get-tuple-element.25), channel_id=1, source_target_pairs={{0,4},{2,6},{4,0},{6,2},{8,12},{10,14},{12,8},{14,10},{16,20},{18,... | collective-permute-start | bytes 589832 | tf_op jit(solution)/shard_map/ppermute | solution.py:459
  11.9 1.3 %pack_own.5 = bf16[2,2,32,1536]{3,2,1,0:T(8,128)(2,1)} custom-call(s32[2]{0:T(128)S(1)} %pad_add_fusion.where_ref, bf16[2,2,32,4096]{3,2,1,0:T(8,128)(2,1)S(1)} %copy-done), custom_call_target="tpu_custom_call" | custom-call | tf_op jit(solution)/shard_map/pack_own/pallas_call | solution.py:80
  13.2 3.0 %collective-permute-done.refs_0_ = bf16[1,2,2,32,768]{4,3,2,1,0:T(8,128)(2,1)S(1)} collective-permute-done((bf16[1,2,2,32,768]{4,3,2,1,0:T(8,128)(2,1)S(1)}, bf16[1,2,2,32,768]{4,3,2,1,0:T(8,128)(2,1)S(1)}, u32[]{:S(2)}, u32[]{:S(2)}) %collective-permute-start) | collective-permute-done | bytes 196640 | tf_op jit(solution)/shard_map/ppermute | solution.py:459
  16.2 0.7 copy-done.5
  16.9 1.0 %collective-permute-start.6 = (bf16[2,2,32,1536]{3,2,1,0:T(8,128)(2,1)}, bf16[2,2,32,1536]{3,2,1,0:T(8,128)(2,1)S(1)}, u32[]{:S(2)}, u32[]{:S(2)}) collective-permute-start(bf16[2,2,32,1536]{3,2,1,0:T(8,128)(2,1)} %pack_own.5), channel_id=1, source_target_pairs={{0,16},{2,18},{4,20},{6,22},{8,24},{10,26},{12,28},{14,30},{16,0},... | collective-permute-start | bytes 1179656 | tf_op jit(solution)/shard_map/ppermute | solution.py:467
  17.9 2.3 %collective-permute-done.1.refs_1_ = bf16[1,2,2,32,768]{4,3,2,1,0:T(8,128)(2,1)S(1)} collective-permute-done((bf16[1,2,2,32,768]{4,3,2,1,0:T(8,128)(2,1)S(1)}, bf16[1,2,2,32,768]{4,3,2,1,0:T(8,128)(2,1)S(1)}, u32[]{:S(2)}, u32[]{:S(2)}) %collective-permute-start.1) | collective-permute-done | bytes 196640 | tf_op jit(solution)/shard_map/ppermute | solution.py:459
  20.2 0.7 copy-done.7
  20.9 0.7 copy-done.9
  21.6 3.1 %collective-permute-done.4.refs_1_.refs_12_ = bf16[2,2,32,1536]{3,2,1,0:T(8,128)(2,1)S(1)} collective-permute-done((bf16[2,2,32,1536]{3,2,1,0:T(8,128)(2,1)S(1)}, bf16[2,2,32,1536]{3,2,1,0:T(8,128)(2,1)S(1)}, u32[]{:S(2)}, u32[]{:S(2)}) %collective-permute-start.4) | collective-permute-done | bytes 393248 | tf_op jit(solution)/shard_map/ppermute | solution.py:467
  24.7 1.6 %pack_panels.2 = (bf16[2,2,2,32,768]{4,3,2,1,0:T(8,128)(2,1)}, bf16[2,2,2,32,768]{4,3,2,1,0:T(8,128)(2,1)}, bf16[2,2,2,32,768]{4,3,2,1,0:T(8,128)(2,1)}) custom-call(s32[2]{0:T(128)S(1)} %pad_add_fusion.where_ref, bf16[2,2,32,1536]{3,2,1,0:T(8,128)(2,1)S(1)} %collective-permute-done.3.refs_0_.refs_10_, ...), custom_call_target="tpu_custom_call" | custom-call | tf_op jit(solution)/shard_map/pack_panels/pallas_call | solution.py:110
  26.3 1.5 %collective-permute-start.5 = (bf16[2,2,2,32,768]{4,3,2,1,0:T(8,128)(2,1)}, bf16[2,2,2,32,768]{4,3,2,1,0:T(8,128)(2,1)}, u32[]{:S(2)}, u32[]{:S(2)}) collective-permute-start(bf16[2,2,2,32,768]{4,3,2,1,0:T(8,128)(2,1)} %get-tuple-element.34), channel_id=1, source_target_pairs={{0,2},{2,0},{4,6},{6,4},{8,10},{10,8},{12,14},{14,12},{16,18},{18,... | collective-permute-start | bytes 1179656 | tf_op jit(solution)/shard_map/ppermute | solution.py:459
  27.8 1.5 %collective-permute-start.7 = (bf16[2,2,2,32,768]{4,3,2,1,0:T(8,128)(2,1)}, bf16[2,2,2,32,768]{4,3,2,1,0:T(8,128)(2,1)}, u32[]{:S(2)}, u32[]{:S(2)}) collective-permute-start(bf16[2,2,2,32,768]{4,3,2,1,0:T(8,128)(2,1)} %get-tuple-element.36), channel_id=1, source_target_pairs={{0,4},{2,6},{4,0},{6,2},{8,12},{10,14},{12,8},{14,10},{16,20},{18,... | collective-permute-start | bytes 1179656 | tf_op jit(solution)/shard_map/ppermute | solution.py:459
  29.8 12.3 %collective-permute-done.6.refs_0_.refs_11_ = bf16[2,2,32,1536]{3,2,1,0:T(8,128)(2,1)S(1)} collective-permute-done((bf16[2,2,32,1536]{3,2,1,0:T(8,128)(2,1)}, bf16[2,2,32,1536]{3,2,1,0:T(8,128)(2,1)S(1)}, u32[]{:S(2)}, u32[]{:S(2)}) %collective-permute-start.6) | collective-permute-done | bytes 393248 | tf_op jit(solution)/shard_map/ppermute | solution.py:467
  42.1 0.6 pack_panels.3
  42.7 1.6 %collective-permute-start.10 = (bf16[1,2,2,32,768]{4,3,2,1,0:T(8,128)(2,1)S(1)}, bf16[1,2,2,32,768]{4,3,2,1,0:T(8,128)(2,1)S(1)}, u32[]{:S(2)}, u32[]{:S(2)}) collective-permute-start(bf16[1,2,2,32,768]{4,3,2,1,0:T(8,128)(2,1)S(1)} %get-tuple-element.40), channel_id=1, source_target_pairs={{0,4},{2,6},{4,0},{6,2},{8,12},{10,14},{12,8},{14,10},{16,20},{18,... | collective-permute-start | bytes 589832 | tf_op jit(solution)/shard_map/ppermute | solution.py:459
  44.3 1.4 %collective-permute-start.11 = (bf16[1,2,2,32,768]{4,3,2,1,0:T(8,128)(2,1)S(1)}, bf16[1,2,2,32,768]{4,3,2,1,0:T(8,128)(2,1)S(1)}, u32[]{:S(2)}, u32[]{:S(2)}) collective-permute-start(bf16[1,2,2,32,768]{4,3,2,1,0:T(8,128)(2,1)S(1)} %get-tuple-element.41), channel_id=1, source_target_pairs={{0,6},{2,4},{4,2},{6,0},{8,14},{10,12},{12,10},{14,8},{16,22},{18,... | collective-permute-start | bytes 589832 | tf_op jit(solution)/shard_map/ppermute | solution.py:459
  46.3 1.5 %build_angle.2.refs_14_ = bf16[12,512,256]{2,1,0:T(8,128)(2,1)S(1)} custom-call(s32[12]{0:T(128)S(1)} %pad_add_fusion.1.blocks_ref, s32[1,32768]{1,0:T(1,128)S(1)} %copy-done.4, bf16[2,16,32768]{2,1,0:T(8,128)(2,1)S(1)} %bitcast.11), custom_call_target="tpu_custom_call" | custom-call | tf_op jit(solution)/shard_map/build_angle/pallas_call | solution.py:153
  47.9 1.6 %copy-done.2 = bf16[12,512,256]{2,1,0:T(8,128)(2,1)} copy-done((bf16[12,512,256]{2,1,0:T(8,128)(2,1)}, bf16[12,512,256]{2,1,0:T(8,128)(2,1)S(1)}, u32[]{:S(2)}) %copy-start.2) | copy-done | bytes 3145752
  49.5 1.2 %build_angle.3.refs_15_ = bf16[8,512,256]{2,1,0:T(8,128)(2,1)S(1)} custom-call(s32[8]{0:T(128)S(1)} %iota_add_fusion.blocks_ref, s32[1,32768]{1,0:T(1,128)S(1)} %copy-done.4, bf16[2,16,32768]{2,1,0:T(8,128)(2,1)S(1)} %bitcast.12), custom_call_target="tpu_custom_call" | custom-call | tf_op jit(solution)/shard_map/build_angle/pallas_call | solution.py:153
  50.8 1.7 %build_range.1.refs_13_ = bf16[3,4,256,256]{3,2,1,0:T(8,128)(2,1)S(1)} custom-call(s32[3,1,512]{2,1,0:T(1,128)S(1)} %bitcast.16, bf16[3,2,16,512]{3,2,1,0:T(8,128)(2,1)S(1)} %bitcast.13), custom_call_target="tpu_custom_call" | custom-call | tf_op jit(solution)/shard_map/build_range/pallas_call | solution.py:180
  52.6 2.4 %collective-permute-done.10.refs_7_ = bf16[1,2,2,32,768]{4,3,2,1,0:T(8,128)(2,1)S(1)} collective-permute-done((bf16[1,2,2,32,768]{4,3,2,1,0:T(8,128)(2,1)S(1)}, bf16[1,2,2,32,768]{4,3,2,1,0:T(8,128)(2,1)S(1)}, u32[]{:S(2)}, u32[]{:S(2)}) %collective-permute-start.10) | collective-permute-done | bytes 196640 | tf_op jit(solution)/shard_map/ppermute | solution.py:459
  55.1 8.2 %merge.1 = (bf16[256,2048]{1,0:T(8,128)(2,1)S(1)}, bf16[256,2048]{1,0:T(8,128)(2,1)}) custom-call(s32[2]{0:T(128)S(1)} %pad_add_fusion.where_ref, s32[3,4]{1,0:T(4,128)S(1)} %bitcast.15, s32[1,256]{1,0:T(1,128)S(1)} %copy-done.13, bf16[1,2,2,32,768]{4,3,2,1,0:T(8,128)(2,1)S(1)} %copy-done.6, bf16[1,2,2,32,768]{4,3,2,1,0:T(8,128)(2,1)S(1)} %copy-done.8, ...), custom_call_target="tpu_custom_call" | custom-call | tf_op jit(solution)/shard_map/merge/pallas_call | solution.py:336
  63.5 0.7 dynamic-slice.3
  64.2 2.2 %collective-permute-done.12.oth_ref = bf16[256,2048]{1,0:T(8,128)(2,1)S(1)} collective-permute-done((bf16[256,2048]{1,0:T(8,128)(2,1)}, bf16[256,2048]{1,0:T(8,128)(2,1)S(1)}, u32[]{:S(2)}, u32[]{:S(2)}) %collective-permute-start.12) | collective-permute-done | bytes 1048608 | tf_op jit(solution)/shard_map/ppermute | solution.py:497
  66.3 2.4 %focus.1 = (bf16[2,256,1024]{2,1,0:T(8,128)(2,1)}, f32[2,64,1]{2,1,0:T(8,128)S(1)}) custom-call(s32[2]{0:T(128)S(1)} %pad_add_fusion.where_ref, bf16[256,2048]{1,0:T(8,128)(2,1)S(1)} %get-tuple-element.42.own_ref, bf16[256,2048]{1,0:T(8,128)(2,1)S(1)} %collective-permute-done.12.oth_ref, s32[1,1024]{1,0:T(1,128)S(1)} %bitcast.14), custom_call_target="tpu_custom_call" | custom-call | tf_op jit(solution)/shard_map/focus/pallas_call | solution.py:412
  68.9 11.5 %all_to_all.9 = f32[32,1,4]{2,1,0:T(1,128)S(1)} all-to-all(f32[32,1,4]{2,1,0:T(1,128)S(1)} %bitcast.17), channel_id=1, replica_groups=mesh['scene'=1,'panel'=16,'aper'=2] {'aper','panel'}, dimensions={0} | all-to-all | bytes 1024 | tf_op jit(solution)/shard_map/all_to_all | solution.py:501
  (44 shorter events, 2.5 us)
Async XLA Ops:
  0.7 1.2 %copy-start = (bf16[2,2,32,4096]{3,2,1,0:T(8,128)(2,1)S(1)}, bf16[2,2,32,4096]{3,2,1,0:T(8,128)(2,1)}, u32[]{:S(2)}) copy-start(bf16[2,2,32,4096]{3,2,1,0:T(8,128)(2,1)} %refs_9_.1) | copy-start | bytes 3145732
  2.6 43.8 %copy-start.3 = (bf16[1,2,16,32768]{3,2,1,0:T(8,128)(2,1)S(1)}, bf16[1,2,16,32768]{3,2,1,0:T(8,128)(2,1)}, u32[]{:S(2)}) copy-start(bf16[1,2,16,32768]{3,2,1,0:T(8,128)(2,1)} %param.14) | copy-start | bytes 6291460
  2.6 43.8 %copy-start.4 = (s32[1,32768]{1,0:T(1,128)S(1)}, s32[1,32768]{1,0:T(1,128)}, u32[]{:S(2)}) copy-start(s32[1,32768]{1,0:T(1,128)} %taps_ref.3) | copy-start | bytes 393220
  2.6 19.0 %collective-permute-start.3 = (bf16[2,2,32,1536]{3,2,1,0:T(8,128)(2,1)S(1)}, bf16[2,2,32,1536]{3,2,1,0:T(8,128)(2,1)S(1)}, u32[]{:S(2)}, u32[]{:S(2)}) collective-permute-start(bf16[2,2,32,1536]{3,2,1,0:T(8,128)(2,1)S(1)} %get-tuple-element.27), channel_id=1, source_target_pairs={{0,8},{2,10},{4,12},{6,14},{8,16},{10,18},{12,20},{14,22},{16,24},... | collective-permute-start | bytes 1179656 | tf_op jit(solution)/shard_map/ppermute | solution.py:467
  5.7 19.0 %collective-permute-start.4 = (bf16[2,2,32,1536]{3,2,1,0:T(8,128)(2,1)S(1)}, bf16[2,2,32,1536]{3,2,1,0:T(8,128)(2,1)S(1)}, u32[]{:S(2)}, u32[]{:S(2)}) collective-permute-start(bf16[2,2,32,1536]{3,2,1,0:T(8,128)(2,1)S(1)} %get-tuple-element.28), channel_id=1, source_target_pairs={{0,24},{2,26},{4,28},{6,30},{8,0},{10,2},{12,4},{14,6},{16,8},{18,... | collective-permute-start | bytes 1179656 | tf_op jit(solution)/shard_map/ppermute | solution.py:467
  8.3 7.9 %collective-permute-start = (bf16[1,2,2,32,768]{4,3,2,1,0:T(8,128)(2,1)S(1)}, bf16[1,2,2,32,768]{4,3,2,1,0:T(8,128)(2,1)S(1)}, u32[]{:S(2)}, u32[]{:S(2)}) collective-permute-start(bf16[1,2,2,32,768]{4,3,2,1,0:T(8,128)(2,1)S(1)} %get-tuple-element.24), channel_id=1, source_target_pairs={{0,2},{2,0},{4,6},{6,4},{8,10},{10,8},{12,14},{14,12},{16,18},{18,... | collective-permute-start | bytes 589832 | tf_op jit(solution)/shard_map/ppermute | solution.py:459
  10.1 10.1 %collective-permute-start.1 = (bf16[1,2,2,32,768]{4,3,2,1,0:T(8,128)(2,1)S(1)}, bf16[1,2,2,32,768]{4,3,2,1,0:T(8,128)(2,1)S(1)}, u32[]{:S(2)}, u32[]{:S(2)}) collective-permute-start(bf16[1,2,2,32,768]{4,3,2,1,0:T(8,128)(2,1)S(1)} %get-tuple-element.25), channel_id=1, source_target_pairs={{0,4},{2,6},{4,0},{6,2},{8,12},{10,14},{12,8},{14,10},{16,20},{18,... | collective-permute-start | bytes 589832 | tf_op jit(solution)/shard_map/ppermute | solution.py:459
  11.6 9.3 %collective-permute-start.2 = (bf16[1,2,2,32,768]{4,3,2,1,0:T(8,128)(2,1)S(1)}, bf16[1,2,2,32,768]{4,3,2,1,0:T(8,128)(2,1)S(1)}, u32[]{:S(2)}, u32[]{:S(2)}) collective-permute-start(bf16[1,2,2,32,768]{4,3,2,1,0:T(8,128)(2,1)S(1)} %get-tuple-element.26), channel_id=1, source_target_pairs={{0,6},{2,4},{4,2},{6,0},{8,14},{10,12},{12,10},{14,8},{16,22},{18,... | collective-permute-start | bytes 589832 | tf_op jit(solution)/shard_map/ppermute | solution.py:459
  16.2 0.7 copy-start.5
  16.9 25.1 %collective-permute-start.6 = (bf16[2,2,32,1536]{3,2,1,0:T(8,128)(2,1)}, bf16[2,2,32,1536]{3,2,1,0:T(8,128)(2,1)S(1)}, u32[]{:S(2)}, u32[]{:S(2)}) collective-permute-start(bf16[2,2,32,1536]{3,2,1,0:T(8,128)(2,1)} %pack_own.5), channel_id=1, source_target_pairs={{0,16},{2,18},{4,20},{6,22},{8,24},{10,26},{12,28},{14,30},{16,0},... | collective-permute-start | bytes 1179656 | tf_op jit(solution)/shard_map/ppermute | solution.py:467
  20.2 0.7 copy-start.7
  20.9 0.7 copy-start.9
  26.3 15.8 %collective-permute-start.5 = (bf16[2,2,2,32,768]{4,3,2,1,0:T(8,128)(2,1)}, bf16[2,2,2,32,768]{4,3,2,1,0:T(8,128)(2,1)}, u32[]{:S(2)}, u32[]{:S(2)}) collective-permute-start(bf16[2,2,2,32,768]{4,3,2,1,0:T(8,128)(2,1)} %get-tuple-element.34), channel_id=1, source_target_pairs={{0,2},{2,0},{4,6},{6,4},{8,10},{10,8},{12,14},{14,12},{16,18},{18,... | collective-permute-start | bytes 1179656 | tf_op jit(solution)/shard_map/ppermute | solution.py:459
  27.8 24.8 %collective-permute-start.7 = (bf16[2,2,2,32,768]{4,3,2,1,0:T(8,128)(2,1)}, bf16[2,2,2,32,768]{4,3,2,1,0:T(8,128)(2,1)}, u32[]{:S(2)}, u32[]{:S(2)}) collective-permute-start(bf16[2,2,2,32,768]{4,3,2,1,0:T(8,128)(2,1)} %get-tuple-element.36), channel_id=1, source_target_pairs={{0,4},{2,6},{4,0},{6,2},{8,12},{10,14},{12,8},{14,10},{16,20},{18,... | collective-permute-start | bytes 1179656 | tf_op jit(solution)/shard_map/ppermute | solution.py:459
  29.3 23.2 %collective-permute-start.8 = (bf16[2,2,2,32,768]{4,3,2,1,0:T(8,128)(2,1)}, bf16[2,2,2,32,768]{4,3,2,1,0:T(8,128)(2,1)}, u32[]{:S(2)}, u32[]{:S(2)}) collective-permute-start(bf16[2,2,2,32,768]{4,3,2,1,0:T(8,128)(2,1)} %get-tuple-element.37), channel_id=1, source_target_pairs={{0,6},{2,4},{4,2},{6,0},{8,14},{10,12},{12,10},{14,8},{16,22},{18,... | collective-permute-start | bytes 1179656 | tf_op jit(solution)/shard_map/ppermute | solution.py:459
  42.7 12.3 %collective-permute-start.10 = (bf16[1,2,2,32,768]{4,3,2,1,0:T(8,128)(2,1)S(1)}, bf16[1,2,2,32,768]{4,3,2,1,0:T(8,128)(2,1)S(1)}, u32[]{:S(2)}, u32[]{:S(2)}) collective-permute-start(bf16[1,2,2,32,768]{4,3,2,1,0:T(8,128)(2,1)S(1)} %get-tuple-element.40), channel_id=1, source_target_pairs={{0,4},{2,6},{4,0},{6,2},{8,12},{10,14},{12,8},{14,10},{16,20},{18,... | collective-permute-start | bytes 589832 | tf_op jit(solution)/shard_map/ppermute | solution.py:459
  44.3 10.7 %collective-permute-start.11 = (bf16[1,2,2,32,768]{4,3,2,1,0:T(8,128)(2,1)S(1)}, bf16[1,2,2,32,768]{4,3,2,1,0:T(8,128)(2,1)S(1)}, u32[]{:S(2)}, u32[]{:S(2)}) collective-permute-start(bf16[1,2,2,32,768]{4,3,2,1,0:T(8,128)(2,1)S(1)} %get-tuple-element.41), channel_id=1, source_target_pairs={{0,6},{2,4},{4,2},{6,0},{8,14},{10,12},{12,10},{14,8},{16,22},{18,... | collective-permute-start | bytes 589832 | tf_op jit(solution)/shard_map/ppermute | solution.py:459
  45.7 9.4 %collective-permute-start.9 = (bf16[1,2,2,32,768]{4,3,2,1,0:T(8,128)(2,1)S(1)}, bf16[1,2,2,32,768]{4,3,2,1,0:T(8,128)(2,1)S(1)}, u32[]{:S(2)}, u32[]{:S(2)}) collective-permute-start(bf16[1,2,2,32,768]{4,3,2,1,0:T(8,128)(2,1)S(1)} %get-tuple-element.39), channel_id=1, source_target_pairs={{0,2},{2,0},{4,6},{6,4},{8,10},{10,8},{12,14},{14,12},{16,18},{18,... | collective-permute-start | bytes 589832 | tf_op jit(solution)/shard_map/ppermute | solution.py:459
  47.8 1.6 %copy-start.2 = (bf16[12,512,256]{2,1,0:T(8,128)(2,1)}, bf16[12,512,256]{2,1,0:T(8,128)(2,1)S(1)}, u32[]{:S(2)}) copy-start(bf16[12,512,256]{2,1,0:T(8,128)(2,1)S(1)} %build_angle.2.refs_14_) | copy-start | bytes 9437188
  49.5 1.3 %copy-start.14 = (s32[1,3,4]{2,0,1:T(1,128)S(1)}, s32[1,3,4]{2,0,1:T(1,128)}, u32[]{:S(2)}) copy-start(s32[1,3,4]{2,0,1:T(1,128)} %param.10) | copy-start | bytes 148
  49.5 1.3 %copy-start.11 = (bf16[1,3,2,16,512]{4,3,2,1,0:T(8,128)(2,1)S(1)}, bf16[1,3,2,16,512]{4,3,2,1,0:T(8,128)(2,1)}, u32[]{:S(2)}) copy-start(bf16[1,3,2,16,512]{4,3,2,1,0:T(8,128)(2,1)} %param.11) | copy-start | bytes 294916
  49.5 1.3 %copy-start.12 = (s32[1,3,512]{2,0,1:T(1,128)S(1)}, s32[1,3,512]{2,0,1:T(1,128)}, u32[]{:S(2)}) copy-start(s32[1,3,512]{2,0,1:T(1,128)} %param.9) | copy-start | bytes 18436
  49.5 5.6 %copy-start.1 = (bf16[2,2,32,4096]{3,2,1,0:T(8,128)(2,1)S(1)}, bf16[2,2,32,4096]{3,2,1,0:T(8,128)(2,1)}, u32[]{:S(2)}) copy-start(bf16[2,2,32,4096]{3,2,1,0:T(8,128)(2,1)} %refs_9_.1) | copy-start | bytes 3145732
  49.5 5.6 %copy-start.6 = (bf16[1,2,2,32,768]{4,3,2,1,0:T(8,128)(2,1)S(1)}, bf16[1,2,2,32,768]{4,3,2,1,0:T(8,128)(2,1)}, u32[]{:S(2)}) copy-start(bf16[1,2,2,32,768]{4,3,2,1,0:T(8,128)(2,1)} %copy-done.5) | copy-start | bytes 589828
  49.5 5.6 %copy-start.8 = (bf16[1,2,2,32,768]{4,3,2,1,0:T(8,128)(2,1)S(1)}, bf16[1,2,2,32,768]{4,3,2,1,0:T(8,128)(2,1)}, u32[]{:S(2)}) copy-start(bf16[1,2,2,32,768]{4,3,2,1,0:T(8,128)(2,1)} %copy-done.7) | copy-start | bytes 589828
  49.5 5.6 %copy-start.10 = (bf16[1,2,2,32,768]{4,3,2,1,0:T(8,128)(2,1)S(1)}, bf16[1,2,2,32,768]{4,3,2,1,0:T(8,128)(2,1)}, u32[]{:S(2)}) copy-start(bf16[1,2,2,32,768]{4,3,2,1,0:T(8,128)(2,1)} %copy-done.9) | copy-start | bytes 589828
  49.5 5.6 %copy-start.13 = (s32[1,256]{1,0:T(1,128)S(1)}, s32[1,256]{1,0:T(1,128)}, u32[]{:S(2)}) copy-start(s32[1,256]{1,0:T(1,128)} %ab_ref.1) | copy-start | bytes 3076
  63.4 2.9 %collective-permute-start.12 = (bf16[256,2048]{1,0:T(8,128)(2,1)}, bf16[256,2048]{1,0:T(8,128)(2,1)S(1)}, u32[]{:S(2)}, u32[]{:S(2)}) collective-permute-start(bf16[256,2048]{1,0:T(8,128)(2,1)} %get-tuple-element.43), channel_id=1, source_target_pairs={{0,1},{1,0},{2,3},{3,2},{4,5},{5,4},{6,7},{7,6},{8,9},{9,8},{10,11... | collective-permute-start | bytes 3145736 | tf_op jit(solution)/shard_map/ppermute | solution.py:497
